TPU v7x, 32 devices: a whole 2x2x4 slice. The times are simulated.
32 devices in a mesh: groups: 2 (over x), band: 16 (over z, y, core).
Axes of the slice: x: 2, y: 2, z: 4, core: 2. Of those that a mesh axis runs over, the one named last changes fastest.
Arguments:
- orbitals: float32 [32, 96, 9216], P(('groups', 'band')), parts along dimension 0, may hold values from -6 to 6
Outputs:
- exchange_term: float32 [32, 96, 9216], P(('groups', 'band')), parts along dimension 0
There are 2 independent parts, one for each index of `groups`. A program takes and returns all parts, laid end to end along the dimension named above; each array names one. Nothing has to cross between parts.
All inputs are finite; a program needn't handle non-finite values.
Results may differ from a plain program's by a relative error of at most 0.0003.
Values sent between devices are 32-bit elements; how exact they have to be, the bound alone decides.
No kernel may reach another device: no remote copies, remote signals or barrier semaphores. Data moves between devices by JAX's collectives and lax.ppermute only.
A program may use at most 128 MiB of HBM per device.

v0:
```python
import math

import jax
import jax.numpy as jnp
from jax import lax
from jax.sharding import PartitionSpec as P

OFFSET = 5


screening = 5.44


def from_behind(value, axis, by):
    count = lax.axis_size(axis)
    return lax.ppermute(value, axis, [(i, (i + by) % count) for i in range(count)])


def screened_kernel(points):
    signed = jnp.arange(points, dtype=jnp.int32)
    signed = jnp.where(signed >= points // 2, signed - points, signed)
    wavenumber = signed.astype(jnp.float32) * (2.0 * math.pi / points)
    squared = (
        wavenumber[:, None, None] ** 2
        + wavenumber[None, :, None] ** 2
        + wavenumber[None, None, :] ** 2
    )
    screen_rate = screening / points
    finite = jnp.where(squared > 0.0, squared, 1.0)
    screened = 4.0 * math.pi / finite * -jnp.expm1(-finite / (4.0 * screen_rate * screen_rate))
    return jnp.where(squared > 0.0, screened, math.pi / (screen_rate * screen_rate))


def block_tables(points, direction):
    counter = jnp.arange(points, dtype=jnp.int32)
    products = counter[:, None] * counter[None, :] % points
    angles = products.astype(jnp.float32) * (2.0 * math.pi / points)
    real_table = jnp.cos(angles)
    imag_table = direction * jnp.sin(angles)
    top_row = jnp.stack([real_table, -imag_table], 1)
    low_row = jnp.stack([imag_table, real_table], 1)
    return (jnp.stack([real_table, imag_table], 0), jnp.stack([top_row, low_row], 0))


def potentials(density, forward_first, forward_block, inverse_block, kernel):
    parts = jnp.einsum("oka,nabc->onbck", forward_first, density, precision=lax.Precision.HIGHEST)
    for repeat in range(2):
        parts = jnp.einsum(
            "okpa,pnabc->onbck", forward_block, parts, precision=lax.Precision.HIGHEST
        )
    parts = parts * kernel[None, None]
    for repeat in range(2):
        parts = jnp.einsum(
            "okpa,pnabc->onbck", inverse_block, parts, precision=lax.Precision.HIGHEST
        )
    real_part = jnp.einsum(
        "kpa,pnabc->nbck", inverse_block[0], parts, precision=lax.Precision.HIGHEST
    )
    points = density.shape[1]
    return real_part / float(points * points * points)


def visit_blocks(resident, visitors, tables, kernel):
    forward_first, forward_block, inverse_block = tables

    def visit(running, visitor):
        potential = potentials(
            resident * visitor[None], forward_first, forward_block, inverse_block, kernel
        )
        running = running - visitor[None] * potential
        return (running, None)

    return lax.scan(visit, jnp.zeros_like(resident), visitors)


def local(orbitals):
    band_count, points, plane = orbitals.shape
    cube_shape = (band_count, points, points, points)
    resident = orbitals.reshape(cube_shape)
    forward_first, forward_block = block_tables(points, -1.0)
    unused_first, inverse_block = block_tables(points, 1.0)
    tables = (forward_first, forward_block, inverse_block)
    kernel = screened_kernel(points)
    lower_block = from_behind(orbitals, "band", OFFSET).reshape(cube_shape)
    upper_block = from_behind(orbitals, "band", -OFFSET).reshape(cube_shape)
    visitors = jnp.concatenate([lower_block, upper_block], 0)
    accumulated, unused = visit_blocks(resident, visitors, tables, kernel)
    return accumulated.reshape(orbitals.shape)


def solution(mesh):
    return jax.shard_map(
        local,
        mesh=mesh,
        in_specs=(P(("groups", "band"), None, None),),
        out_specs=P(("groups", "band"), None, None),
        check_vma=False,
    )
```

profile of v0, /device:TPU:26, one launch (start us, length us, event | category | flops | bytes accessed | tf_op | source)
XLA Modules:
  0.0 483.1 jit_solution(6470827229223324633)
XLA Ops:
  0.0 0.0 collective-permute-start
  0.0 3.5 collective-permute-start.1
  3.5 5.9 %reshape.244 = f32[1,96,96,96]{3,2,1,0:T(8,128)} reshape(f32[1,96,9216]{2,1,0:T(8,128)} %param.3) | data formatting | bytes 7077888 | tf_op jit(solution)/shard_map/reshape | solution.py:79
  9.4 0.2 broadcast_multiply_fusion
  9.7 0.2 fusion.54
  9.9 0.2 fusion.55
  10.1 0.2 fusion.61
  10.3 0.2 fusion.62
  10.5 0.2 sine_multiply_fusion
  10.8 0.1 broadcast_add_fusion
  10.9 182.8 %collective-permute-done = f32[1,96,9216]{2,1,0:T(8,128)} collective-permute-done((f32[1,96,9216]{2,1,0:T(8,128)}, f32[1,96,9216]{2,1,0:T(8,128)}, u32[]{:S(2)}, u32[]{:S(2)}) %collective-permute-start) | collective-permute-done | bytes 3538976 | tf_op jit(solution)/shard_map/ppermute | solution.py:16
  193.8 5.8 %reshape.242 = f32[1,96,96,96]{3,2,1,0:T(8,128)} reshape(f32[1,96,9216]{2,1,0:T(8,128)} %collective-permute-done) | data formatting | bytes 7077888 | tf_op jit(solution)/shard_map/reshape | solution.py:84
  199.6 0.0 collective-permute-done.1
  199.6 5.8 %reshape.243 = f32[1,96,96,96]{3,2,1,0:T(8,128)} reshape(f32[1,96,9216]{2,1,0:T(8,128)} %collective-permute-done.1) | data formatting | bytes 7077888 | tf_op jit(solution)/shard_map/reshape | solution.py:85
  205.4 8.5 %pad_maximum_fusion = f32[2,96,96,96]{3,2,1,0:T(8,128)} fusion(f32[1,96,96,96]{3,2,1,0:T(8,128)} %reshape.243, f32[1,96,96,96]{3,2,1,0:T(8,128)} %reshape.242), kind=kLoop, calls=%fused_computation.38 | loop fusion | flops 1769472 | bytes 14155776 | tf_op jit(solution)/shard_map/concatenate | solution.py:86
  213.9 262.8 %while.11 = (s32[]{:T(128)}, f32[1,96,96,96]{3,2,1,0:T(8,128)}, f32[2,96,96,96]{3,2,1,0:T(8,128)}, f32[1,96,96,96]{3,2,1,0:T(8,128)}, f32[2,96,96]{2,1,0:T(8,128...) while((s32[]{:T(128)}, f32[1,96,96,96]{3,2,1,0:T(8,128)}, ...), condition=%wide.region_1.2_spmd.clone, body=%wide.region_0.1_spmd.clone.sunk | while | flops 20398473216 | bytes 103404040 | solution.py:73
  213.9 4.8 multiply_bitcast_fusion.2
  218.7 10.0 %fusion.99 = f32[2,96,96,96,1]{3,2,0,1,4:T(8,128)S(1)} fusion(f32[96,96,96,1]{2,1,0,3:T(8,128)S(1)} %multiply_bitcast_fusion.2, f32[2,96,96]{2,1,0:T(8,128)S(1)} %get-tuple-element.208), kind=kOutput, calls=%fused_computation.31.clone.1 | convolution fusion | flops 2038431744 | bytes 10690560 | tf_op jit(solution)/shard_map/while/body/eval_jaxpr/oka,nabc->onbck/dot_general | solution.py:46
  228.7 20.3 %fusion.100 = f32[2,96,96,96,1]{3,2,0,1,4:T(8,128)S(1)} fusion(f32[2,96,96,96,1]{3,2,0,1,4:T(8,128)S(1)} %fusion.99, f32[2,96,2,96]{3,1,2,0:T(8,128)S(1)} %get-tuple-element.209), kind=kOutput, calls=%fused_computation.28.clone.1 | convolution fusion | flops 4076863488 | bytes 14303232 | tf_op jit(solution)/shard_map/while/body/eval_jaxpr/okpa,pnabc->onbck/dot_general | solution.py:48
  249.1 3.0 fusion.98
  252.1 20.3 %fusion.101 = f32[2,96,96,96,1]{3,2,0,1,4:T(8,128)S(1)} fusion(f32[96,96,96]{2,1,0:T(8,128)S(1)} %fusion.98, f32[2,96,96,96,1]{3,2,0,1,4:T(8,128)S(1)} %fusion.100, f32[2,96,2,96]{3,1,2,0:T(8,128)S(1)} %get-tuple-element.209), kind=kOutput, calls=%fused_computation.6.clone.1 | convolution fusion | flops 4078632960 | bytes 17842176 | tf_op jit(solution)/shard_map/while/body/eval_jaxpr/okpa,pnabc->onbck/dot_general | solution.py:48
  272.3 19.3 %fusion.102 = f32[2,96,96,96,1]{3,2,0,1,4:T(8,128)S(1)} fusion(f32[2,96,96,96,1]{3,2,0,1,4:T(8,128)S(1)} %fusion.101, f32[2,96,2,96]{3,1,2,0:T(8,128)S(1)} %get-tuple-element.210), kind=kOutput, calls=%fused_computation.29.clone.1 | convolution fusion | flops 4076863488 | bytes 14303232 | tf_op jit(solution)/shard_map/while/body/eval_jaxpr/okpa,pnabc->onbck/dot_general | solution.py:53
  291.6 24.6 %fusion.103 = f32[2,96,96,96]{3,2,0,1:T(8,128)} fusion(f32[2,96,96,96,1]{3,2,0,1,4:T(8,128)S(1)} %fusion.102, f32[2,96,2,96]{3,1,2,0:T(8,128)S(1)} %get-tuple-element.210), kind=kOutput, calls=%fused_computation.30.clone.1 | convolution fusion | flops 4076863488 | bytes 14303232 | tf_op jit(solution)/shard_map/while/body/eval_jaxpr/okpa,pnabc->onbck/dot_general | solution.py:53
  316.3 27.9 %fusion.104 = f32[1,96,96,96]{3,2,1,0:T(8,128)} fusion(f32[1,96,96,96]{3,2,1,0:T(8,128)} %get-tuple-element.193, f32[2,96,96,96]{3,2,1,0:T(8,128)} %get-tuple-element.206, s32[]{:T(128)} %get-tuple-element.192, pred[]{:T(512)S(6)} %compare.3, f32[2,96,96,96]{3,2,0,1:T(8,128)} %fusion.103, f32[96,2,96]{2,0,1:T(8,128)S(1)} %get-tuple-element.211), kind=kOutput, calls=%fused_computation.23.clone.1 | convolution fusion | flops 2041970688 | bytes 17768452 | tf_op jit(solution)/shard_map/while/body/eval_jaxpr/kpa,pnabc->nbck/dot_general | solution.py:56
  344.3 4.8 multiply_bitcast_fusion.2
  349.1 10.0 %fusion.99 = f32[2,96,96,96,1]{3,2,0,1,4:T(8,128)S(1)} fusion(f32[96,96,96,1]{2,1,0,3:T(8,128)S(1)} %multiply_bitcast_fusion.2, f32[2,96,96]{2,1,0:T(8,128)S(1)} %get-tuple-element.208), kind=kOutput, calls=%fused_computation.31.clone.1 | convolution fusion | flops 2038431744 | bytes 10690560 | tf_op jit(solution)/shard_map/while/body/eval_jaxpr/oka,nabc->onbck/dot_general | solution.py:46
  359.1 20.3 %fusion.100 = f32[2,96,96,96,1]{3,2,0,1,4:T(8,128)S(1)} fusion(f32[2,96,96,96,1]{3,2,0,1,4:T(8,128)S(1)} %fusion.99, f32[2,96,2,96]{3,1,2,0:T(8,128)S(1)} %get-tuple-element.209), kind=kOutput, calls=%fused_computation.28.clone.1 | convolution fusion | flops 4076863488 | bytes 14303232 | tf_op jit(solution)/shard_map/while/body/eval_jaxpr/okpa,pnabc->onbck/dot_general | solution.py:48
  379.5 3.0 fusion.98
  382.5 20.3 %fusion.101 = f32[2,96,96,96,1]{3,2,0,1,4:T(8,128)S(1)} fusion(f32[96,96,96]{2,1,0:T(8,128)S(1)} %fusion.98, f32[2,96,96,96,1]{3,2,0,1,4:T(8,128)S(1)} %fusion.100, f32[2,96,2,96]{3,1,2,0:T(8,128)S(1)} %get-tuple-element.209), kind=kOutput, calls=%fused_computation.6.clone.1 | convolution fusion | flops 4078632960 | bytes 17842176 | tf_op jit(solution)/shard_map/while/body/eval_jaxpr/okpa,pnabc->onbck/dot_general | solution.py:48
  402.7 19.3 %fusion.102 = f32[2,96,96,96,1]{3,2,0,1,4:T(8,128)S(1)} fusion(f32[2,96,96,96,1]{3,2,0,1,4:T(8,128)S(1)} %fusion.101, f32[2,96,2,96]{3,1,2,0:T(8,128)S(1)} %get-tuple-element.210), kind=kOutput, calls=%fused_computation.29.clone.1 | convolution fusion | flops 4076863488 | bytes 14303232 | tf_op jit(solution)/shard_map/while/body/eval_jaxpr/okpa,pnabc->onbck/dot_general | solution.py:53
  422.0 24.6 %fusion.103 = f32[2,96,96,96]{3,2,0,1:T(8,128)} fusion(f32[2,96,96,96,1]{3,2,0,1,4:T(8,128)S(1)} %fusion.102, f32[2,96,2,96]{3,1,2,0:T(8,128)S(1)} %get-tuple-element.210), kind=kOutput, calls=%fused_computation.30.clone.1 | convolution fusion | flops 4076863488 | bytes 14303232 | tf_op jit(solution)/shard_map/while/body/eval_jaxpr/okpa,pnabc->onbck/dot_general | solution.py:53
  446.7 28.5 %fusion.104 = f32[1,96,96,96]{3,2,1,0:T(8,128)} fusion(f32[1,96,96,96]{3,2,1,0:T(8,128)} %get-tuple-element.193, f32[2,96,96,96]{3,2,1,0:T(8,128)} %get-tuple-element.206, s32[]{:T(128)} %get-tuple-element.192, pred[]{:T(512)S(6)} %compare.3, f32[2,96,96,96]{3,2,0,1:T(8,128)} %fusion.103, f32[96,2,96]{2,0,1:T(8,128)S(1)} %get-tuple-element.211), kind=kOutput, calls=%fused_computation.23.clone.1 | convolution fusion | flops 2041970688 | bytes 17768452 | tf_op jit(solution)/shard_map/while/body/eval_jaxpr/kpa,pnabc->nbck/dot_general | solution.py:56
  476.8 6.1 %reshape.245 = f32[1,96,9216]{2,1,0:T(8,128)} reshape(f32[1,96,96,96]{3,2,1,0:T(8,128)} %get-tuple-element.52) | data formatting | bytes 7077888 | tf_op jit(solution)/shard_map/reshape | solution.py:88
  (5 shorter events, 0.1 us)
Async XLA Ops:
  0.0 193.8 %collective-permute-start = (f32[1,96,9216]{2,1,0:T(8,128)}, f32[1,96,9216]{2,1,0:T(8,128)}, u32[]{:S(2)}, u32[]{:S(2)}) collective-permute-start(f32[1,96,9216]{2,1,0:T(8,128)} %param.3), channel_id=1, source_target_pairs={{0,5},{1,6},{2,7},{3,8},{4,9},{5,10},{6,11},{7,12},{8,13},{9,14},{... | collective-permute-start | bytes 10616840 | tf_op jit(solution)/shard_map/ppermute | solution.py:16
  0.0 199.6 %collective-permute-start.1 = (f32[1,96,9216]{2,1,0:T(8,128)}, f32[1,96,9216]{2,1,0:T(8,128)}, u32[]{:S(2)}, u32[]{:S(2)}) collective-permute-start(f32[1,96,9216]{2,1,0:T(8,128)} %param.3), channel_id=1, source_target_pairs={{0,11},{1,12},{2,13},{3,14},{4,15},{5,0},{6,1},{7,2},{8,3},{9,4},{... | collective-permute-start | bytes 10616840 | tf_op jit(solution)/shard_map/ppermute | solution.py:16
where the time goes:
time: 487 us; the launch traced here: 483 us
  matrix products  245 us (50%)
  waiting for transfers between devices  183 us (38%)
  other arithmetic  25.4 us (5%)
  local copies, waits for them, and re-layouts  23.6 us (5%)
    ppermute x2, waiting for transfers between devices, from_behind(): lax.ppermute(value, axis, [(i, (i + by) % count) for i in range(count)])  183 us
    dot_general x4, matrix products, potentials(): jnp.einsum('okpa,pnabc->onbck', inverse_block, parts, precision=lax.Preci...  87.9 us
    dot_general x4, matrix products, potentials(): jnp.einsum('okpa,pnabc->onbck', forward_block, parts, precision=lax.Preci...  81.2 us
    dot_general x2, matrix products, potentials(): jnp.einsum('kpa,pnabc->nbck', inverse_block[0], parts, precision=lax.Prec...  56.3 us
    dot_general x2, matrix products, potentials(): jnp.einsum('oka,nabc->onbck', forward_first, density, precision=lax.Preci...  20 us
  transfers between devices with their start and end apart: 2, of which 1 were waited for; matrix products, arithmetic and copies ran while one was open for 3% of the time, Pallas kernels for 0%

commit v1 on v0

v1 whole, which is shorter than its diff:
```python
import functools
import math

import jax
import jax.numpy as jnp
import numpy as np
from jax import lax
from jax.experimental import pallas as pl
from jax.experimental.pallas import tpu as pltpu
from jax.sharding import PartitionSpec as P

OFFSET = 5
screening = 5.44
LANES = 128
X_STEPS = 6
PLANE_STEPS = 6


def from_behind(value, axis, by):
    count = lax.axis_size(axis)
    return lax.ppermute(value, axis, [(i, (i + by) % count) for i in range(count)])


def screened_kernel(points):
    signed = jnp.arange(points, dtype=jnp.int32)
    signed = jnp.where(signed >= points // 2, signed - points, signed)
    wavenumber = signed.astype(jnp.float32) * (2.0 * math.pi / points)
    squared = (
        wavenumber[:, None, None] ** 2
        + wavenumber[None, :, None] ** 2
        + wavenumber[None, None, :] ** 2
    )
    screen_rate = screening / points
    finite = jnp.where(squared > 0.0, squared, 1.0)
    screened = 4.0 * math.pi / finite * -jnp.expm1(-finite / (4.0 * screen_rate * screen_rate))
    kernel = jnp.where(squared > 0.0, screened, math.pi / (screen_rate * screen_rate))
    kernel = kernel / float(points * points * points)
    return jnp.pad(kernel, ((0, 0), (0, 0), (0, LANES - points)))


def hartley_tables(points):
    counter = np.arange(points)
    angles = 2.0 * np.pi * (counter[:, None] * counter[None, :] % points) / points
    table = np.cos(angles) + np.sin(angles)
    high = table.astype(jnp.bfloat16)
    low = (table - high.astype(np.float64)).astype(jnp.bfloat16)
    left = np.zeros((2 * points, 2 * points), jnp.bfloat16)
    left[:points, :points] = high
    left[:points, points:] = high
    left[points:, :points] = low
    right = np.zeros((2 * LANES, 2 * LANES), jnp.bfloat16)
    right[:points, :points] = high
    right[:points, LANES:LANES + points] = low
    right[LANES:LANES + points, :points] = high
    return jnp.asarray(left), jnp.asarray(right)


def two_terms(value, axis):
    high = value.astype(jnp.bfloat16)
    low = (value - high.astype(jnp.float32)).astype(jnp.bfloat16)
    return jnp.concatenate([high, low], axis)


def from_left(left, value):
    half = value.shape[0]
    out = jnp.dot(left, two_terms(value, 0), preferred_element_type=jnp.float32)
    return out[:half] + out[half:]


def from_right(value, right):
    out = jnp.dot(two_terms(value, 1), right, preferred_element_type=jnp.float32)
    return out[:, :LANES] + out[:, LANES:]


def pair_body(points, have_sum, both, *refs):
    refs = list(refs)
    a_ref, b_ref, kernel_ref, left_ref, right_ref = refs[:5]
    refs = refs[5:]
    sum_ref = refs.pop(0) if have_sum else None
    for_a_ref = refs.pop(0)
    for_b_ref = refs.pop(0) if both else None
    (held,) = refs
    step = pl.program_id(0)
    group = 4 * points
    columns = a_ref.shape[1]
    groups = columns // group
    rows_of = columns // points

    @pl.when(step < X_STEPS)
    def forward_x():
        left = left_ref[...]
        for part in range(groups):
            span = pl.ds(part * group, group)
            density = a_ref[:, span] * b_ref[:, span]
            spectrum = from_left(left, density)
            for q in range(4):
                row = step * rows_of + part * 4 + q
                piece = spectrum[:, q * points:(q + 1) * points]
                piece = jnp.concatenate([piece, jnp.zeros((points, LANES - points), jnp.float32)], 1)
                held[pl.ds(row, points, stride=points), :] = piece

    @pl.when((step >= X_STEPS) & (step < X_STEPS + PLANE_STEPS))
    def planes():
        left = left_ref[...]
        right = right_ref[...]
        per_step = points // PLANE_STEPS
        first = (step - X_STEPS) * per_step

        def two_planes(index, carry):
            start = pl.multiple_of((first + 2 * index) * points, points)
            block = held[pl.ds(start, 2 * points), :]
            block = from_right(block, right)
            wide = jnp.concatenate([block[:points], block[points:]], 1)
            wide = from_left(left, wide)
            scale = kernel_ref[pl.ds(2 * index, 2)]
            wide = wide * jnp.concatenate([scale[0], scale[1]], 1)
            wide = from_left(left, wide)
            block = jnp.concatenate([wide[:, :LANES], wide[:, LANES:]], 0)
            held[pl.ds(start, 2 * points), :] = from_right(block, right)
            return carry

        lax.fori_loop(0, per_step // 2, two_planes, 0, unroll=2)

    @pl.when(step >= X_STEPS + PLANE_STEPS)
    def inverse_x():
        left = left_ref[...]
        for part in range(groups):
            span = pl.ds(part * group, group)
            pieces = []
            for q in range(4):
                row = (step - X_STEPS - PLANE_STEPS) * rows_of + part * 4 + q
                pieces.append(held[pl.ds(row, points, stride=points), :][:, :points])
            potential = from_left(left, jnp.concatenate(pieces, 1))
            for_a = -b_ref[:, span] * potential
            if have_sum:
                for_a = for_a + sum_ref[:, span]
            for_a_ref[:, span] = for_a
            if both:
                for_b_ref[:, span] = -a_ref[:, span] * potential


def pair_terms(a, b, kernel, tables, running=None, both=False):
    points, plane = a.shape
    columns = plane // X_STEPS
    late = X_STEPS + PLANE_STEPS

    def ends(i):
        return (0, jnp.where(i < X_STEPS, i, jnp.where(i < late, X_STEPS - 1, i - late)))

    def tail(i):
        return (0, jnp.maximum(i - late, 0))

    def middle(i):
        return (jnp.clip(i - X_STEPS, 0, PLANE_STEPS - 1), 0, 0)

    wide = pl.BlockSpec((points, columns), ends)
    in_specs = [
        wide,
        wide,
        pl.BlockSpec((points // PLANE_STEPS, points, LANES), middle),
        pl.BlockSpec(tables[0].shape, lambda i: (0, 0)),
        pl.BlockSpec(tables[1].shape, lambda i: (0, 0)),
    ]
    operands = [a, b, kernel, *tables]
    if running is not None:
        in_specs.append(pl.BlockSpec((points, columns), tail))
        operands.append(running)
    n_out = 2 if both else 1
    out = pl.pallas_call(
        functools.partial(pair_body, points, running is not None, both),
        grid=(2 * X_STEPS + PLANE_STEPS,),
        in_specs=in_specs,
        out_specs=[pl.BlockSpec((points, columns), tail)] * n_out,
        out_shape=[jax.ShapeDtypeStruct((points, plane), jnp.float32)] * n_out,
        scratch_shapes=[pltpu.VMEM((points * points, LANES), jnp.float32)],
        compiler_params=pltpu.CompilerParams(vmem_limit_bytes=40 * 2**20),
        cost_estimate=pl.CostEstimate(
            flops=40_000_000_000, bytes_accessed=20_000_000, transcendentals=0
        ),
        name="pair_terms",
    )(*operands)
    return out if both else out[0]


def local(orbitals):
    bands, points, plane = orbitals.shape
    resident = orbitals[0]
    lower = from_behind(orbitals, "band", OFFSET)[0]
    upper = from_behind(orbitals, "band", -OFFSET)[0]
    tables = hartley_tables(points)
    kernel = screened_kernel(points)
    total = pair_terms(resident, lower, kernel, tables)
    total = pair_terms(resident, upper, kernel, tables, running=total)
    return total[None]


def solution(mesh):
    return jax.shard_map(
        local,
        mesh=mesh,
        in_specs=(P(("groups", "band"), None, None),),
        out_specs=P(("groups", "band"), None, None),
        check_vma=False,
    )
```

time: 487 us -> 273 us (0.56)
  the two profiles are of different devices: /device:TPU:26 before, /device:TPU:24 now
where the time goes in v1:
time: 273 us
  waiting for transfers between devices  184 us (67%)
  Pallas kernels  79.2 us (29%)
  starting transfers between devices  3.54 us (1%)
  other arithmetic  3.01 us (1%)
  local copies, waits for them, and re-layouts  2.82 us (1%)
    ppermute x2, waiting for transfers between devices, from_behind(): lax.ppermute(value, axis, [(i, (i + by) % count) for i in range(count)])  184 us
    pallas_call x2, Pallas kernels, pair_terms(): pl.pallas_call(functools.partial(pair_body, points, running is not None,...  79.2 us
  transfers between devices with their start and end apart: 2, of which 1 were waited for; matrix products, arithmetic and copies ran while one was open for 2% of the time, Pallas kernels for 14%

profile of v1, /device:TPU:24, one launch (start us, length us, event | category | flops | bytes accessed | tf_op | source)
XLA Modules:
  0.0 272.9 jit_solution(8413594366846299466)
XLA Ops:
  0.0 0.0 collective-permute-start.1
  0.0 3.5 %collective-permute-start = (f32[1,96,9216]{2,1,0:T(8,128)}, f32[1,96,9216]{2,1,0:T(8,128)S(1)}, u32[]{:S(2)}, u32[]{:S(2)}) collective-permute-start(f32[1,96,9216]{2,1,0:T(8,128)} %param.3), channel_id=1, source_target_pairs={{0,11},{1,12},{2,13},{3,14},{4,15},{5,0},{6,1},{7,2},{8,3},{9,4},{... | collective-permute-start | bytes 10616840 | tf_op jit(solution)/shard_map/ppermute | solution.py:21
  3.6 0.1 broadcast_add_fusion
  3.6 2.9 %fusion.4 = f32[96,96,96]{2,1,0:T(8,128)S(1)} fusion(f32[96]{0:T(128)S(1)} %fusion.10, f32[96,96]{1,0:T(8,128)S(1)} %broadcast_add_fusion), kind=kLoop, calls=%fused_computation.6 | loop fusion | flops 8847360 | bytes 3576192 | tf_op jit(solution)/shard_map/div | solution.py:37
  6.6 0.0 copy-start
  6.6 0.0 copy-start.1
  6.6 0.0 copy-start.2
  6.6 2.8 %pad.4.refs_2_ = f32[96,96,128]{2,1,0:T(8,128)} pad(f32[96,96,96]{2,1,0:T(8,128)S(1)} %fusion.4, f32[]{:T(128)} %constant.8.clone.1), padding=0_0x0_0x0_32 | pad | bytes 8257540 | tf_op jit(solution)/shard_map/jit(_pad)/pad | solution.py:38
  9.4 184.3 %collective-permute-done.1 = f32[1,96,9216]{2,1,0:T(8,128)S(1)} collective-permute-done((f32[1,96,9216]{2,1,0:T(8,128)}, f32[1,96,9216]{2,1,0:T(8,128)S(1)}, u32[]{:S(2)}, u32[]{:S(2)}) %collective-permute-start.1) | collective-permute-done | bytes 3538976 | tf_op jit(solution)/shard_map/ppermute | solution.py:21
  193.7 0.0 copy-done
  193.7 0.0 copy-done.1
  193.7 0.0 copy-done.2
  193.7 39.1 %pair_terms.2.refs_5_ = f32[96,9216]{1,0:T(8,128)S(1)} custom-call(f32[96,9216]{1,0:T(8,128)S(1)} %bitcast.4, f32[96,9216]{1,0:T(8,128)S(1)} %bitcast.7, f32[96,96,128]{2,1,0:T(8,128)} %pad.4.refs_2_, bf16[192,192]{1,0:T(8,128)(2,1)S(1)} %copy-done.2, bf16[256,256]{1,0:T(8,128)(2,1)S(1)} %copy-done.1), custom_call_target="tpu_custom_call" | custom-call | flops 40000000000 | bytes 20000000 | tf_op jit(solution)/shard_map/pair_terms/pallas_call | solution.py:169
  232.8 0.0 collective-permute-done
  232.8 40.1 %pair_terms.3 = f32[96,9216]{1,0:T(8,128)} custom-call(f32[96,9216]{1,0:T(8,128)S(1)} %bitcast.5, f32[96,9216]{1,0:T(8,128)S(1)} %bitcast.6, f32[96,96,128]{2,1,0:T(8,128)} %pad.4.refs_2_, bf16[192,192]{1,0:T(8,128)(2,1)S(1)} %copy-done.2, bf16[256,256]{1,0:T(8,128)(2,1)S(1)} %copy-done.1, f32[96,9216]{1,0:T(8,128)S(1)} %pair_terms.2.refs_5_), custom_call_target="tpu_custom_call" | custom-call | flops 40000000000 | bytes 20000000 | tf_op jit(solution)/shard_map/pair_terms/pallas_call | solution.py:169
  (1 shorter events, 0.0 us)
Async XLA Ops:
  0.0 193.7 %collective-permute-start.1 = (f32[1,96,9216]{2,1,0:T(8,128)}, f32[1,96,9216]{2,1,0:T(8,128)S(1)}, u32[]{:S(2)}, u32[]{:S(2)}) collective-permute-start(f32[1,96,9216]{2,1,0:T(8,128)} %param.3), channel_id=1, source_target_pairs={{0,5},{1,6},{2,7},{3,8},{4,9},{5,10},{6,11},{7,12},{8,13},{9,14},{... | collective-permute-start | bytes 10616840 | tf_op jit(solution)/shard_map/ppermute | solution.py:21
  0.0 232.8 %collective-permute-start = (f32[1,96,9216]{2,1,0:T(8,128)}, f32[1,96,9216]{2,1,0:T(8,128)S(1)}, u32[]{:S(2)}, u32[]{:S(2)}) collective-permute-start(f32[1,96,9216]{2,1,0:T(8,128)} %param.3), channel_id=1, source_target_pairs={{0,11},{1,12},{2,13},{3,14},{4,15},{5,0},{6,1},{7,2},{8,3},{9,4},{... | collective-permute-start | bytes 10616840 | tf_op jit(solution)/shard_map/ppermute | solution.py:21
  6.6 187.1 %copy-start = (f32[1,96,9216]{2,1,0:T(8,128)S(1)}, f32[1,96,9216]{2,1,0:T(8,128)}, u32[]{:S(2)}) copy-start(f32[1,96,9216]{2,1,0:T(8,128)} %param.3) | copy-start | bytes 10616836
  6.6 187.1 %copy-start.1 = (bf16[256,256]{1,0:T(8,128)(2,1)S(1)}, bf16[256,256]{1,0:T(8,128)(2,1)}, u32[]{:S(2)}) copy-start(bf16[256,256]{1,0:T(8,128)(2,1)} %constant.28.clone.refs_4_) | copy-start | bytes 393220
  6.6 187.1 %copy-start.2 = (bf16[192,192]{1,0:T(8,128)(2,1)S(1)}, bf16[192,192]{1,0:T(8,128)(2,1)}, u32[]{:S(2)}) copy-start(bf16[192,192]{1,0:T(8,128)(2,1)} %constant.27.clone.refs_3_) | copy-start | bytes 221188

commit v2 on v1

--- a/solution.py
+++ b/solution.py
@@ -81,62 +81,55 @@
     for_b_ref = refs.pop(0) if both else None
     (held,) = refs
     step = pl.program_id(0)
-    group = 4 * points
-    columns = a_ref.shape[1]
-    groups = columns // group
-    rows_of = columns // points
+    ys = a_ref.shape[1] // points
+    per_step = points // PLANE_STEPS
+
+    def lanes_apart(block):
+        gap = jnp.zeros((points, LANES - points), jnp.float32)
+        rows = [
+            jnp.concatenate([block[:, q * points:(q + 1) * points], gap], 1) for q in range(ys)
+        ]
+        return jnp.swapaxes(jnp.stack(rows, 0), 0, 1)
+
+    def lanes_together(block):
+        block = jnp.swapaxes(block, 0, 1)
+        return jnp.concatenate([block[q][:, :points] for q in range(ys)], 1)
+
+    def side_by_side(block):
+        return jnp.concatenate([block[i] for i in range(per_step)], 1)
 
     @pl.when(step < X_STEPS)
     def forward_x():
-        left = left_ref[...]
-        for part in range(groups):
-            span = pl.ds(part * group, group)
-            density = a_ref[:, span] * b_ref[:, span]
-            spectrum = from_left(left, density)
-            for q in range(4):
-                row = step * rows_of + part * 4 + q
-                piece = spectrum[:, q * points:(q + 1) * points]
-                piece = jnp.concatenate([piece, jnp.zeros((points, LANES - points), jnp.float32)], 1)
-                held[pl.ds(row, points, stride=points), :] = piece
+        spectrum = from_left(left_ref[...], a_ref[...] * b_ref[...])
+        start = pl.multiple_of(step * ys, ys)
+        held[:, pl.ds(start, ys), :] = lanes_apart(spectrum)
 
     @pl.when((step >= X_STEPS) & (step < X_STEPS + PLANE_STEPS))
     def planes():
         left = left_ref[...]
         right = right_ref[...]
-        per_step = points // PLANE_STEPS
         first = (step - X_STEPS) * per_step
-
-        def two_planes(index, carry):
-            start = pl.multiple_of((first + 2 * index) * points, points)
-            block = held[pl.ds(start, 2 * points), :]
-            block = from_right(block, right)
-            wide = jnp.concatenate([block[:points], block[points:]], 1)
-            wide = from_left(left, wide)
-            scale = kernel_ref[pl.ds(2 * index, 2)]
-            wide = wide * jnp.concatenate([scale[0], scale[1]], 1)
-            wide = from_left(left, wide)
-            block = jnp.concatenate([wide[:, :LANES], wide[:, LANES:]], 0)
-            held[pl.ds(start, 2 * points), :] = from_right(block, right)
-            return carry
-
-        lax.fori_loop(0, per_step // 2, two_planes, 0, unroll=2)
+        block = held[pl.ds(first, per_step)].reshape(per_step * points, LANES)
+        block = from_right(block, right).reshape(per_step, points, LANES)
+        wide = from_left(left, side_by_side(block))
+        wide = from_left(left, wide * side_by_side(kernel_ref[...]))
+        block = jnp.concatenate(
+            [wide[:, i * LANES:(i + 1) * LANES] for i in range(per_step)], 0
+        )
+        block = from_right(block, right)
+        held[pl.ds(first, per_step)] = block.reshape(per_step, points, LANES)
 
     @pl.when(step >= X_STEPS + PLANE_STEPS)
     def inverse_x():
-        left = left_ref[...]
-        for part in range(groups):
-            span = pl.ds(part * group, group)
-            pieces = []
-            for q in range(4):
-                row = (step - X_STEPS - PLANE_STEPS) * rows_of + part * 4 + q
-                pieces.append(held[pl.ds(row, points, stride=points), :][:, :points])
-            potential = from_left(left, jnp.concatenate(pieces, 1))
-            for_a = -b_ref[:, span] * potential
-            if have_sum:
-                for_a = for_a + sum_ref[:, span]
-            for_a_ref[:, span] = for_a
-            if both:
-                for_b_ref[:, span] = -a_ref[:, span] * potential
+        start = pl.multiple_of((step - X_STEPS - PLANE_STEPS) * ys, ys)
+        block = lanes_together(held[:, pl.ds(start, ys), :])
+        potential = from_left(left_ref[...], block)
+        for_a = -b_ref[...] * potential
+        if have_sum:
+            for_a = for_a + sum_ref[...]
+        for_a_ref[...] = for_a
+        if both:
+            for_b_ref[...] = -a_ref[...] * potential
 
 
 def pair_terms(a, b, kernel, tables, running=None, both=False):
@@ -172,7 +165,7 @@
         in_specs=in_specs,
         out_specs=[pl.BlockSpec((points, columns), tail)] * n_out,
         out_shape=[jax.ShapeDtypeStruct((points, plane), jnp.float32)] * n_out,
-        scratch_shapes=[pltpu.VMEM((points * points, LANES), jnp.float32)],
+        scratch_shapes=[pltpu.VMEM((points, points, LANES), jnp.float32)],
         compiler_params=pltpu.CompilerParams(vmem_limit_bytes=40 * 2**20),
         cost_estimate=pl.CostEstimate(
             flops=40_000_000_000, bytes_accessed=20_000_000, transcendentals=0

time: 273 us -> 228 us (0.84)
  Pallas kernels: 79.2 us -> 34.1 us
    pallas_call x2, Pallas kernels: 79.2 us -> 34.1 us  [pair_terms(): pl.pallas_call(functools.partial(pair_body, points, running is not None,...]
  transfers between devices with their start and end apart: 2 -> 2, of which waited for: 1 -> 1; matrix products, arithmetic and copies ran while one was open for 2% -> 3% of each run, Pallas kernels for 14% -> 7%
where the time goes in v2:
time: 228 us
  waiting for transfers between devices  184 us (81%)
  Pallas kernels  34.1 us (15%)
  starting transfers between devices  3.54 us (2%)
  other arithmetic  3.01 us (1%)
  local copies, waits for them, and re-layouts  2.82 us (1%)
    ppermute x2, waiting for transfers between devices, from_behind(): lax.ppermute(value, axis, [(i, (i + by) % count) for i in range(count)])  184 us
    pallas_call x2, Pallas kernels, pair_terms(): pl.pallas_call(functools.partial(pair_body, points, running is not None,...  34.1 us
  transfers between devices with their start and end apart: 2, of which 1 were waited for; matrix products, arithmetic and copies ran while one was open for 3% of the time, Pallas kernels for 7%

profile of v2, /device:TPU:24, one launch (start us, length us, event | category | flops | bytes accessed | tf_op | source)
XLA Modules:
  0.0 227.8 jit_solution(13120869093826756185)
XLA Ops:
  0.0 0.0 collective-permute-start.1
  0.0 3.5 %collective-permute-start = (f32[1,96,9216]{2,1,0:T(8,128)}, f32[1,96,9216]{2,1,0:T(8,128)S(1)}, u32[]{:S(2)}, u32[]{:S(2)}) collective-permute-start(f32[1,96,9216]{2,1,0:T(8,128)} %param.3), channel_id=1, source_target_pairs={{0,11},{1,12},{2,13},{3,14},{4,15},{5,0},{6,1},{7,2},{8,3},{9,4},{... | collective-permute-start | bytes 10616840 | tf_op jit(solution)/shard_map/ppermute | solution.py:21
  3.6 0.1 broadcast_add_fusion
  3.6 2.9 %fusion.4 = f32[96,96,96]{2,1,0:T(8,128)S(1)} fusion(f32[96]{0:T(128)S(1)} %fusion.10, f32[96,96]{1,0:T(8,128)S(1)} %broadcast_add_fusion), kind=kLoop, calls=%fused_computation.6 | loop fusion | flops 8847360 | bytes 3576192 | tf_op jit(solution)/shard_map/div | solution.py:37
  6.6 0.0 copy-start
  6.6 0.0 copy-start.1
  6.6 0.0 copy-start.2
  6.6 2.8 %pad.4.refs_2_ = f32[96,96,128]{2,1,0:T(8,128)} pad(f32[96,96,96]{2,1,0:T(8,128)S(1)} %fusion.4, f32[]{:T(128)} %constant.8.clone.1), padding=0_0x0_0x0_32 | pad | bytes 8257540 | tf_op jit(solution)/shard_map/jit(_pad)/pad | solution.py:38
  9.4 184.3 %collective-permute-done.1 = f32[1,96,9216]{2,1,0:T(8,128)S(1)} collective-permute-done((f32[1,96,9216]{2,1,0:T(8,128)}, f32[1,96,9216]{2,1,0:T(8,128)S(1)}, u32[]{:S(2)}, u32[]{:S(2)}) %collective-permute-start.1) | collective-permute-done | bytes 3538976 | tf_op jit(solution)/shard_map/ppermute | solution.py:21
  193.7 0.0 copy-done
  193.7 0.0 copy-done.1
  193.7 0.0 copy-done.2
  193.7 16.5 %pair_terms.2.refs_5_ = f32[96,9216]{1,0:T(8,128)S(1)} custom-call(f32[96,9216]{1,0:T(8,128)S(1)} %bitcast.4, f32[96,9216]{1,0:T(8,128)S(1)} %bitcast.7, f32[96,96,128]{2,1,0:T(8,128)} %pad.4.refs_2_, bf16[192,192]{1,0:T(8,128)(2,1)S(1)} %copy-done.2, bf16[256,256]{1,0:T(8,128)(2,1)S(1)} %copy-done.1), custom_call_target="tpu_custom_call" | custom-call | flops 40000000000 | bytes 20000000 | tf_op jit(solution)/shard_map/pair_terms/pallas_call | solution.py:162
  210.1 0.0 collective-permute-done
  210.1 17.7 %pair_terms.3 = f32[96,9216]{1,0:T(8,128)} custom-call(f32[96,9216]{1,0:T(8,128)S(1)} %bitcast.5, f32[96,9216]{1,0:T(8,128)S(1)} %bitcast.6, f32[96,96,128]{2,1,0:T(8,128)} %pad.4.refs_2_, bf16[192,192]{1,0:T(8,128)(2,1)S(1)} %copy-done.2, bf16[256,256]{1,0:T(8,128)(2,1)S(1)} %copy-done.1, f32[96,9216]{1,0:T(8,128)S(1)} %pair_terms.2.refs_5_), custom_call_target="tpu_custom_call" | custom-call | flops 40000000000 | bytes 20000000 | tf_op jit(solution)/shard_map/pair_terms/pallas_call | solution.py:162
  (1 shorter events, 0.0 us)
Async XLA Ops:
  0.0 193.7 %collective-permute-start.1 = (f32[1,96,9216]{2,1,0:T(8,128)}, f32[1,96,9216]{2,1,0:T(8,128)S(1)}, u32[]{:S(2)}, u32[]{:S(2)}) collective-permute-start(f32[1,96,9216]{2,1,0:T(8,128)} %param.3), channel_id=1, source_target_pairs={{0,5},{1,6},{2,7},{3,8},{4,9},{5,10},{6,11},{7,12},{8,13},{9,14},{... | collective-permute-start | bytes 10616840 | tf_op jit(solution)/shard_map/ppermute | solution.py:21
  0.0 210.1 %collective-permute-start = (f32[1,96,9216]{2,1,0:T(8,128)}, f32[1,96,9216]{2,1,0:T(8,128)S(1)}, u32[]{:S(2)}, u32[]{:S(2)}) collective-permute-start(f32[1,96,9216]{2,1,0:T(8,128)} %param.3), channel_id=1, source_target_pairs={{0,11},{1,12},{2,13},{3,14},{4,15},{5,0},{6,1},{7,2},{8,3},{9,4},{... | collective-permute-start | bytes 10616840 | tf_op jit(solution)/shard_map/ppermute | solution.py:21
  6.6 187.1 %copy-start = (f32[1,96,9216]{2,1,0:T(8,128)S(1)}, f32[1,96,9216]{2,1,0:T(8,128)}, u32[]{:S(2)}) copy-start(f32[1,96,9216]{2,1,0:T(8,128)} %param.3) | copy-start | bytes 10616836
  6.6 187.1 %copy-start.1 = (bf16[256,256]{1,0:T(8,128)(2,1)S(1)}, bf16[256,256]{1,0:T(8,128)(2,1)}, u32[]{:S(2)}) copy-start(bf16[256,256]{1,0:T(8,128)(2,1)} %constant.28.clone.refs_4_) | copy-start | bytes 393220
  6.6 187.1 %copy-start.2 = (bf16[192,192]{1,0:T(8,128)(2,1)S(1)}, bf16[192,192]{1,0:T(8,128)(2,1)}, u32[]{:S(2)}) copy-start(bf16[192,192]{1,0:T(8,128)(2,1)} %constant.27.clone.refs_3_) | copy-start | bytes 221188

commit v3 on v2

--- a/solution.py
+++ b/solution.py
@@ -72,17 +72,22 @@
     return out[:, :LANES] + out[:, LANES:]
 
 
-def pair_body(points, have_sum, both, *refs):
+def pair_body(points, has, *refs):
     refs = list(refs)
-    a_ref, b_ref, kernel_ref, left_ref, right_ref = refs[:5]
-    refs = refs[5:]
-    sum_ref = refs.pop(0) if have_sum else None
+    a_ref, b_ref = refs.pop(0), refs.pop(0)
+    more_ref = refs.pop(0) if "more" in has else None
+    kernel_ref, left_ref, right_ref = refs.pop(0), refs.pop(0), refs.pop(0)
+    sum_a_ref = refs.pop(0) if "sum_a" in has else None
+    sum_b_ref = refs.pop(0) if "sum_b" in has else None
     for_a_ref = refs.pop(0)
-    for_b_ref = refs.pop(0) if both else None
+    for_b_ref = refs.pop(0) if "for_b" in has else None
     (held,) = refs
     step = pl.program_id(0)
     ys = a_ref.shape[1] // points
     per_step = points // PLANE_STEPS
+
+    def visitor():
+        return b_ref[...] if more_ref is None else b_ref[...] + more_ref[...]
 
     def lanes_apart(block):
         gap = jnp.zeros((points, LANES - points), jnp.float32)
@@ -100,7 +105,7 @@
 
     @pl.when(step < X_STEPS)
     def forward_x():
-        spectrum = from_left(left_ref[...], a_ref[...] * b_ref[...])
+        spectrum = from_left(left_ref[...], a_ref[...] * visitor())
         start = pl.multiple_of(step * ys, ys)
         held[:, pl.ds(start, ys), :] = lanes_apart(spectrum)
 
@@ -124,18 +129,18 @@
         start = pl.multiple_of((step - X_STEPS - PLANE_STEPS) * ys, ys)
         block = lanes_together(held[:, pl.ds(start, ys), :])
         potential = from_left(left_ref[...], block)
-        for_a = -b_ref[...] * potential
-        if have_sum:
-            for_a = for_a + sum_ref[...]
-        for_a_ref[...] = for_a
-        if both:
-            for_b_ref[...] = -a_ref[...] * potential
-
-
-def pair_terms(a, b, kernel, tables, running=None, both=False):
+        for_a = visitor() * potential
+        for_a_ref[...] = -for_a if sum_a_ref is None else sum_a_ref[...] - for_a
+        if for_b_ref is not None:
+            for_b = a_ref[...] * potential
+            for_b_ref[...] = -for_b if sum_b_ref is None else sum_b_ref[...] - for_b
+
+
+def pair_terms(a, b, constants, more=None, sum_a=None, sum_b=None, for_b=False):
     points, plane = a.shape
     columns = plane // X_STEPS
     late = X_STEPS + PLANE_STEPS
+    kernel, left, right = constants
 
     def ends(i):
         return (0, jnp.where(i < X_STEPS, i, jnp.where(i < late, X_STEPS - 1, i - late)))
@@ -146,50 +151,139 @@
     def middle(i):
         return (jnp.clip(i - X_STEPS, 0, PLANE_STEPS - 1), 0, 0)
 
-    wide = pl.BlockSpec((points, columns), ends)
-    in_specs = [
-        wide,
-        wide,
-        pl.BlockSpec((points // PLANE_STEPS, points, LANES), middle),
-        pl.BlockSpec(tables[0].shape, lambda i: (0, 0)),
-        pl.BlockSpec(tables[1].shape, lambda i: (0, 0)),
-    ]
-    operands = [a, b, kernel, *tables]
-    if running is not None:
-        in_specs.append(pl.BlockSpec((points, columns), tail))
-        operands.append(running)
-    n_out = 2 if both else 1
+    def whole(i):
+        return (0, 0)
+
+    at_ends = pl.BlockSpec((points, columns), ends)
+    at_tail = pl.BlockSpec((points, columns), tail)
+    operands = [(None, a, at_ends), (None, b, at_ends), ("more", more, at_ends)]
+    operands.append((None, kernel, pl.BlockSpec((points // PLANE_STEPS, points, LANES), middle)))
+    operands.append((None, left, pl.BlockSpec(left.shape, whole)))
+    operands.append((None, right, pl.BlockSpec(right.shape, whole)))
+    operands += [("sum_a", sum_a, at_tail), ("sum_b", sum_b, at_tail)]
+    operands = [entry for entry in operands if entry[1] is not None]
+    has = [name for name, value, spec in operands if name] + ["for_b"] * for_b
+    n_out = 2 if for_b else 1
     out = pl.pallas_call(
-        functools.partial(pair_body, points, running is not None, both),
+        functools.partial(pair_body, points, has),
         grid=(2 * X_STEPS + PLANE_STEPS,),
-        in_specs=in_specs,
-        out_specs=[pl.BlockSpec((points, columns), tail)] * n_out,
+        in_specs=[spec for name, value, spec in operands],
+        out_specs=[at_tail] * n_out,
         out_shape=[jax.ShapeDtypeStruct((points, plane), jnp.float32)] * n_out,
         scratch_shapes=[pltpu.VMEM((points, points, LANES), jnp.float32)],
-        compiler_params=pltpu.CompilerParams(vmem_limit_bytes=40 * 2**20),
+        compiler_params=pltpu.CompilerParams(vmem_limit_bytes=60 * 2**20),
         cost_estimate=pl.CostEstimate(
-            flops=40_000_000_000, bytes_accessed=20_000_000, transcendentals=0
+            flops=16_000_000_000, bytes_accessed=20_000_000, transcendentals=0
         ),
         name="pair_terms",
-    )(*operands)
-    return out if both else out[0]
-
-
-def local(orbitals):
-    bands, points, plane = orbitals.shape
-    resident = orbitals[0]
+    )(*[value for name, value, spec in operands])
+    return out if for_b else out[0]
+
+
+def corner_body(block_ref, kernel_ref, corner_ref, sem):
+    copy = pltpu.make_async_copy(block_ref.at[pl.ds(0, 8), pl.ds(0, LANES)], corner_ref, sem)
+    copy.start()
+    copy.wait()
+
+
+def corner(block, kernel):
+    anywhere = pl.BlockSpec(memory_space=pl.ANY)
+    return pl.pallas_call(
+        corner_body,
+        in_specs=[anywhere, anywhere],
+        out_specs=pl.BlockSpec(memory_space=pltpu.VMEM),
+        out_shape=jax.ShapeDtypeStruct((8, LANES), block.dtype),
+        scratch_shapes=[pltpu.SemaphoreType.DMA],
+        compiler_params=pltpu.CompilerParams(vmem_limit_bytes=60 * 2**20),
+        name="corner",
+    )(block, kernel)
+
+
+def after_body(token_ref, left_ref, block_ref, new_left_ref, new_block_ref, sem):
+    copy = pltpu.make_async_copy(block_ref, new_block_ref, sem)
+    copy.start()
+    new_left_ref[...] = left_ref[...]
+    copy.wait()
+
+
+def after(token, left, block):
+    in_vmem = pl.BlockSpec(memory_space=pltpu.VMEM)
+    anywhere = pl.BlockSpec(memory_space=pl.ANY)
+    return pl.pallas_call(
+        after_body,
+        in_specs=[in_vmem, in_vmem, anywhere],
+        out_specs=[in_vmem, anywhere],
+        out_shape=[
+            jax.ShapeDtypeStruct(left.shape, left.dtype),
+            jax.ShapeDtypeStruct(block.shape, block.dtype),
+        ],
+        scratch_shapes=[pltpu.SemaphoreType.DMA],
+        compiler_params=pltpu.CompilerParams(vmem_limit_bytes=60 * 2**20),
+        name="after",
+    )(token, left, block)
+
+
+def both_halves(*pairs):
+    return list(pairs) + [(15 - source, 15 - target) for source, target in pairs]
+
+
+CROSSING = both_halves((3, 14), (4, 9))
+PARTNERS = both_halves((8, 14), (15, 9))
+TURN_FIRST = both_halves((9, 11), (14, 12))
+TURN_SECOND = both_halves((11, 14), (12, 9))
+ARRIVED = both_halves((14, 2), (9, 5))
+SINGLES = both_halves((5, 10), (2, 13))
+BESIDE = both_halves((13, 14), (10, 9))
+HOME_ACROSS = both_halves((9, 4), (14, 3))
+HOME_FAR = both_halves((9, 15), (14, 8))
+HOME_BESIDE = both_halves((9, 10), (14, 13))
+
+
+def sixteen_bands(orbitals, constants):
+    def send(value, pairs):
+        return lax.ppermute(value, "band", pairs)
+
+    own = orbitals[0]
+    crossed = send(orbitals, CROSSING)[0]
+    partner = send(orbitals, PARTNERS)[0]
+    turned = send(orbitals, TURN_FIRST)
+    kernel, left, right = constants
+    token = send(corner(crossed, kernel)[None], ARRIVED)
+    left, held_back = after(token[0], left, orbitals)
+    constants = (kernel, left, right)
+    single = send(held_back, SINGLES)[0]
+    beside = send(held_back, BESIDE)[0]
+    turned = send(turned, TURN_SECOND)[0]
+
+    partner_sum, crossed_sum = pair_terms(partner, crossed, constants, for_b=True)
+    own_sum, crossed_sum = pair_terms(own, crossed, constants, sum_b=crossed_sum, for_b=True)
+    home = send(crossed_sum[None], HOME_ACROSS)[0]
+    partner_sum, beside_sum = pair_terms(partner, beside, constants, sum_a=partner_sum, for_b=True)
+    home_far = send(partner_sum[None], HOME_FAR)[0]
+    home_beside = send(beside_sum[None], HOME_BESIDE)[0]
+    own_sum = pair_terms(own, single, constants, more=turned, sum_a=own_sum)
+    return (own_sum + home + home_beside + home_far)[None]
+
+
+def any_bands(orbitals, constants):
+    own = orbitals[0]
     lower = from_behind(orbitals, "band", OFFSET)[0]
     upper = from_behind(orbitals, "band", -OFFSET)[0]
-    tables = hartley_tables(points)
-    kernel = screened_kernel(points)
-    total = pair_terms(resident, lower, kernel, tables)
-    total = pair_terms(resident, upper, kernel, tables, running=total)
-    return total[None]
+    total = pair_terms(own, lower, constants)
+    return pair_terms(own, upper, constants, sum_a=total)[None]
+
+
+def local(bands, orbitals):
+    points = orbitals.shape[1]
+    constants = (screened_kernel(points), *hartley_tables(points))
+    if bands == 16:
+        return sixteen_bands(orbitals, constants)
+    return any_bands(orbitals, constants)
 
 
 def solution(mesh):
     return jax.shard_map(
-        local,
+        functools.partial(local, mesh.shape["band"]),
         mesh=mesh,
         in_specs=(P(("groups", "band"), None, None),),
         out_specs=P(("groups", "band"), None, None),

time: 228 us -> 306 us (1.34)
  the two profiles are of different devices: /device:TPU:24 before, /device:TPU:0 now
where the time goes in v3:
time: 306 us; the launch traced here: 305 us
  Pallas kernels  201 us (66%)
  waiting for transfers between devices  61 us (20%)
  starting transfers between devices  27.6 us (9%)
  other arithmetic  9.57 us (3%)
  local copies, waits for them, and re-layouts  4.94 us (2%)
    pallas_call x1, Pallas kernels, after(): pl.pallas_call(after_body, in_specs=[in_vmem, in_vmem, anywhere], out_spe...  110 us
    pallas_call x4, Pallas kernels, pair_terms(): pl.pallas_call(functools.partial(pair_body, points, has), grid=(2 * X_STE...  90.3 us
    ppermute x10, waiting for transfers between devices, send(): return lax.ppermute(value, 'band', pairs)  61 us
    ppermute x10, starting transfers between devices, send(): return lax.ppermute(value, 'band', pairs)  27.6 us
    broadcast_in_dim x1, other arithmetic, sixteen_bands(): return (own_sum + home + home_beside + home_far)[None]  6.57 us
  transfers between devices with their start and end apart: 10, of which 1 were waited for; matrix products, arithmetic and copies ran while one was open for 2% of the time, Pallas kernels for 66%

profile of v3, /device:TPU:0, one launch (start us, length us, event | category | flops | bytes accessed | tf_op | source)
XLA Modules:
  0.0 304.6 jit_solution(16894859852124062442)
XLA Ops:
  0.0 0.9 collective-permute-start
  0.9 2.5 collective-permute-start.3
  3.3 11.7 %collective-permute-start.5 = (f32[1,96,9216]{2,1,0:T(8,128)}, f32[1,96,9216]{2,1,0:T(8,128)}, u32[]{:S(2)}, u32[]{:S(2)}) collective-permute-start(f32[1,96,9216]{2,1,0:T(8,128)} %block_ref.1), channel_id=1, source_target_pairs={{8,14},{15,9},{7,1},{0,6},{24,30},{31,25},{23,17},{16,22}} | collective-permute-start | bytes 10616840 | tf_op jit(solution)/shard_map/ppermute | solution.py:244
  15.1 0.1 broadcast_add_fusion
  15.1 2.9 fusion.4
  18.1 2.6 pad.4.kernel_ref.refs_2_.refs_3_
  20.6 0.0 collective-permute-done
  20.6 0.0 copy-start
  20.6 1.8 copy-done
  22.4 1.3 corner.1
  23.7 0.7 collective-permute-start.1
  24.4 0.0 collective-permute-done.1
  24.4 0.0 copy-start.1
  24.4 0.6 copy-done.1
  25.0 109.8 %after.1 = (bf16[192,192]{1,0:T(8,128)(2,1)}, f32[1,96,9216]{2,1,0:T(8,128)}) custom-call(f32[8,128]{1,0:T(8,128)} %bitcast.31, bf16[192,192]{1,0:T(8,128)(2,1)} %constant.27.clone.left_ref, f32[1,96,9216]{2,1,0:T(8,128)} %block_ref.1), custom_call_target="tpu_custom_call" | custom-call | tf_op jit(solution)/shard_map/after/pallas_call | solution.py:212
  134.8 2.4 collective-permute-start.7
  137.2 0.0 collective-permute-done.3
  137.2 2.4 collective-permute-start.4
  139.7 2.5 collective-permute-start.2
  142.1 0.0 collective-permute-done.5
  142.1 21.7 %pair_terms.4 = (f32[96,9216]{1,0:T(8,128)}, f32[96,9216]{1,0:T(8,128)}) custom-call(f32[96,9216]{1,0:T(8,128)} %bitcast.6.refs_0_, f32[96,9216]{1,0:T(8,128)} %bitcast.26, f32[96,96,128]{2,1,0:T(8,128)} %pad.4.kernel_ref.refs_2_.refs_3_, bf16[192,192]{1,0:T(8,128)(2,1)} %get-tuple-element.14.refs_3_.refs_4_, bf16[256,256]{1,0:T(8,128)(2,1)} %constant.28.clone.refs_4_.refs_5_), custom_call_target="tpu_custom_call" | custom-call | flops 16000000000 | bytes 20000000 | tf_op jit(solution)/shard_map/pair_terms/pallas_call | solution.py:167
  163.8 22.5 %pair_terms.5 = (f32[96,9216]{1,0:T(8,128)}, f32[96,9216]{1,0:T(8,128)}) custom-call(f32[96,9216]{1,0:T(8,128)} %bitcast.28, f32[96,9216]{1,0:T(8,128)} %bitcast.27, f32[96,96,128]{2,1,0:T(8,128)} %pad.4.kernel_ref.refs_2_.refs_3_, bf16[192,192]{1,0:T(8,128)(2,1)} %get-tuple-element.14.refs_3_.refs_4_, bf16[256,256]{1,0:T(8,128)(2,1)} %constant.28.clone.refs_4_.refs_5_, ...), custom_call_target="tpu_custom_call" | custom-call | flops 16000000000 | bytes 20000000 | tf_op jit(solution)/shard_map/pair_terms/pallas_call | solution.py:167
  186.3 0.9 collective-permute-start.6
  187.2 0.0 collective-permute-done.7
  187.2 22.4 %pair_terms.7 = (f32[96,9216]{1,0:T(8,128)}, f32[96,9216]{1,0:T(8,128)}) custom-call(f32[96,9216]{1,0:T(8,128)} %bitcast.6.refs_0_, f32[96,9216]{1,0:T(8,128)} %bitcast.9.refs_1_, f32[96,96,128]{2,1,0:T(8,128)} %pad.4.kernel_ref.refs_2_.refs_3_, bf16[192,192]{1,0:T(8,128)(2,1)} %get-tuple-element.14.refs_3_.refs_4_, ...), custom_call_target="tpu_custom_call" | custom-call | flops 16000000000 | bytes 20000000 | tf_op jit(solution)/shard_map/pair_terms/pallas_call | solution.py:167
  209.6 1.3 collective-permute-start.9
  210.9 2.4 collective-permute-start.8
  213.3 0.0 collective-permute-done.4
  213.3 0.0 collective-permute-done.2
  213.3 23.7 %pair_terms.6 = f32[96,9216]{1,0:T(8,128)} custom-call(f32[96,9216]{1,0:T(8,128)} %bitcast.29, f32[96,9216]{1,0:T(8,128)} %bitcast.4.refs_1_, f32[96,9216]{1,0:T(8,128)} %bitcast.5.refs_2_, f32[96,96,128]{2,1,0:T(8,128)} %pad.4.kernel_ref.refs_2_.refs_3_, bf16[192,192]{1,0:T(8,128)(2,1)} %get-tuple-element.14.refs_3_.refs_4_, ...), custom_call_target="tpu_custom_call" | custom-call | flops 16000000000 | bytes 20000000 | tf_op jit(solution)/shard_map/pair_terms/pallas_call | solution.py:167
  237.0 0.0 collective-permute-done.6
  237.0 61.0 %collective-permute-done.9 = f32[1,96,9216]{2,1,0:T(8,128)} collective-permute-done((f32[1,96,9216]{2,1,0:T(8,128)}, f32[1,96,9216]{2,1,0:T(8,128)}, u32[]{:S(2)}, u32[]{:S(2)}) %collective-permute-start.9) | collective-permute-done | bytes 3538976 | tf_op jit(solution)/shard_map/ppermute | solution.py:244
  298.0 0.0 collective-permute-done.8
  298.0 6.6 %fusion.8 = f32[1,96,9216]{2,1,0:T(8,128)} fusion(f32[1,96,9216]{2,1,0:T(8,128)} %collective-permute-done.9, f32[1,96,9216]{2,1,0:T(8,128)} %collective-permute-done.8, f32[96,9216]{1,0:T(8,128)} %pair_terms.6, f32[1,96,9216]{2,1,0:T(8,128)S(1)} %collective-permute-done.6), kind=kLoop, calls=%fused_computation.11 | loop fusion | flops 2654208 | bytes 17694720 | tf_op jit(solution)/shard_map/broadcast_in_dim | solution.py:265
  (1 shorter events, 0.0 us)
Async XLA Ops:
  0.0 20.6 %collective-permute-start = (f32[1,96,9216]{2,1,0:T(8,128)}, f32[1,96,9216]{2,1,0:T(8,128)S(1)}, u32[]{:S(2)}, u32[]{:S(2)}) collective-permute-start(f32[1,96,9216]{2,1,0:T(8,128)} %block_ref.1), channel_id=1, source_target_pairs={{3,14},{4,9},{12,1},{11,6},{19,30},{20,25},{28,17},{27,22}} | collective-permute-start | bytes 10616840 | tf_op jit(solution)/shard_map/ppermute | solution.py:244
  0.9 136.4 %collective-permute-start.3 = (f32[1,96,9216]{2,1,0:T(8,128)}, f32[1,96,9216]{2,1,0:T(8,128)}, u32[]{:S(2)}, u32[]{:S(2)}) collective-permute-start(f32[1,96,9216]{2,1,0:T(8,128)} %block_ref.1), channel_id=1, source_target_pairs={{9,11},{14,12},{6,4},{1,3},{25,27},{30,28},{22,20},{17,19}} | collective-permute-start | bytes 10616840 | tf_op jit(solution)/shard_map/ppermute | solution.py:244
  3.3 138.8 %collective-permute-start.5 = (f32[1,96,9216]{2,1,0:T(8,128)}, f32[1,96,9216]{2,1,0:T(8,128)}, u32[]{:S(2)}, u32[]{:S(2)}) collective-permute-start(f32[1,96,9216]{2,1,0:T(8,128)} %block_ref.1), channel_id=1, source_target_pairs={{8,14},{15,9},{7,1},{0,6},{24,30},{31,25},{23,17},{16,22}} | collective-permute-start | bytes 10616840 | tf_op jit(solution)/shard_map/ppermute | solution.py:244
  20.6 1.8 copy-start
  23.7 0.7 collective-permute-start.1
  24.4 0.6 copy-start.1
  134.8 52.3 %collective-permute-start.7 = (f32[1,96,9216]{2,1,0:T(8,128)}, f32[1,96,9216]{2,1,0:T(8,128)}, u32[]{:S(2)}, u32[]{:S(2)}) collective-permute-start(f32[1,96,9216]{2,1,0:T(8,128)} %get-tuple-element.13), channel_id=1, source_target_pairs={{13,14},{10,9},{2,1},{5,6},{29,30},{26,25},{18,17},{21,22}} | collective-permute-start | bytes 10616840 | tf_op jit(solution)/shard_map/ppermute | solution.py:244
  137.2 76.1 %collective-permute-start.4 = (f32[1,96,9216]{2,1,0:T(8,128)}, f32[1,96,9216]{2,1,0:T(8,128)}, u32[]{:S(2)}, u32[]{:S(2)}) collective-permute-start(f32[1,96,9216]{2,1,0:T(8,128)} %collective-permute-done.3), channel_id=1, source_target_pairs={{11,14},{12,9},{4,1},{3,6},{27,30},{28,25},{20,17},{19,22}} | collective-permute-start | bytes 10616840 | tf_op jit(solution)/shard_map/ppermute | solution.py:244
  139.7 73.7 %collective-permute-start.2 = (f32[1,96,9216]{2,1,0:T(8,128)}, f32[1,96,9216]{2,1,0:T(8,128)}, u32[]{:S(2)}, u32[]{:S(2)}) collective-permute-start(f32[1,96,9216]{2,1,0:T(8,128)} %get-tuple-element.13), channel_id=1, source_target_pairs={{5,10},{2,13},{10,5},{13,2},{21,26},{18,29},{26,21},{29,18}} | collective-permute-start | bytes 10616840 | tf_op jit(solution)/shard_map/ppermute | solution.py:244
  186.3 50.7 %collective-permute-start.6 = (f32[1,96,9216]{2,1,0:T(8,128)}, f32[1,96,9216]{2,1,0:T(8,128)S(1)}, u32[]{:S(2)}, u32[]{:S(2)}) collective-permute-start(f32[1,96,9216]{2,1,0:T(8,128)} %bitcast.32), channel_id=1, source_target_pairs={{9,4},{14,3},{6,11},{1,12},{25,20},{30,19},{22,27},{17,28}} | collective-permute-start | bytes 10616840 | tf_op jit(solution)/shard_map/ppermute | solution.py:244
  209.6 88.4 %collective-permute-start.9 = (f32[1,96,9216]{2,1,0:T(8,128)}, f32[1,96,9216]{2,1,0:T(8,128)}, u32[]{:S(2)}, u32[]{:S(2)}) collective-permute-start(f32[1,96,9216]{2,1,0:T(8,128)} %bitcast.34), channel_id=1, source_target_pairs={{9,15},{14,8},{6,0},{1,7},{25,31},{30,24},{22,16},{17,23}} | collective-permute-start | bytes 10616840 | tf_op jit(solution)/shard_map/ppermute | solution.py:244
  210.9 87.1 %collective-permute-start.8 = (f32[1,96,9216]{2,1,0:T(8,128)}, f32[1,96,9216]{2,1,0:T(8,128)}, u32[]{:S(2)}, u32[]{:S(2)}) collective-permute-start(f32[1,96,9216]{2,1,0:T(8,128)} %bitcast.33), channel_id=1, source_target_pairs={{9,10},{14,13},{6,5},{1,2},{25,26},{30,29},{22,21},{17,18}} | collective-permute-start | bytes 10616840 | tf_op jit(solution)/shard_map/ppermute | solution.py:244

commit v4 on v3

--- a/solution.py
+++ b/solution.py
@@ -44,10 +44,7 @@
     table = np.cos(angles) + np.sin(angles)
     high = table.astype(jnp.bfloat16)
     low = (table - high.astype(np.float64)).astype(jnp.bfloat16)
-    left = np.zeros((2 * points, 2 * points), jnp.bfloat16)
-    left[:points, :points] = high
-    left[:points, points:] = high
-    left[points:, :points] = low
+    left = np.concatenate([high, high, low], 1)
     right = np.zeros((2 * LANES, 2 * LANES), jnp.bfloat16)
     right[:points, :points] = high
     right[:points, LANES:LANES + points] = low
@@ -55,39 +52,67 @@
     return jnp.asarray(left), jnp.asarray(right)
 
 
-def two_terms(value, axis):
+def two_terms(value):
     high = value.astype(jnp.bfloat16)
     low = (value - high.astype(jnp.float32)).astype(jnp.bfloat16)
-    return jnp.concatenate([high, low], axis)
+    return high, low
 
 
 def from_left(left, value):
-    half = value.shape[0]
-    out = jnp.dot(left, two_terms(value, 0), preferred_element_type=jnp.float32)
-    return out[:half] + out[half:]
+    high, low = two_terms(value)
+    terms = jnp.concatenate([high, low, high], 0)
+    return jnp.dot(left, terms, preferred_element_type=jnp.float32)
 
 
 def from_right(value, right):
-    out = jnp.dot(two_terms(value, 1), right, preferred_element_type=jnp.float32)
+    out = jnp.dot(jnp.concatenate(two_terms(value), 1), right, preferred_element_type=jnp.float32)
     return out[:, :LANES] + out[:, LANES:]
 
 
 def pair_body(points, has, *refs):
     refs = list(refs)
-    a_ref, b_ref = refs.pop(0), refs.pop(0)
-    more_ref = refs.pop(0) if "more" in has else None
+    names = ["a", "b"] + [name for name in ("more", "sum_a", "sum_b") if name in has]
+    far = {name: refs.pop(0) for name in names}
     kernel_ref, left_ref, right_ref = refs.pop(0), refs.pop(0), refs.pop(0)
-    sum_a_ref = refs.pop(0) if "sum_a" in has else None
-    sum_b_ref = refs.pop(0) if "sum_b" in has else None
     for_a_ref = refs.pop(0)
     for_b_ref = refs.pop(0) if "for_b" in has else None
-    (held,) = refs
+    held, near, sems = refs
     step = pl.program_id(0)
-    ys = a_ref.shape[1] // points
+    columns = for_a_ref.shape[1]
+    ys = columns // points
     per_step = points // PLANE_STEPS
-
-    def visitor():
-        return b_ref[...] if more_ref is None else b_ref[...] + more_ref[...]
+    late = X_STEPS + PLANE_STEPS
+
+    def fetch(name, chunk):
+        place = names.index(name)
+        span = pl.ds(pl.multiple_of(chunk * columns, columns), columns)
+        return pltpu.make_async_copy(
+            far[name].at[:, span], near.at[place, :, span], sems.at[place, chunk]
+        )
+
+    def here(name, chunk):
+        span = pl.ds(pl.multiple_of(chunk * columns, columns), columns)
+        return near[names.index(name), :, span]
+
+    def visitor(chunk):
+        block = here("b", chunk)
+        return block + here("more", chunk) if "more" in has else block
+
+    ends = [name for name in names if not name.startswith("sum")]
+    sums = [name for name in names if name.startswith("sum")]
+
+    @pl.when(step == 0)
+    def start_ends():
+        for chunk in range(X_STEPS):
+            for name in ends:
+                fetch(name, chunk).start()
+
+    if sums:
+        @pl.when(step == X_STEPS)
+        def start_sums():
+            for chunk in range(X_STEPS):
+                for name in sums:
+                    fetch(name, chunk).start()
 
     def lanes_apart(block):
         gap = jnp.zeros((points, LANES - points), jnp.float32)
@@ -105,11 +130,13 @@
 
     @pl.when(step < X_STEPS)
     def forward_x():
-        spectrum = from_left(left_ref[...], a_ref[...] * visitor())
+        for name in ends:
+            fetch(name, step).wait()
+        spectrum = from_left(left_ref[...], here("a", step) * visitor(step))
         start = pl.multiple_of(step * ys, ys)
         held[:, pl.ds(start, ys), :] = lanes_apart(spectrum)
 
-    @pl.when((step >= X_STEPS) & (step < X_STEPS + PLANE_STEPS))
+    @pl.when((step >= X_STEPS) & (step < late))
     def planes():
         left = left_ref[...]
         right = right_ref[...]
@@ -124,16 +151,19 @@
         block = from_right(block, right)
         held[pl.ds(first, per_step)] = block.reshape(per_step, points, LANES)
 
-    @pl.when(step >= X_STEPS + PLANE_STEPS)
+    @pl.when(step >= late)
     def inverse_x():
-        start = pl.multiple_of((step - X_STEPS - PLANE_STEPS) * ys, ys)
+        chunk = step - late
+        start = pl.multiple_of(chunk * ys, ys)
+        for name in sums:
+            fetch(name, chunk).wait()
         block = lanes_together(held[:, pl.ds(start, ys), :])
         potential = from_left(left_ref[...], block)
-        for_a = visitor() * potential
-        for_a_ref[...] = -for_a if sum_a_ref is None else sum_a_ref[...] - for_a
+        for_a = visitor(chunk) * potential
+        for_a_ref[...] = here("sum_a", chunk) - for_a if "sum_a" in has else -for_a
         if for_b_ref is not None:
-            for_b = a_ref[...] * potential
-            for_b_ref[...] = -for_b if sum_b_ref is None else sum_b_ref[...] - for_b
+            for_b = here("a", chunk) * potential
+            for_b_ref[...] = here("sum_b", chunk) - for_b if "sum_b" in has else -for_b
 
 
 def pair_terms(a, b, constants, more=None, sum_a=None, sum_b=None, for_b=False):
@@ -142,9 +172,6 @@
     late = X_STEPS + PLANE_STEPS
     kernel, left, right = constants
 
-    def ends(i):
-        return (0, jnp.where(i < X_STEPS, i, jnp.where(i < late, X_STEPS - 1, i - late)))
-
     def tail(i):
         return (0, jnp.maximum(i - late, 0))
 
@@ -154,29 +181,34 @@
     def whole(i):
         return (0, 0)
 
-    at_ends = pl.BlockSpec((points, columns), ends)
     at_tail = pl.BlockSpec((points, columns), tail)
-    operands = [(None, a, at_ends), (None, b, at_ends), ("more", more, at_ends)]
-    operands.append((None, kernel, pl.BlockSpec((points // PLANE_STEPS, points, LANES), middle)))
-    operands.append((None, left, pl.BlockSpec(left.shape, whole)))
-    operands.append((None, right, pl.BlockSpec(right.shape, whole)))
-    operands += [("sum_a", sum_a, at_tail), ("sum_b", sum_b, at_tail)]
-    operands = [entry for entry in operands if entry[1] is not None]
-    has = [name for name, value, spec in operands if name] + ["for_b"] * for_b
+    optional = {"more": more, "sum_a": sum_a, "sum_b": sum_b}
+    optional = {name: value for name, value in optional.items() if value is not None}
+    blocks = [a, b, *optional.values()]
+    has = list(optional) + ["for_b"] * for_b
     n_out = 2 if for_b else 1
     out = pl.pallas_call(
         functools.partial(pair_body, points, has),
         grid=(2 * X_STEPS + PLANE_STEPS,),
-        in_specs=[spec for name, value, spec in operands],
+        in_specs=[pl.BlockSpec(memory_space=pl.ANY)] * len(blocks)
+        + [
+            pl.BlockSpec((points // PLANE_STEPS, points, LANES), middle),
+            pl.BlockSpec(left.shape, whole),
+            pl.BlockSpec(right.shape, whole),
+        ],
         out_specs=[at_tail] * n_out,
         out_shape=[jax.ShapeDtypeStruct((points, plane), jnp.float32)] * n_out,
-        scratch_shapes=[pltpu.VMEM((points, points, LANES), jnp.float32)],
+        scratch_shapes=[
+            pltpu.VMEM((points, points, LANES), jnp.float32),
+            pltpu.VMEM((len(blocks), points, plane), jnp.float32),
+            pltpu.SemaphoreType.DMA((len(blocks), X_STEPS)),
+        ],
         compiler_params=pltpu.CompilerParams(vmem_limit_bytes=60 * 2**20),
         cost_estimate=pl.CostEstimate(
             flops=16_000_000_000, bytes_accessed=20_000_000, transcendentals=0
         ),
         name="pair_terms",
-    )(*[value for name, value, spec in operands])
+    )(*blocks, kernel, left, right)
     return out if for_b else out[0]
 
 
@@ -199,25 +231,24 @@
     )(block, kernel)
 
 
-def after_body(token_ref, left_ref, block_ref, new_left_ref, new_block_ref, sem):
-    copy = pltpu.make_async_copy(block_ref, new_block_ref, sem)
-    copy.start()
+def after_body(token_ref, left_ref, block_ref, new_left_ref, new_block_ref):
+    new_block_ref[...] = block_ref[...]
     new_left_ref[...] = left_ref[...]
-    copy.wait()
 
 
 def after(token, left, block):
-    in_vmem = pl.BlockSpec(memory_space=pltpu.VMEM)
-    anywhere = pl.BlockSpec(memory_space=pl.ANY)
+    points, plane = block.shape
+    part = pl.BlockSpec((points, plane // X_STEPS), lambda i: (0, i))
+    table = pl.BlockSpec(left.shape, lambda i: (0, 0))
     return pl.pallas_call(
         after_body,
-        in_specs=[in_vmem, in_vmem, anywhere],
-        out_specs=[in_vmem, anywhere],
+        grid=(X_STEPS,),
+        in_specs=[pl.BlockSpec(token.shape, lambda i: (0, 0)), table, part],
+        out_specs=[table, part],
         out_shape=[
             jax.ShapeDtypeStruct(left.shape, left.dtype),
             jax.ShapeDtypeStruct(block.shape, block.dtype),
         ],
-        scratch_shapes=[pltpu.SemaphoreType.DMA],
         compiler_params=pltpu.CompilerParams(vmem_limit_bytes=60 * 2**20),
         name="after",
     )(token, left, block)
@@ -249,7 +280,8 @@
     turned = send(orbitals, TURN_FIRST)
     kernel, left, right = constants
     token = send(corner(crossed, kernel)[None], ARRIVED)
-    left, held_back = after(token[0], left, orbitals)
+    left, held_back = after(token[0], left, own)
+    held_back = held_back[None]
     constants = (kernel, left, right)
     single = send(held_back, SINGLES)[0]
     beside = send(held_back, BESIDE)[0]
@@ -262,7 +294,8 @@
     home_far = send(partner_sum[None], HOME_FAR)[0]
     home_beside = send(beside_sum[None], HOME_BESIDE)[0]
     own_sum = pair_terms(own, single, constants, more=turned, sum_a=own_sum)
-    return (own_sum + home + home_beside + home_far)[None]
+    own_sum = own_sum + home + home_beside
+    return (own_sum + home_far)[None]
 
 
 def any_bands(orbitals, constants):

time: 306 us -> 197 us (0.64)
  Pallas kernels: 201 us -> 86.8 us
  waiting for transfers between devices: 61 us -> 67.2 us
    pallas_call x1, Pallas kernels: 110 us -> 5.54 us  [after(): pl.pallas_call(after_body, grid=(X_STEPS,), in_specs=[pl.BlockSpec(token....]
    pallas_call x4, Pallas kernels: 90.3 us -> 79.9 us  [pair_terms(): pl.pallas_call(functools.partial(pair_body, points, has), grid=(2 * X_STE...]
    ppermute x10, waiting for transfers between devices: 61 us -> 67.2 us  [send(): return lax.ppermute(value, 'band', pairs)]
  transfers between devices with their start and end apart: 10 -> 10, of which waited for: 1 -> 2; matrix products, arithmetic and copies ran while one was open for 2% -> 3% of each run, Pallas kernels for 66% -> 44%
where the time goes in v4:
time: 197 us; the launch traced here: 196 us
  Pallas kernels  86.8 us (44%)
  waiting for transfers between devices  67.2 us (34%)
  starting transfers between devices  27.6 us (14%)
  other arithmetic  9.57 us (5%)
  local copies, waits for them, and re-layouts  4.94 us (3%)
    pallas_call x4, Pallas kernels, pair_terms(): pl.pallas_call(functools.partial(pair_body, points, has), grid=(2 * X_STE...  79.9 us
    ppermute x10, waiting for transfers between devices, send(): return lax.ppermute(value, 'band', pairs)  67.2 us
    ppermute x10, starting transfers between devices, send(): return lax.ppermute(value, 'band', pairs)  27.6 us
    broadcast_in_dim x1, other arithmetic, sixteen_bands(): return (own_sum + home_far)[None]  6.57 us
    pallas_call x1, Pallas kernels, after(): pl.pallas_call(after_body, grid=(X_STEPS,), in_specs=[pl.BlockSpec(token....  5.54 us
  transfers between devices with their start and end apart: 10, of which 2 were waited for; matrix products, arithmetic and copies ran while one was open for 3% of the time, Pallas kernels for 44%

profile of v4, /device:TPU:0, one launch (start us, length us, event | category | flops | bytes accessed | tf_op | source)
XLA Modules:
  0.0 196.2 jit_solution(12789752929665135712)
XLA Ops:
  0.0 0.9 collective-permute-start
  0.9 2.5 %collective-permute-start.3 = (f32[1,96,9216]{2,1,0:T(8,128)}, f32[1,96,9216]{2,1,0:T(8,128)}, u32[]{:S(2)}, u32[]{:S(2)}) collective-permute-start(f32[1,96,9216]{2,1,0:T(8,128)} %param.3), channel_id=1, source_target_pairs={{9,11},{14,12},{6,4},{1,3},{25,27},{30,28},{22,20},{17,19}} | collective-permute-start | bytes 10616840 | tf_op jit(solution)/shard_map/ppermute | solution.py:275
  3.3 11.7 %collective-permute-start.5 = (f32[1,96,9216]{2,1,0:T(8,128)}, f32[1,96,9216]{2,1,0:T(8,128)}, u32[]{:S(2)}, u32[]{:S(2)}) collective-permute-start(f32[1,96,9216]{2,1,0:T(8,128)} %param.3), channel_id=1, source_target_pairs={{8,14},{15,9},{7,1},{0,6},{24,30},{31,25},{23,17},{16,22}} | collective-permute-start | bytes 10616840 | tf_op jit(solution)/shard_map/ppermute | solution.py:275
  15.1 0.1 broadcast_add_fusion
  15.1 2.9 %fusion.4 = f32[96,96,96]{2,1,0:T(8,128)S(1)} fusion(f32[96]{0:T(128)S(1)} %fusion.11, f32[96,96]{1,0:T(8,128)S(1)} %broadcast_add_fusion), kind=kLoop, calls=%fused_computation.6 | loop fusion | flops 8847360 | bytes 3576192 | tf_op jit(solution)/shard_map/div | solution.py:37
  18.1 2.6 %pad.4.kernel_ref.refs_2_.refs_3_.refs_4_ = f32[96,96,128]{2,1,0:T(8,128)} pad(f32[96,96,96]{2,1,0:T(8,128)S(1)} %fusion.4, f32[]{:T(128)} %constant.8.clone.1), padding=0_0x0_0x0_32 | pad | bytes 8257540 | tf_op jit(solution)/shard_map/jit(_pad)/pad | solution.py:38
  20.6 0.0 collective-permute-done
  20.6 0.0 copy-start
  20.6 1.8 copy-done
  22.4 1.3 corner.1
  23.7 0.7 collective-permute-start.1
  24.4 0.0 collective-permute-done.1
  24.4 0.0 copy-start.1
  24.4 0.6 copy-done.1
  25.0 5.5 %after.1 = (bf16[96,288]{1,0:T(8,128)(2,1)}, f32[96,9216]{1,0:T(8,128)}) custom-call(f32[8,128]{1,0:T(8,128)} %bitcast.33, bf16[96,288]{1,0:T(8,128)(2,1)} %constant.27.clone.left_ref, f32[96,9216]{1,0:T(8,128)} %bitcast.29), custom_call_target="tpu_custom_call" | custom-call | tf_op jit(solution)/shard_map/after/pallas_call | solution.py:243
  30.5 2.4 %collective-permute-start.7 = (f32[1,96,9216]{2,1,0:T(8,128)}, f32[1,96,9216]{2,1,0:T(8,128)}, u32[]{:S(2)}, u32[]{:S(2)}) collective-permute-start(f32[1,96,9216]{2,1,0:T(8,128)} %bitcast.34), channel_id=1, source_target_pairs={{13,14},{10,9},{2,1},{5,6},{29,30},{26,25},{18,17},{21,22}} | collective-permute-start | bytes 10616840 | tf_op jit(solution)/shard_map/ppermute | solution.py:275
  32.9 0.0 collective-permute-done.3
  32.9 2.4 %collective-permute-start.4 = (f32[1,96,9216]{2,1,0:T(8,128)}, f32[1,96,9216]{2,1,0:T(8,128)}, u32[]{:S(2)}, u32[]{:S(2)}) collective-permute-start(f32[1,96,9216]{2,1,0:T(8,128)} %collective-permute-done.3), channel_id=1, source_target_pairs={{11,14},{12,9},{4,1},{3,6},{27,30},{28,25},{20,17},{19,22}} | collective-permute-start | bytes 10616840 | tf_op jit(solution)/shard_map/ppermute | solution.py:275
  35.4 2.5 %collective-permute-start.2 = (f32[1,96,9216]{2,1,0:T(8,128)}, f32[1,96,9216]{2,1,0:T(8,128)}, u32[]{:S(2)}, u32[]{:S(2)}) collective-permute-start(f32[1,96,9216]{2,1,0:T(8,128)} %bitcast.35), channel_id=1, source_target_pairs={{5,10},{2,13},{10,5},{13,2},{21,26},{18,29},{26,21},{29,18}} | collective-permute-start | bytes 10616840 | tf_op jit(solution)/shard_map/ppermute | solution.py:275
  37.8 14.8 %collective-permute-done.5 = f32[1,96,9216]{2,1,0:T(8,128)} collective-permute-done((f32[1,96,9216]{2,1,0:T(8,128)}, f32[1,96,9216]{2,1,0:T(8,128)}, u32[]{:S(2)}, u32[]{:S(2)}) %collective-permute-start.5) | collective-permute-done | bytes 3538976 | tf_op jit(solution)/shard_map/ppermute | solution.py:275
  52.6 19.9 %pair_terms.4 = (f32[96,9216]{1,0:T(8,128)}, f32[96,9216]{1,0:T(8,128)}) custom-call(f32[96,9216]{1,0:T(8,128)} %bitcast.7.refs_0_, f32[96,9216]{1,0:T(8,128)} %bitcast.27, f32[96,96,128]{2,1,0:T(8,128)} %pad.4.kernel_ref.refs_2_.refs_3_.refs_4_, bf16[96,288]{1,0:T(8,128)(2,1)} %get-tuple-element.14.refs_3_.refs_4_.refs_5_, ...), custom_call_target="tpu_custom_call" | custom-call | flops 16000000000 | bytes 20000000 | tf_op jit(solution)/shard_map/pair_terms/pallas_call | solution.py:190
  72.5 20.1 %pair_terms.5 = (f32[96,9216]{1,0:T(8,128)}, f32[96,9216]{1,0:T(8,128)}) custom-call(f32[96,9216]{1,0:T(8,128)} %bitcast.30, f32[96,9216]{1,0:T(8,128)} %bitcast.28, f32[96,9216]{1,0:T(8,128)} %get-tuple-element.15.refs_2_, f32[96,96,128]{2,1,0:T(8,128)} %pad.4.kernel_ref.refs_2_.refs_3_.refs_4_, bf16[96,288]{1,0:T(8,128)(2,1)} %get-tuple-element.14.refs_3_.refs_4_.refs_5_, ...), custom_call_target="tpu_custom_call" | custom-call | flops 16000000000 | bytes 20000000 | tf_op jit(solution)/shard_map/pair_terms/pallas_call | solution.py:190
  92.6 0.9 collective-permute-start.6
  93.5 0.0 collective-permute-done.7
  93.5 20.0 %pair_terms.7 = (f32[96,9216]{1,0:T(8,128)}, f32[96,9216]{1,0:T(8,128)}) custom-call(f32[96,9216]{1,0:T(8,128)} %bitcast.7.refs_0_, f32[96,9216]{1,0:T(8,128)} %bitcast.10.refs_1_, f32[96,9216]{1,0:T(8,128)} %get-tuple-element.18.refs_2_, f32[96,96,128]{2,1,0:T(8,128)} %pad.4.kernel_ref.refs_2_.refs_3_.refs_4_, ...), custom_call_target="tpu_custom_call" | custom-call | flops 16000000000 | bytes 20000000 | tf_op jit(solution)/shard_map/pair_terms/pallas_call | solution.py:190
  113.6 1.3 collective-permute-start.9
  114.9 2.4 %collective-permute-start.8 = (f32[1,96,9216]{2,1,0:T(8,128)}, f32[1,96,9216]{2,1,0:T(8,128)}, u32[]{:S(2)}, u32[]{:S(2)}) collective-permute-start(f32[1,96,9216]{2,1,0:T(8,128)} %bitcast.37), channel_id=1, source_target_pairs={{9,10},{14,13},{6,5},{1,2},{25,26},{30,29},{22,21},{17,18}} | collective-permute-start | bytes 10616840 | tf_op jit(solution)/shard_map/ppermute | solution.py:275
  117.3 0.0 collective-permute-done.4
  117.3 0.0 collective-permute-done.2
  117.3 19.9 %pair_terms.6 = f32[96,9216]{1,0:T(8,128)} custom-call(f32[96,9216]{1,0:T(8,128)} %bitcast.31, f32[96,9216]{1,0:T(8,128)} %bitcast.5.refs_1_, f32[96,9216]{1,0:T(8,128)} %bitcast.6.refs_2_, f32[96,9216]{1,0:T(8,128)} %get-tuple-element.16.refs_3_, f32[96,96,128]{2,1,0:T(8,128)} %pad.4.kernel_ref.refs_2_.refs_3_.refs_4_, ...), custom_call_target="tpu_custom_call" | custom-call | flops 16000000000 | bytes 20000000 | tf_op jit(solution)/shard_map/pair_terms/pallas_call | solution.py:190
  137.2 0.0 collective-permute-done.6
  137.2 52.5 %collective-permute-done.9 = f32[1,96,9216]{2,1,0:T(8,128)} collective-permute-done((f32[1,96,9216]{2,1,0:T(8,128)}, f32[1,96,9216]{2,1,0:T(8,128)}, u32[]{:S(2)}, u32[]{:S(2)}) %collective-permute-start.9) | collective-permute-done | bytes 3538976 | tf_op jit(solution)/shard_map/ppermute | solution.py:275
  189.6 0.0 collective-permute-done.8
  189.6 6.6 %fusion.8 = f32[1,96,9216]{2,1,0:T(8,128)} fusion(f32[1,96,9216]{2,1,0:T(8,128)} %collective-permute-done.9, f32[1,96,9216]{2,1,0:T(8,128)} %collective-permute-done.8, f32[96,9216]{1,0:T(8,128)} %pair_terms.6, f32[1,96,9216]{2,1,0:T(8,128)S(1)} %collective-permute-done.6), kind=kLoop, calls=%fused_computation.11 | loop fusion | flops 2654208 | bytes 17694720 | tf_op jit(solution)/shard_map/broadcast_in_dim | solution.py:298
  (1 shorter events, 0.0 us)
Async XLA Ops:
  0.0 20.6 %collective-permute-start = (f32[1,96,9216]{2,1,0:T(8,128)}, f32[1,96,9216]{2,1,0:T(8,128)S(1)}, u32[]{:S(2)}, u32[]{:S(2)}) collective-permute-start(f32[1,96,9216]{2,1,0:T(8,128)} %param.3), channel_id=1, source_target_pairs={{3,14},{4,9},{12,1},{11,6},{19,30},{20,25},{28,17},{27,22}} | collective-permute-start | bytes 10616840 | tf_op jit(solution)/shard_map/ppermute | solution.py:275
  0.9 32.0 %collective-permute-start.3 = (f32[1,96,9216]{2,1,0:T(8,128)}, f32[1,96,9216]{2,1,0:T(8,128)}, u32[]{:S(2)}, u32[]{:S(2)}) collective-permute-start(f32[1,96,9216]{2,1,0:T(8,128)} %param.3), channel_id=1, source_target_pairs={{9,11},{14,12},{6,4},{1,3},{25,27},{30,28},{22,20},{17,19}} | collective-permute-start | bytes 10616840 | tf_op jit(solution)/shard_map/ppermute | solution.py:275
  3.3 49.2 %collective-permute-start.5 = (f32[1,96,9216]{2,1,0:T(8,128)}, f32[1,96,9216]{2,1,0:T(8,128)}, u32[]{:S(2)}, u32[]{:S(2)}) collective-permute-start(f32[1,96,9216]{2,1,0:T(8,128)} %param.3), channel_id=1, source_target_pairs={{8,14},{15,9},{7,1},{0,6},{24,30},{31,25},{23,17},{16,22}} | collective-permute-start | bytes 10616840 | tf_op jit(solution)/shard_map/ppermute | solution.py:275
  20.6 1.8 copy-start
  23.7 0.7 collective-permute-start.1
  24.4 0.6 copy-start.1
  30.5 63.0 %collective-permute-start.7 = (f32[1,96,9216]{2,1,0:T(8,128)}, f32[1,96,9216]{2,1,0:T(8,128)}, u32[]{:S(2)}, u32[]{:S(2)}) collective-permute-start(f32[1,96,9216]{2,1,0:T(8,128)} %bitcast.34), channel_id=1, source_target_pairs={{13,14},{10,9},{2,1},{5,6},{29,30},{26,25},{18,17},{21,22}} | collective-permute-start | bytes 10616840 | tf_op jit(solution)/shard_map/ppermute | solution.py:275
  32.9 84.4 %collective-permute-start.4 = (f32[1,96,9216]{2,1,0:T(8,128)}, f32[1,96,9216]{2,1,0:T(8,128)}, u32[]{:S(2)}, u32[]{:S(2)}) collective-permute-start(f32[1,96,9216]{2,1,0:T(8,128)} %collective-permute-done.3), channel_id=1, source_target_pairs={{11,14},{12,9},{4,1},{3,6},{27,30},{28,25},{20,17},{19,22}} | collective-permute-start | bytes 10616840 | tf_op jit(solution)/shard_map/ppermute | solution.py:275
  35.4 82.0 %collective-permute-start.2 = (f32[1,96,9216]{2,1,0:T(8,128)}, f32[1,96,9216]{2,1,0:T(8,128)}, u32[]{:S(2)}, u32[]{:S(2)}) collective-permute-start(f32[1,96,9216]{2,1,0:T(8,128)} %bitcast.35), channel_id=1, source_target_pairs={{5,10},{2,13},{10,5},{13,2},{21,26},{18,29},{26,21},{29,18}} | collective-permute-start | bytes 10616840 | tf_op jit(solution)/shard_map/ppermute | solution.py:275
  92.6 44.5 %collective-permute-start.6 = (f32[1,96,9216]{2,1,0:T(8,128)}, f32[1,96,9216]{2,1,0:T(8,128)S(1)}, u32[]{:S(2)}, u32[]{:S(2)}) collective-permute-start(f32[1,96,9216]{2,1,0:T(8,128)} %bitcast.36), channel_id=1, source_target_pairs={{9,4},{14,3},{6,11},{1,12},{25,20},{30,19},{22,27},{17,28}} | collective-permute-start | bytes 10616840 | tf_op jit(solution)/shard_map/ppermute | solution.py:275
  113.6 76.0 %collective-permute-start.9 = (f32[1,96,9216]{2,1,0:T(8,128)}, f32[1,96,9216]{2,1,0:T(8,128)}, u32[]{:S(2)}, u32[]{:S(2)}) collective-permute-start(f32[1,96,9216]{2,1,0:T(8,128)} %bitcast.38), channel_id=1, source_target_pairs={{9,15},{14,8},{6,0},{1,7},{25,31},{30,24},{22,16},{17,23}} | collective-permute-start | bytes 10616840 | tf_op jit(solution)/shard_map/ppermute | solution.py:275
  114.9 74.7 %collective-permute-start.8 = (f32[1,96,9216]{2,1,0:T(8,128)}, f32[1,96,9216]{2,1,0:T(8,128)}, u32[]{:S(2)}, u32[]{:S(2)}) collective-permute-start(f32[1,96,9216]{2,1,0:T(8,128)} %bitcast.37), channel_id=1, source_target_pairs={{9,10},{14,13},{6,5},{1,2},{25,26},{30,29},{22,21},{17,18}} | collective-permute-start | bytes 10616840 | tf_op jit(solution)/shard_map/ppermute | solution.py:275

commit v5 on v4

--- a/solution.py
+++ b/solution.py
@@ -22,20 +22,20 @@
 
 
 def screened_kernel(points):
-    signed = jnp.arange(points, dtype=jnp.int32)
+    signed = jnp.arange(LANES, dtype=jnp.int32)
+    inside = signed < points
     signed = jnp.where(signed >= points // 2, signed - points, signed)
     wavenumber = signed.astype(jnp.float32) * (2.0 * math.pi / points)
     squared = (
-        wavenumber[:, None, None] ** 2
-        + wavenumber[None, :, None] ** 2
+        wavenumber[:points, None, None] ** 2
+        + wavenumber[None, :points, None] ** 2
         + wavenumber[None, None, :] ** 2
     )
     screen_rate = screening / points
     finite = jnp.where(squared > 0.0, squared, 1.0)
     screened = 4.0 * math.pi / finite * -jnp.expm1(-finite / (4.0 * screen_rate * screen_rate))
     kernel = jnp.where(squared > 0.0, screened, math.pi / (screen_rate * screen_rate))
-    kernel = kernel / float(points * points * points)
-    return jnp.pad(kernel, ((0, 0), (0, 0), (0, LANES - points)))
+    return jnp.where(inside, kernel / float(points * points * points), 0.0)
 
 
 def hartley_tables(points):
@@ -44,7 +44,10 @@
     table = np.cos(angles) + np.sin(angles)
     high = table.astype(jnp.bfloat16)
     low = (table - high.astype(np.float64)).astype(jnp.bfloat16)
-    left = np.concatenate([high, high, low], 1)
+    left = np.zeros((2 * points, 2 * points), jnp.bfloat16)
+    left[:points, :points] = high
+    left[:points, points:] = high
+    left[points:, :points] = low
     right = np.zeros((2 * LANES, 2 * LANES), jnp.bfloat16)
     right[:points, :points] = high
     right[:points, LANES:LANES + points] = low
@@ -59,9 +62,10 @@
 
 
 def from_left(left, value):
-    high, low = two_terms(value)
-    terms = jnp.concatenate([high, low, high], 0)
-    return jnp.dot(left, terms, preferred_element_type=jnp.float32)
+    half = value.shape[0]
+    terms = jnp.concatenate(two_terms(value), 0)
+    out = jnp.dot(left, terms, preferred_element_type=jnp.float32)
+    return out[:half] + out[half:]
 
 
 def from_right(value, right):
@@ -71,10 +75,11 @@
 
 def pair_body(points, has, *refs):
     refs = list(refs)
-    names = ["a", "b"] + [name for name in ("more", "sum_a", "sum_b") if name in has]
+    names = ["a", "b"] + [name for name in ("sum_a", "sum_b") if name in has]
     far = {name: refs.pop(0) for name in names}
     kernel_ref, left_ref, right_ref = refs.pop(0), refs.pop(0), refs.pop(0)
     for_a_ref = refs.pop(0)
+    low_a_ref = refs.pop(0) if "halves" in has else None
     for_b_ref = refs.pop(0) if "for_b" in has else None
     held, near, sems = refs
     step = pl.program_id(0)
@@ -94,10 +99,6 @@
         span = pl.ds(pl.multiple_of(chunk * columns, columns), columns)
         return near[names.index(name), :, span]
 
-    def visitor(chunk):
-        block = here("b", chunk)
-        return block + here("more", chunk) if "more" in has else block
-
     ends = [name for name in names if not name.startswith("sum")]
     sums = [name for name in names if name.startswith("sum")]
 
@@ -132,7 +133,7 @@
     def forward_x():
         for name in ends:
             fetch(name, step).wait()
-        spectrum = from_left(left_ref[...], here("a", step) * visitor(step))
+        spectrum = from_left(left_ref[...], here("a", step) * here("b", step))
         start = pl.multiple_of(step * ys, ys)
         held[:, pl.ds(start, ys), :] = lanes_apart(spectrum)
 
@@ -159,14 +160,19 @@
             fetch(name, chunk).wait()
         block = lanes_together(held[:, pl.ds(start, ys), :])
         potential = from_left(left_ref[...], block)
-        for_a = visitor(chunk) * potential
-        for_a_ref[...] = here("sum_a", chunk) - for_a if "sum_a" in has else -for_a
+        for_a = here("b", chunk) * potential
+        for_a = here("sum_a", chunk) - for_a if "sum_a" in has else -for_a
+        if low_a_ref is None:
+            for_a_ref[...] = for_a
+        else:
+            for_a_ref[...] = for_a[:points // 2]
+            low_a_ref[...] = for_a[points // 2:]
         if for_b_ref is not None:
             for_b = here("a", chunk) * potential
             for_b_ref[...] = here("sum_b", chunk) - for_b if "sum_b" in has else -for_b
 
 
-def pair_terms(a, b, constants, more=None, sum_a=None, sum_b=None, for_b=False):
+def pair_terms(a, b, constants, sum_a=None, sum_b=None, for_b=False, halves=False):
     points, plane = a.shape
     columns = plane // X_STEPS
     late = X_STEPS + PLANE_STEPS
@@ -181,12 +187,11 @@
     def whole(i):
         return (0, 0)
 
-    at_tail = pl.BlockSpec((points, columns), tail)
-    optional = {"more": more, "sum_a": sum_a, "sum_b": sum_b}
+    optional = {"sum_a": sum_a, "sum_b": sum_b}
     optional = {name: value for name, value in optional.items() if value is not None}
     blocks = [a, b, *optional.values()]
-    has = list(optional) + ["for_b"] * for_b
-    n_out = 2 if for_b else 1
+    has = list(optional) + ["for_b"] * for_b + ["halves"] * halves
+    rows = ([points // 2] * 2 if halves else [points]) + [points] * for_b
     out = pl.pallas_call(
         functools.partial(pair_body, points, has),
         grid=(2 * X_STEPS + PLANE_STEPS,),
@@ -196,8 +201,8 @@
             pl.BlockSpec(left.shape, whole),
             pl.BlockSpec(right.shape, whole),
         ],
-        out_specs=[at_tail] * n_out,
-        out_shape=[jax.ShapeDtypeStruct((points, plane), jnp.float32)] * n_out,
+        out_specs=[pl.BlockSpec((n, columns), tail) for n in rows],
+        out_shape=[jax.ShapeDtypeStruct((n, plane), jnp.float32) for n in rows],
         scratch_shapes=[
             pltpu.VMEM((points, points, LANES), jnp.float32),
             pltpu.VMEM((len(blocks), points, plane), jnp.float32),
@@ -209,93 +214,105 @@
         ),
         name="pair_terms",
     )(*blocks, kernel, left, right)
-    return out if for_b else out[0]
-
-
-def corner_body(block_ref, kernel_ref, corner_ref, sem):
-    copy = pltpu.make_async_copy(block_ref.at[pl.ds(0, 8), pl.ds(0, LANES)], corner_ref, sem)
-    copy.start()
-    copy.wait()
-
-
-def corner(block, kernel):
+    return out if len(rows) > 1 else out[0]
+
+
+def gate_body(token_ref, left_ref, role_ref, own_ref, turned_ref, new_left_ref, block_ref, near, sems):
+    new_left_ref[...] = left_ref[...]
+    role = role_ref[0]
+    columns = own_ref.shape[1] // X_STEPS
+
+    def copies(source_ref):
+        spans = [pl.ds(i * columns, columns) for i in range(X_STEPS)]
+        inward = [
+            pltpu.make_async_copy(source_ref.at[:, span], near.at[:, span], sems.at[0, i])
+            for i, span in enumerate(spans)
+        ]
+        outward = [
+            pltpu.make_async_copy(near.at[:, span], block_ref.at[:, span], sems.at[1, i])
+            for i, span in enumerate(spans)
+        ]
+        for copy in inward:
+            copy.start()
+        for first, second in zip(inward, outward):
+            first.wait()
+            second.start()
+        for copy in outward:
+            copy.wait()
+
+    @pl.when(role == 1)
+    def from_own():
+        copies(own_ref)
+
+    @pl.when(role == 2)
+    def from_turned():
+        copies(turned_ref)
+
+
+def gate(token, left, role, own, turned):
+    in_vmem = pl.BlockSpec(memory_space=pltpu.VMEM)
+    in_smem = pl.BlockSpec(memory_space=pltpu.SMEM)
     anywhere = pl.BlockSpec(memory_space=pl.ANY)
     return pl.pallas_call(
-        corner_body,
-        in_specs=[anywhere, anywhere],
-        out_specs=pl.BlockSpec(memory_space=pltpu.VMEM),
-        out_shape=jax.ShapeDtypeStruct((8, LANES), block.dtype),
-        scratch_shapes=[pltpu.SemaphoreType.DMA],
-        compiler_params=pltpu.CompilerParams(vmem_limit_bytes=60 * 2**20),
-        name="corner",
-    )(block, kernel)
-
-
-def after_body(token_ref, left_ref, block_ref, new_left_ref, new_block_ref):
-    new_block_ref[...] = block_ref[...]
-    new_left_ref[...] = left_ref[...]
-
-
-def after(token, left, block):
-    points, plane = block.shape
-    part = pl.BlockSpec((points, plane // X_STEPS), lambda i: (0, i))
-    table = pl.BlockSpec(left.shape, lambda i: (0, 0))
-    return pl.pallas_call(
-        after_body,
-        grid=(X_STEPS,),
-        in_specs=[pl.BlockSpec(token.shape, lambda i: (0, 0)), table, part],
-        out_specs=[table, part],
+        gate_body,
+        in_specs=[in_vmem, in_vmem, in_smem, anywhere, anywhere],
+        out_specs=[in_vmem, anywhere],
         out_shape=[
             jax.ShapeDtypeStruct(left.shape, left.dtype),
-            jax.ShapeDtypeStruct(block.shape, block.dtype),
+            jax.ShapeDtypeStruct(own.shape, own.dtype),
         ],
+        scratch_shapes=[pltpu.VMEM(own.shape, own.dtype), pltpu.SemaphoreType.DMA((2, X_STEPS))],
         compiler_params=pltpu.CompilerParams(vmem_limit_bytes=60 * 2**20),
-        name="after",
-    )(token, left, block)
+        name="gate",
+    )(token, left, role, own, turned)
 
 
 def both_halves(*pairs):
     return list(pairs) + [(15 - source, 15 - target) for source, target in pairs]
 
 
-CROSSING = both_halves((3, 14), (4, 9))
+CROSSING = both_halves((3, 14), (4, 9), (9, 11), (14, 12))
 PARTNERS = both_halves((8, 14), (15, 9))
-TURN_FIRST = both_halves((9, 11), (14, 12))
-TURN_SECOND = both_halves((11, 14), (12, 9))
 ARRIVED = both_halves((14, 2), (9, 5))
-SINGLES = both_halves((5, 10), (2, 13))
+SECOND = both_halves((5, 10), (2, 13), (11, 14), (12, 9))
 BESIDE = both_halves((13, 14), (10, 9))
 HOME_ACROSS = both_halves((9, 4), (14, 3))
 HOME_FAR = both_halves((9, 15), (14, 8))
+HOME_TURN = both_halves((9, 11), (14, 12))
+HOME_TURNED = both_halves((11, 15), (12, 8))
 HOME_BESIDE = both_halves((9, 10), (14, 13))
+SECOND_ROLES = {5: 1, 10: 1, 2: 1, 13: 1, 11: 2, 4: 2, 12: 2, 3: 2}
 
 
 def sixteen_bands(orbitals, constants):
     def send(value, pairs):
-        return lax.ppermute(value, "band", pairs)
-
+        return lax.ppermute(value[None], "band", pairs)[0]
+
+    kernel, left, right = constants
     own = orbitals[0]
-    crossed = send(orbitals, CROSSING)[0]
-    partner = send(orbitals, PARTNERS)[0]
-    turned = send(orbitals, TURN_FIRST)
-    kernel, left, right = constants
-    token = send(corner(crossed, kernel)[None], ARRIVED)
-    left, held_back = after(token[0], left, own)
-    held_back = held_back[None]
+    roles = jnp.asarray([SECOND_ROLES.get(i, 0) for i in range(16)], jnp.int32)
+    role = roles[lax.axis_index("band")][None]
+    crossed = send(own, CROSSING)
+    partner = send(own, PARTNERS)
+    token = send(crossed[:8, :LANES] + kernel[0, :8], ARRIVED)
+    left, held_back = gate(token, left, role, own, crossed)
     constants = (kernel, left, right)
-    single = send(held_back, SINGLES)[0]
-    beside = send(held_back, BESIDE)[0]
-    turned = send(turned, TURN_SECOND)[0]
+    beside = send(held_back, BESIDE)
+    second = send(held_back, SECOND)
 
     partner_sum, crossed_sum = pair_terms(partner, crossed, constants, for_b=True)
     own_sum, crossed_sum = pair_terms(own, crossed, constants, sum_b=crossed_sum, for_b=True)
-    home = send(crossed_sum[None], HOME_ACROSS)[0]
-    partner_sum, beside_sum = pair_terms(partner, beside, constants, sum_a=partner_sum, for_b=True)
-    home_far = send(partner_sum[None], HOME_FAR)[0]
-    home_beside = send(beside_sum[None], HOME_BESIDE)[0]
-    own_sum = pair_terms(own, single, constants, more=turned, sum_a=own_sum)
-    own_sum = own_sum + home + home_beside
-    return (own_sum + home_far)[None]
+    home = send(crossed_sum, HOME_ACROSS)
+    top, bottom, beside_sum = pair_terms(
+        partner, beside, constants, sum_a=partner_sum, for_b=True, halves=True
+    )
+    bottom = send(bottom, HOME_TURN)
+    top = send(top, HOME_FAR)
+    home_beside = send(beside_sum, HOME_BESIDE)
+    bottom = send(bottom, HOME_TURNED)
+    own_sum = pair_terms(own, second, constants, sum_a=own_sum)
+    own_sum = jnp.where(role == 2, 0.0, own_sum)
+    return (own_sum + home + home_beside + jnp.concatenate([top, bottom], 0))[None]
 
 
 def any_bands(orbitals, constants):

time: 197 us -> 198 us (level)
  the two profiles are of different devices: /device:TPU:0 before, /device:TPU:1 now
where the time goes in v5:
time: 198 us; the launch traced here: 197 us
  Pallas kernels  78 us (39%)
  waiting for transfers between devices  75.8 us (38%)
  starting transfers between devices  31.3 us (16%)
  other arithmetic  9.87 us (5%)
    ppermute x10, waiting for transfers between devices, send(): return lax.ppermute(value[None], 'band', pairs)[0]  75.8 us
    pallas_call x4, Pallas kernels, pair_terms(): pl.pallas_call(functools.partial(pair_body, points, has), grid=(2 * X_STE...  75.8 us
    ppermute x10, starting transfers between devices, send(): return lax.ppermute(value[None], 'band', pairs)[0]  31.3 us
    broadcast_in_dim x1, other arithmetic, sixteen_bands(): (own_sum + home + home_beside + jnp.concatenate([top, bottom], 0))[None]  6.7 us
  transfers between devices with their start and end apart: 10, of which 4 were waited for; matrix products, arithmetic and copies ran while one was open for 2% of the time, Pallas kernels for 40%

profile of v5, /device:TPU:1, one launch (start us, length us, event | category | flops | bytes accessed | tf_op | source)
XLA Modules:
  0.0 197.1 jit_solution(1763670565124968656)
XLA Ops:
  0.0 0.0 copy-start.3
  0.0 4.1 %collective-permute-start = (f32[1,96,9216]{2,1,0:T(8,128)}, f32[1,96,9216]{2,1,0:T(8,128)S(1)}, u32[]{:S(2)}, u32[]{:S(2)}) collective-permute-start(f32[1,96,9216]{2,1,0:T(8,128)} %param.4), channel_id=1, source_target_pairs={{3,14},{4,9},{9,11},{14,12},{12,1},{11,6},{6,4},{1,3},{19,30},{20,... | collective-permute-start | bytes 10616840 | tf_op jit(solution)/shard_map/ppermute | solution.py:289
  4.1 1.3 collective-permute-start.3
  5.5 0.1 broadcast_add_fusion
  5.5 3.1 %fusion.5.refs_2_.refs_3_ = f32[96,96,128]{2,1,0:T(8,128)S(1)} fusion(f32[128]{0:T(128)S(1)} %fusion.14, f32[96,96]{1,0:T(8,128)S(1)} %broadcast_add_fusion, pred[128]{0:T(512)(128)(4,1)S(1)} %iota_compare_fusion), kind=kLoop, calls=%fused_computation.7 | loop fusion | flops 12976128 | bytes 4756096 | tf_op jit(solution)/shard_map/jit(_where)/select_n | solution.py:38
  8.6 0.0 copy-start
  8.6 37.5 %collective-permute-done = f32[1,96,9216]{2,1,0:T(8,128)S(1)} collective-permute-done((f32[1,96,9216]{2,1,0:T(8,128)}, f32[1,96,9216]{2,1,0:T(8,128)S(1)}, u32[]{:S(2)}, u32[]{:S(2)}) %collective-permute-start) | collective-permute-done | bytes 3538976 | tf_op jit(solution)/shard_map/ppermute | solution.py:289
  46.1 0.0 copy-start.1
  46.1 0.0 copy-done
  46.1 1.3 collective-permute-start.1
  47.4 0.0 copy-done.3
  47.4 0.6 dynamic_slice.3.role_ref
  48.1 0.1 collective-permute-done.1
  48.2 0.0 copy-start.2
  48.2 0.0 copy-done.1
  48.2 0.6 copy-done.2
  48.8 2.3 %gate.1 = (bf16[192,192]{1,0:T(8,128)(2,1)}, f32[96,9216]{1,0:T(8,128)}) custom-call(f32[8,128]{1,0:T(8,128)} %bitcast.39, bf16[192,192]{1,0:T(8,128)(2,1)} %constant.39.clone.left_ref, s32[1]{0:T(128)} %dynamic_slice.3.role_ref, f32[96,9216]{1,0:T(8,128)} %bitcast.36, f32[96,9216]{1,0:T(8,128)} %bitcast.33), custom_call_target="tpu_custom_call" | custom-call | tf_op jit(solution)/shard_map/gate/pallas_call | solution.py:256
  51.0 1.3 collective-permute-start.5
  52.3 1.3 collective-permute-start.2
  53.6 0.0 collective-permute-done.3
  53.6 19.0 %pair_terms.4 = (f32[96,9216]{1,0:T(8,128)}, f32[96,9216]{1,0:T(8,128)}) custom-call(f32[96,9216]{1,0:T(8,128)} %bitcast.8.refs_0_, f32[96,9216]{1,0:T(8,128)} %bitcast.34, f32[96,96,128]{2,1,0:T(8,128)} %copy-done, bf16[192,192]{1,0:T(8,128)(2,1)} %get-tuple-element.15.refs_3_.refs_4_, bf16[256,256]{1,0:T(8,128)(2,1)} %constant.40.clone.refs_4_.refs_5_), custom_call_target="tpu_custom_call" | custom-call | flops 16000000000 | bytes 20000000 | tf_op jit(solution)/shard_map/pair_terms/pallas_call | solution.py:195
  72.6 19.2 %pair_terms.5 = (f32[96,9216]{1,0:T(8,128)}, f32[96,9216]{1,0:T(8,128)}) custom-call(f32[96,9216]{1,0:T(8,128)} %bitcast.37, f32[96,9216]{1,0:T(8,128)} %bitcast.35, f32[96,9216]{1,0:T(8,128)} %get-tuple-element.16.refs_2_, f32[96,96,128]{2,1,0:T(8,128)} %copy-done, bf16[192,192]{1,0:T(8,128)(2,1)} %get-tuple-element.15.refs_3_.refs_4_, ...), custom_call_target="tpu_custom_call" | custom-call | flops 16000000000 | bytes 20000000 | tf_op jit(solution)/shard_map/pair_terms/pallas_call | solution.py:195
  91.8 9.9 %collective-permute-start.4 = (f32[1,96,9216]{2,1,0:T(8,128)}, f32[1,96,9216]{2,1,0:T(8,128)S(1)}, u32[]{:S(2)}, u32[]{:S(2)}) collective-permute-start(f32[1,96,9216]{2,1,0:T(8,128)} %bitcast.42), channel_id=1, source_target_pairs={{9,4},{14,3},{6,11},{1,12},{25,20},{30,19},{22,27},{17,28}} | collective-permute-start | bytes 10616840 | tf_op jit(solution)/shard_map/ppermute | solution.py:289
  101.7 0.0 collective-permute-done.5
  101.7 19.1 %pair_terms.7 = (f32[48,9216]{1,0:T(8,128)}, f32[48,9216]{1,0:T(8,128)}, f32[96,9216]{1,0:T(8,128)}) custom-call(f32[96,9216]{1,0:T(8,128)} %bitcast.8.refs_0_, f32[96,9216]{1,0:T(8,128)} %bitcast.11.refs_1_, f32[96,9216]{1,0:T(8,128)} %get-tuple-element.19.refs_2_, f32[96,96,128]{2,1,0:T(8,128)} %copy-done, ...), custom_call_target="tpu_custom_call" | custom-call | flops 16000000000 | bytes 20000000 | tf_op jit(solution)/shard_map/pair_terms/pallas_call | solution.py:195
  120.8 2.5 %collective-permute-start.8 = (f32[1,48,9216]{2,1,0:T(8,128)}, f32[1,48,9216]{2,1,0:T(8,128)}, u32[]{:S(2)}, u32[]{:S(2)}) collective-permute-start(f32[1,48,9216]{2,1,0:T(8,128)} %bitcast.45), channel_id=1, source_target_pairs={{9,11},{14,12},{6,4},{1,3},{25,27},{30,28},{22,20},{17,19}} | collective-permute-start | bytes 5308424 | tf_op jit(solution)/shard_map/ppermute | solution.py:289
  123.4 5.2 %collective-permute-start.6 = (f32[1,96,9216]{2,1,0:T(8,128)}, f32[1,96,9216]{2,1,0:T(8,128)}, u32[]{:S(2)}, u32[]{:S(2)}) collective-permute-start(f32[1,96,9216]{2,1,0:T(8,128)} %bitcast.43), channel_id=1, source_target_pairs={{9,10},{14,13},{6,5},{1,2},{25,26},{30,29},{22,21},{17,18}} | collective-permute-start | bytes 10616840 | tf_op jit(solution)/shard_map/ppermute | solution.py:289
  128.6 2.6 %collective-permute-start.7 = (f32[1,48,9216]{2,1,0:T(8,128)}, f32[1,48,9216]{2,1,0:T(8,128)}, u32[]{:S(2)}, u32[]{:S(2)}) collective-permute-start(f32[1,48,9216]{2,1,0:T(8,128)} %bitcast.44), channel_id=1, source_target_pairs={{9,15},{14,8},{6,0},{1,7},{25,31},{30,24},{22,16},{17,23}} | collective-permute-start | bytes 5308424 | tf_op jit(solution)/shard_map/ppermute | solution.py:289
  131.1 21.4 %collective-permute-done.8 = f32[1,48,9216]{2,1,0:T(8,128)} collective-permute-done((f32[1,48,9216]{2,1,0:T(8,128)}, f32[1,48,9216]{2,1,0:T(8,128)}, u32[]{:S(2)}, u32[]{:S(2)}) %collective-permute-start.8) | collective-permute-done | bytes 1769504 | tf_op jit(solution)/shard_map/ppermute | solution.py:289
  152.5 1.9 collective-permute-start.9
  155.0 0.0 collective-permute-done.2
  155.0 18.5 %pair_terms.6 = f32[96,9216]{1,0:T(8,128)} custom-call(f32[96,9216]{1,0:T(8,128)} %bitcast.38, f32[96,9216]{1,0:T(8,128)} %bitcast.7.refs_1_, f32[96,9216]{1,0:T(8,128)} %get-tuple-element.17.refs_2_, f32[96,96,128]{2,1,0:T(8,128)} %copy-done, bf16[192,192]{1,0:T(8,128)(2,1)} %get-tuple-element.15.refs_3_.refs_4_, ...), custom_call_target="tpu_custom_call" | custom-call | flops 16000000000 | bytes 20000000 | tf_op jit(solution)/shard_map/pair_terms/pallas_call | solution.py:195
  173.5 0.0 collective-permute-done.4
  173.5 0.0 collective-permute-done.7
  173.6 0.0 collective-permute-done.9
  173.6 16.8 %collective-permute-done.6 = f32[1,96,9216]{2,1,0:T(8,128)} collective-permute-done((f32[1,96,9216]{2,1,0:T(8,128)}, f32[1,96,9216]{2,1,0:T(8,128)}, u32[]{:S(2)}, u32[]{:S(2)}) %collective-permute-start.6) | collective-permute-done | bytes 3538976 | tf_op jit(solution)/shard_map/ppermute | solution.py:289
  190.4 6.7 %fusion.9 = f32[1,96,9216]{2,1,0:T(8,128)} fusion(f32[48,9216]{1,0:T(8,128)} %bitcast.17, f32[48,9216]{1,0:T(8,128)} %bitcast.15, f32[1,96,9216]{2,1,0:T(8,128)} %collective-permute-done.6, f32[1,96,9216]{2,1,0:T(8,128)S(1)} %collective-permute-done.4, f32[96,9216]{1,0:T(8,128)} %pair_terms.6, pred[]{:T(512)} %bitcast), kind=kLoop, calls=%fused_computation.12 | loop fusion | flops 4423680 | bytes 17694720 | tf_op jit(solution)/shard_map/broadcast_in_dim | solution.py:315
  (5 shorter events, 0.0 us)
Async XLA Ops:
  0.0 47.4 %copy-start.3 = (s32[16]{0:T(128)S(1)}, s32[16]{0:T(128)}, u32[]{:S(2)}) copy-start(s32[16]{0:T(128)} %constant.41.clone) | copy-start | bytes 196
  0.0 46.1 %collective-permute-start = (f32[1,96,9216]{2,1,0:T(8,128)}, f32[1,96,9216]{2,1,0:T(8,128)S(1)}, u32[]{:S(2)}, u32[]{:S(2)}) collective-permute-start(f32[1,96,9216]{2,1,0:T(8,128)} %param.4), channel_id=1, source_target_pairs={{3,14},{4,9},{9,11},{14,12},{12,1},{11,6},{6,4},{1,3},{19,30},{20,... | collective-permute-start | bytes 10616840 | tf_op jit(solution)/shard_map/ppermute | solution.py:289
  4.1 49.5 %collective-permute-start.3 = (f32[1,96,9216]{2,1,0:T(8,128)}, f32[1,96,9216]{2,1,0:T(8,128)}, u32[]{:S(2)}, u32[]{:S(2)}) collective-permute-start(f32[1,96,9216]{2,1,0:T(8,128)} %param.4), channel_id=1, source_target_pairs={{8,14},{15,9},{7,1},{0,6},{24,30},{31,25},{23,17},{16,22}} | collective-permute-start | bytes 10616840 | tf_op jit(solution)/shard_map/ppermute | solution.py:289
  8.6 37.5 %copy-start = (f32[96,96,128]{2,1,0:T(8,128)}, f32[96,96,128]{2,1,0:T(8,128)S(1)}, u32[]{:S(2)}) copy-start(f32[96,96,128]{2,1,0:T(8,128)S(1)} %fusion.5.refs_2_.refs_3_) | copy-start | bytes 14155780
  46.1 2.0 %copy-start.1 = (f32[1,96,9216]{2,1,0:T(8,128)}, f32[1,96,9216]{2,1,0:T(8,128)S(1)}, u32[]{:S(2)}) copy-start(f32[1,96,9216]{2,1,0:T(8,128)S(1)} %collective-permute-done) | copy-start | bytes 10616836
  46.1 2.0 %collective-permute-start.1 = (f32[1,8,128]{2,1,0:T(8,128)S(1)}, f32[1,8,128]{2,1,0:T(8,128)S(1)}, u32[]{:S(2)}, u32[]{:S(2)}) collective-permute-start(f32[1,8,128]{2,1,0:T(8,128)S(1)} %fusion.11), channel_id=1, source_target_pairs={{14,2},{9,5},{1,13},{6,10},{30,18},{25,21},{17,29},{22,26}} | collective-permute-start | bytes 12296 | tf_op jit(solution)/shard_map/ppermute | solution.py:289
  48.2 0.6 copy-start.2
  51.0 50.7 %collective-permute-start.5 = (f32[1,96,9216]{2,1,0:T(8,128)}, f32[1,96,9216]{2,1,0:T(8,128)}, u32[]{:S(2)}, u32[]{:S(2)}) collective-permute-start(f32[1,96,9216]{2,1,0:T(8,128)} %bitcast.40), channel_id=1, source_target_pairs={{13,14},{10,9},{2,1},{5,6},{29,30},{26,25},{18,17},{21,22}} | collective-permute-start | bytes 10616840 | tf_op jit(solution)/shard_map/ppermute | solution.py:289
  52.3 102.7 %collective-permute-start.2 = (f32[1,96,9216]{2,1,0:T(8,128)}, f32[1,96,9216]{2,1,0:T(8,128)}, u32[]{:S(2)}, u32[]{:S(2)}) collective-permute-start(f32[1,96,9216]{2,1,0:T(8,128)} %bitcast.41), channel_id=1, source_target_pairs={{5,10},{2,13},{11,14},{12,9},{10,5},{13,2},{4,1},{3,6},{21,26},{18... | collective-permute-start | bytes 10616840 | tf_op jit(solution)/shard_map/ppermute | solution.py:289
  91.8 81.8 %collective-permute-start.4 = (f32[1,96,9216]{2,1,0:T(8,128)}, f32[1,96,9216]{2,1,0:T(8,128)S(1)}, u32[]{:S(2)}, u32[]{:S(2)}) collective-permute-start(f32[1,96,9216]{2,1,0:T(8,128)} %bitcast.42), channel_id=1, source_target_pairs={{9,4},{14,3},{6,11},{1,12},{25,20},{30,19},{22,27},{17,28}} | collective-permute-start | bytes 10616840 | tf_op jit(solution)/shard_map/ppermute | solution.py:289
  120.8 31.7 %collective-permute-start.8 = (f32[1,48,9216]{2,1,0:T(8,128)}, f32[1,48,9216]{2,1,0:T(8,128)}, u32[]{:S(2)}, u32[]{:S(2)}) collective-permute-start(f32[1,48,9216]{2,1,0:T(8,128)} %bitcast.45), channel_id=1, source_target_pairs={{9,11},{14,12},{6,4},{1,3},{25,27},{30,28},{22,20},{17,19}} | collective-permute-start | bytes 5308424 | tf_op jit(solution)/shard_map/ppermute | solution.py:289
  123.4 67.0 %collective-permute-start.6 = (f32[1,96,9216]{2,1,0:T(8,128)}, f32[1,96,9216]{2,1,0:T(8,128)}, u32[]{:S(2)}, u32[]{:S(2)}) collective-permute-start(f32[1,96,9216]{2,1,0:T(8,128)} %bitcast.43), channel_id=1, source_target_pairs={{9,10},{14,13},{6,5},{1,2},{25,26},{30,29},{22,21},{17,18}} | collective-permute-start | bytes 10616840 | tf_op jit(solution)/shard_map/ppermute | solution.py:289
  128.6 45.0 %collective-permute-start.7 = (f32[1,48,9216]{2,1,0:T(8,128)}, f32[1,48,9216]{2,1,0:T(8,128)}, u32[]{:S(2)}, u32[]{:S(2)}) collective-permute-start(f32[1,48,9216]{2,1,0:T(8,128)} %bitcast.44), channel_id=1, source_target_pairs={{9,15},{14,8},{6,0},{1,7},{25,31},{30,24},{22,16},{17,23}} | collective-permute-start | bytes 5308424 | tf_op jit(solution)/shard_map/ppermute | solution.py:289
  152.5 21.1 %collective-permute-start.9 = (f32[1,48,9216]{2,1,0:T(8,128)}, f32[1,48,9216]{2,1,0:T(8,128)}, u32[]{:S(2)}, u32[]{:S(2)}) collective-permute-start(f32[1,48,9216]{2,1,0:T(8,128)} %collective-permute-done.8), channel_id=1, source_target_pairs={{11,15},{12,8},{4,0},{3,7},{27,31},{28,24},{20,16},{19,23}} | collective-permute-start | bytes 5308424 | tf_op jit(solution)/shard_map/ppermute | solution.py:289

commit v6 on v5

v6 whole, which is shorter than its diff:
```python
import functools
import math

import jax
import jax.numpy as jnp
import numpy as np
from jax import lax
from jax.experimental import pallas as pl
from jax.experimental.pallas import tpu as pltpu
from jax.sharding import PartitionSpec as P

OFFSET = 5
screening = 5.44
LANES = 128
X_STEPS = 6
PLANE_STEPS = 6


def from_behind(value, axis, by):
    count = lax.axis_size(axis)
    return lax.ppermute(value, axis, [(i, (i + by) % count) for i in range(count)])


def screened_kernel(points):
    signed = jnp.arange(LANES, dtype=jnp.int32)
    inside = signed < points
    signed = jnp.where(signed >= points // 2, signed - points, signed)
    wavenumber = signed.astype(jnp.float32) * (2.0 * math.pi / points)
    squared = (
        wavenumber[:points, None, None] ** 2
        + wavenumber[None, :points, None] ** 2
        + wavenumber[None, None, :] ** 2
    )
    screen_rate = screening / points
    finite = jnp.where(squared > 0.0, squared, 1.0)
    screened = 4.0 * math.pi / finite * -jnp.expm1(-finite / (4.0 * screen_rate * screen_rate))
    kernel = jnp.where(squared > 0.0, screened, math.pi / (screen_rate * screen_rate))
    return jnp.where(inside, kernel / float(points * points * points), 0.0)


def hartley_tables(points):
    counter = np.arange(points)
    angles = 2.0 * np.pi * (counter[:, None] * counter[None, :] % points) / points
    table = np.cos(angles) + np.sin(angles)
    high = table.astype(jnp.bfloat16)
    low = (table - high.astype(np.float64)).astype(jnp.bfloat16)
    left = np.zeros((2 * points, 2 * points), jnp.bfloat16)
    left[:points, :points] = high
    left[:points, points:] = high
    left[points:, :points] = low
    right = np.zeros((2 * LANES, 2 * LANES), jnp.bfloat16)
    right[:points, :points] = high
    right[:points, LANES:LANES + points] = low
    right[LANES:LANES + points, :points] = high
    return jnp.asarray(left), jnp.asarray(right)


def two_terms(value):
    high = value.astype(jnp.bfloat16)
    low = (value - high.astype(jnp.float32)).astype(jnp.bfloat16)
    return high, low


def from_left(left, value):
    half = value.shape[0]
    terms = jnp.concatenate(two_terms(value), 0)
    out = jnp.dot(left, terms, preferred_element_type=jnp.float32)
    return out[:half] + out[half:]


def from_right(value, right):
    out = jnp.dot(jnp.concatenate(two_terms(value), 1), right, preferred_element_type=jnp.float32)
    return out[:, :LANES] + out[:, LANES:]


def pair_body(points, slot, has, *refs):
    refs = list(refs)
    flags_ref = refs.pop(0)
    names = ["a", "b"] + [name for name in ("sum_a", "sum_b") if name in has]
    far = {name: refs.pop(0) for name in names}
    if "then" in has:
        refs.pop(0)
    kernel_ref, left_ref, right_ref = refs.pop(0), refs.pop(0), refs.pop(0)
    out_refs = {"for_a": refs.pop(0)}
    if "halves" in has:
        out_refs["low_a"] = refs.pop(0)
    if "for_b" in has:
        out_refs["for_b"] = refs.pop(0)
    held, near, near_kernel, near_out, sems, kernel_sems, out_sems = refs
    outs = list(out_refs)
    step = pl.program_id(0)
    active = flags_ref[2 * slot] == 1
    with_sum = flags_ref[2 * slot + 1] == 1
    columns = near.shape[2] // X_STEPS
    ys = columns // points
    per_step = points // PLANE_STEPS
    late = X_STEPS + PLANE_STEPS

    def span_of(chunk):
        start = chunk * columns
        return pl.ds(start if isinstance(chunk, int) else pl.multiple_of(start, columns), columns)

    def fetch(name, chunk):
        place, span = names.index(name), span_of(chunk)
        return pltpu.make_async_copy(
            far[name].at[:, span], near.at[place, :, span], sems.at[place, chunk]
        )

    def fetch_kernel(part):
        span = pl.ds(part * per_step, per_step)
        return pltpu.make_async_copy(
            kernel_ref.at[span], near_kernel.at[span], kernel_sems.at[part]
        )

    def give(name, chunk):
        span = span_of(chunk)
        source = near_out.at[0 if name != "for_b" else 1]
        if "halves" in has and name != "for_b":
            rows = pl.ds(points // 2 if name == "low_a" else 0, points // 2)
            source = source.at[rows, span]
        else:
            source = source.at[:, span]
        return pltpu.make_async_copy(
            source, out_refs[name].at[:, span], out_sems.at[outs.index(name), chunk]
        )

    def here(name, chunk):
        return near[names.index(name), :, span_of(chunk)]

    sums = [name for name in names if name.startswith("sum")]

    @pl.when(active & (step == 0))
    def start_first():
        for chunk in range(2):
            for name in ("a", "b"):
                fetch(name, chunk).start()

    @pl.when(active & (step + 2 < X_STEPS))
    def start_next():
        for name in ("a", "b"):
            fetch(name, step + 2).start()

    @pl.when(active & (step == X_STEPS - 2))
    def start_kernel():
        for part in range(PLANE_STEPS):
            fetch_kernel(part).start()

    if sums:
        @pl.when(active & (step == X_STEPS))
        def start_sums():
            for chunk in range(X_STEPS):
                for name in sums:
                    fetch(name, chunk).start()

    def lanes_apart(block):
        gap = jnp.zeros((points, LANES - points), jnp.float32)
        rows = [
            jnp.concatenate([block[:, q * points:(q + 1) * points], gap], 1) for q in range(ys)
        ]
        return jnp.swapaxes(jnp.stack(rows, 0), 0, 1)

    def lanes_together(block):
        block = jnp.swapaxes(block, 0, 1)
        return jnp.concatenate([block[q][:, :points] for q in range(ys)], 1)

    def side_by_side(block):
        return jnp.concatenate([block[i] for i in range(per_step)], 1)

    @pl.when(active & (step < X_STEPS))
    def forward_x():
        for name in ("a", "b"):
            fetch(name, step).wait()
        spectrum = from_left(left_ref[...], here("a", step) * here("b", step))
        start = pl.multiple_of(step * ys, ys)
        held[:, pl.ds(start, ys), :] = lanes_apart(spectrum)

    @pl.when(active & (step >= X_STEPS) & (step < late))
    def planes():
        left = left_ref[...]
        right = right_ref[...]
        part = step - X_STEPS
        first = part * per_step
        block = held[pl.ds(first, per_step)].reshape(per_step * points, LANES)
        block = from_right(block, right).reshape(per_step, points, LANES)
        wide = from_left(left, side_by_side(block))
        fetch_kernel(part).wait()
        wide = from_left(left, wide * side_by_side(near_kernel[pl.ds(first, per_step)]))
        block = jnp.concatenate(
            [wide[:, i * LANES:(i + 1) * LANES] for i in range(per_step)], 0
        )
        block = from_right(block, right)
        held[pl.ds(first, per_step)] = block.reshape(per_step, points, LANES)

    @pl.when(active & (step >= late))
    def inverse_x():
        chunk = step - late
        start = pl.multiple_of(chunk * ys, ys)
        for name in sums:
            fetch(name, chunk).wait()
        block = lanes_together(held[:, pl.ds(start, ys), :])
        potential = from_left(left_ref[...], block)
        for_a = -(here("b", chunk) * potential)
        if "sum_a" in has:
            for_a = for_a + jnp.where(with_sum, here("sum_a", chunk), 0.0)
        near_out[0, :, span_of(chunk)] = for_a
        if "for_b" in has:
            for_b = -(here("a", chunk) * potential)
            if "sum_b" in has:
                for_b = for_b + here("sum_b", chunk)
            near_out[1, :, span_of(chunk)] = for_b
        for name in outs:
            give(name, chunk).start()

    @pl.when(active & (step == late + X_STEPS - 1))
    def wait_outs():
        for chunk in range(X_STEPS):
            for name in outs:
                give(name, chunk).wait()


def pair_terms(
    flags, slot, a, b, constants, sum_a=None, sum_b=None, for_b=False, halves=False, in_place=False, then=None
):
    points, plane = a.shape
    kernel, left, right = constants
    optional = {"sum_a": sum_a, "sum_b": sum_b}
    optional = {name: value for name, value in optional.items() if value is not None}
    blocks = [a, b, *optional.values()]
    waited = [] if then is None else [then]
    has = list(optional) + ["for_b"] * for_b + ["halves"] * halves + ["then"] * len(waited)
    rows = ([points // 2] * 2 if halves else [points]) + [points] * for_b
    anywhere = pl.BlockSpec(memory_space=pl.ANY)
    out = pl.pallas_call(
        functools.partial(pair_body, points, slot, has),
        grid=(2 * X_STEPS + PLANE_STEPS,),
        in_specs=[pl.BlockSpec(memory_space=pltpu.SMEM)]
        + [anywhere] * (len(blocks) + len(waited) + 1)
        + [pl.BlockSpec(table.shape, lambda i: (0, 0)) for table in (left, right)],
        out_specs=[anywhere] * len(rows),
        out_shape=[jax.ShapeDtypeStruct((n, plane), jnp.float32) for n in rows],
        input_output_aliases={3: 0} if in_place else {},
        scratch_shapes=[
            pltpu.VMEM((points, points, LANES), jnp.float32),
            pltpu.VMEM((len(blocks), points, plane), jnp.float32),
            pltpu.VMEM((points, points, LANES), jnp.float32),
            pltpu.VMEM((2 if for_b else 1, points, plane), jnp.float32),
            pltpu.SemaphoreType.DMA((len(blocks), X_STEPS)),
            pltpu.SemaphoreType.DMA((PLANE_STEPS,)),
            pltpu.SemaphoreType.DMA((len(rows), X_STEPS)),
        ],
        compiler_params=pltpu.CompilerParams(vmem_limit_bytes=60 * 2**20),
        cost_estimate=pl.CostEstimate(
            flops=16_000_000_000, bytes_accessed=20_000_000, transcendentals=0
        ),
        name="pair_terms",
    )(flags, *blocks, *waited, kernel, left, right)
    return out if len(rows) > 1 else out[0]


def copy_body(block_ref, new_block_ref):
    new_block_ref[...] = block_ref[...]


def copied(block):
    points, plane = block.shape
    part = pl.BlockSpec((points, plane // X_STEPS), lambda i: (0, i))
    return pl.pallas_call(
        copy_body,
        grid=(X_STEPS,),
        in_specs=[part],
        out_specs=part,
        out_shape=jax.ShapeDtypeStruct(block.shape, block.dtype),
        compiler_params=pltpu.CompilerParams(vmem_limit_bytes=60 * 2**20),
        name="copied",
    )(block)


def gate_body(token_ref, left_ref, block_ref, new_left_ref, new_block_ref):
    new_left_ref[...] = left_ref[...]


def gate(token, left, block):
    in_vmem = pl.BlockSpec(memory_space=pltpu.VMEM)
    anywhere = pl.BlockSpec(memory_space=pl.ANY)
    return pl.pallas_call(
        gate_body,
        in_specs=[in_vmem, in_vmem, anywhere],
        out_specs=[in_vmem, anywhere],
        out_shape=[
            jax.ShapeDtypeStruct(left.shape, left.dtype),
            jax.ShapeDtypeStruct(block.shape, block.dtype),
        ],
        input_output_aliases={2: 1},
        compiler_params=pltpu.CompilerParams(vmem_limit_bytes=60 * 2**20),
        name="gate",
    )(token, left, block)


def both_halves(*pairs):
    return list(pairs) + [(15 - source, 15 - target) for source, target in pairs]


CROSSING = both_halves((3, 14), (4, 9))
PARTNERS = both_halves((8, 14), (15, 9), (9, 11), (14, 12))
ARRIVED = both_halves((14, 2), (9, 5))
SINGLES = both_halves((5, 10), (2, 13))
BESIDE = both_halves((13, 14), (10, 9))
PASSED = both_halves((9, 10), (14, 13), (11, 14), (12, 9))
HOME_ACROSS = both_halves((9, 4), (14, 3))
HOME_FAR = both_halves((9, 15), (14, 8))
HOME_TURN = both_halves((9, 11), (14, 12))
HOME_TURNED = both_halves((11, 15), (12, 8))
HUB_FLAGS = (1, 0, 1, 0, 1, 1, 1, 1, 0, 0)
SINGLE_FLAGS = (0, 0, 0, 0, 0, 0, 1, 0, 1, 1)
FLAGS = {9: HUB_FLAGS, 14: HUB_FLAGS, 6: HUB_FLAGS, 1: HUB_FLAGS}
FLAGS.update({10: SINGLE_FLAGS, 13: SINGLE_FLAGS, 5: SINGLE_FLAGS, 2: SINGLE_FLAGS})


def sixteen_bands(orbitals, constants):
    def send(value, pairs):
        return lax.ppermute(value[None], "band", pairs)[0]

    kernel, left, right = constants
    own = orbitals[0]
    flags = jnp.asarray([FLAGS.get(i, (0,) * 10) for i in range(16)], jnp.int32)
    flags = flags[lax.axis_index("band")]
    pair = functools.partial(pair_terms, flags)
    crossed = send(own, CROSSING)
    partner = send(own, PARTNERS)
    own_copy = copied(own)
    token = crossed[:8, :LANES] + kernel[0, :8] + own_copy[:8, :LANES]
    left, held_back = gate(send(token, ARRIVED), left, own_copy)
    constants = (kernel, left, right)
    single = send(held_back, SINGLES)
    beside = send(held_back, BESIDE)
    passed = send(partner, PASSED)

    partner_sum, crossed_sum = pair(0, partner, crossed, constants, for_b=True)
    own_sum, crossed_sum = pair(1, own, crossed, constants, sum_b=crossed_sum, for_b=True)
    home = send(crossed_sum, HOME_ACROSS)
    top, bottom = pair(2, partner, beside, constants, sum_a=partner_sum, halves=True, then=own_sum)
    bottom = send(bottom, HOME_TURN)
    top = send(top, HOME_FAR)
    bottom = send(bottom, HOME_TURNED)
    own_sum = pair(3, own, passed, constants, sum_a=own_sum)
    own_sum = pair(4, own, single, constants, sum_a=own_sum, in_place=True)
    own_sum = jnp.where(flags[6] == 1, own_sum, 0.0)
    return (own_sum + home + jnp.concatenate([top, bottom], 0))[None]


def any_bands(orbitals, constants):
    own = orbitals[0]
    flags = jnp.ones((4,), jnp.int32)
    lower = from_behind(orbitals, "band", OFFSET)[0]
    upper = from_behind(orbitals, "band", -OFFSET)[0]
    total = pair_terms(flags, 0, own, lower, constants)
    return pair_terms(flags, 1, own, upper, constants, sum_a=total)[None]


def local(bands, orbitals):
    points = orbitals.shape[1]
    constants = (screened_kernel(points), *hartley_tables(points))
    if bands == 16:
        return sixteen_bands(orbitals, constants)
    return any_bands(orbitals, constants)


def solution(mesh):
    return jax.shard_map(
        functools.partial(local, mesh.shape["band"]),
        mesh=mesh,
        in_specs=(P(("groups", "band"), None, None),),
        out_specs=P(("groups", "band"), None, None),
        check_vma=False,
    )
```

time: 198 us -> 193 us (0.975)
  the two profiles are of different devices: /device:TPU:1 before, /device:TPU:0 now
where the time goes in v6:
time: 193 us; the launch traced here: 192 us
  waiting for transfers between devices  135 us (70%)
  starting transfers between devices  20.9 us (11%)
  Pallas kernels  19.9 us (10%)
  other arithmetic  8.64 us (4%)
  local copies, waits for them, and re-layouts  6.37 us (3%)
    ppermute x10, waiting for transfers between devices, send(): return lax.ppermute(value[None], 'band', pairs)[0]  135 us
    ppermute x10, starting transfers between devices, send(): return lax.ppermute(value[None], 'band', pairs)[0]  20.9 us
    pallas_call x5, Pallas kernels, pair_terms(): pl.pallas_call(functools.partial(pair_body, points, slot, has), grid=(2 *...  12.9 us
    pallas_call x1, Pallas kernels, copied(): pl.pallas_call(copy_body, grid=(X_STEPS,), in_specs=[part], out_specs=par...  5.44 us
    broadcast_in_dim x1, other arithmetic, sixteen_bands(): return (own_sum + home + jnp.concatenate([top, bottom], 0))[None]  4.77 us
    unnamed x6, local copies, waits for them, and re-layouts  4.5 us
  transfers between devices with their start and end apart: 10, of which 2 were waited for; matrix products, arithmetic and copies ran while one was open for 3% of the time, Pallas kernels for 10%

profile of v6, /device:TPU:0, one launch (start us, length us, event | category | flops | bytes accessed | tf_op | source)
XLA Modules:
  0.0 192.1 jit_solution(2397342636208076853)
XLA Ops:
  0.0 2.5 %collective-permute-start = (f32[1,96,9216]{2,1,0:T(8,128)}, f32[1,96,9216]{2,1,0:T(8,128)}, u32[]{:S(2)}, u32[]{:S(2)}) collective-permute-start(f32[1,96,9216]{2,1,0:T(8,128)} %param.4), channel_id=1, source_target_pairs={{3,14},{4,9},{12,1},{11,6},{19,30},{20,25},{28,17},{27,22}} | collective-permute-start | bytes 10616840 | tf_op jit(solution)/shard_map/ppermute | solution.py:321
  2.5 6.5 %collective-permute-start.3 = (f32[1,96,9216]{2,1,0:T(8,128)}, f32[1,96,9216]{2,1,0:T(8,128)}, u32[]{:S(2)}, u32[]{:S(2)}) collective-permute-start(f32[1,96,9216]{2,1,0:T(8,128)} %param.4), channel_id=1, source_target_pairs={{8,14},{15,9},{9,11},{14,12},{7,1},{0,6},{6,4},{1,3},{24,30},{31,2... | collective-permute-start | bytes 10616840 | tf_op jit(solution)/shard_map/ppermute | solution.py:321
  9.0 5.4 %copied.1.block_ref = f32[96,9216]{1,0:T(8,128)} custom-call(f32[96,9216]{1,0:T(8,128)} %bitcast.32), custom_call_target="tpu_custom_call" | custom-call | tf_op jit(solution)/shard_map/copied/pallas_call | solution.py:267
  14.5 0.1 broadcast_add_fusion
  14.5 3.1 %fusion.5.refs_3_.refs_4_.refs_5_ = f32[96,96,128]{2,1,0:T(8,128)S(1)} fusion(f32[128]{0:T(128)S(1)} %fusion.14, f32[96,96]{1,0:T(8,128)S(1)} %broadcast_add_fusion, pred[128]{0:T(512)(128)(4,1)S(1)} %iota_compare_fusion), kind=kLoop, calls=%fused_computation.7 | loop fusion | flops 12976128 | bytes 4756096 | tf_op jit(solution)/shard_map/jit(_where)/select_n | solution.py:38
  17.6 0.0 copy-start
  17.6 0.0 collective-permute-done
  17.6 2.1 %copy-done = f32[96,96,128]{2,1,0:T(8,128)} copy-done((f32[96,96,128]{2,1,0:T(8,128)}, f32[96,96,128]{2,1,0:T(8,128)S(1)}, u32[]{:S(2)}) %copy-start) | copy-done | bytes 4718616
  19.7 0.7 fusion.10
  20.4 0.6 collective-permute-start.1
  21.1 0.0 collective-permute-done.1
  21.1 0.0 copy-start.1
  21.1 0.6 copy-done.1
  21.7 1.5 gate.1
  23.2 0.9 collective-permute-start.6
  24.1 1.3 constant_dynamic-slice_fusion
  25.4 21.1 %collective-permute-done.3 = f32[1,96,9216]{2,1,0:T(8,128)} collective-permute-done((f32[1,96,9216]{2,1,0:T(8,128)}, f32[1,96,9216]{2,1,0:T(8,128)}, u32[]{:S(2)}, u32[]{:S(2)}) %collective-permute-start.3) | collective-permute-done | bytes 3538976 | tf_op jit(solution)/shard_map/ppermute | solution.py:321
  46.5 2.4 %collective-permute-start.4 = (f32[1,96,9216]{2,1,0:T(8,128)}, f32[1,96,9216]{2,1,0:T(8,128)}, u32[]{:S(2)}, u32[]{:S(2)}) collective-permute-start(f32[1,96,9216]{2,1,0:T(8,128)} %collective-permute-done.3), channel_id=1, source_target_pairs={{9,10},{14,13},{11,14},{12,9},{6,5},{1,2},{4,1},{3,6},{25,26},{30,... | collective-permute-start | bytes 10616840 | tf_op jit(solution)/shard_map/ppermute | solution.py:321
  48.9 2.4 %collective-permute-start.2 = (f32[1,96,9216]{2,1,0:T(8,128)}, f32[1,96,9216]{2,1,0:T(8,128)}, u32[]{:S(2)}, u32[]{:S(2)}) collective-permute-start(f32[1,96,9216]{2,1,0:T(8,128)} %bitcast.31), channel_id=1, source_target_pairs={{5,10},{2,13},{10,5},{13,2},{21,26},{18,29},{26,21},{29,18}} | collective-permute-start | bytes 10616840 | tf_op jit(solution)/shard_map/ppermute | solution.py:321
  51.4 2.5 %pair_terms.5 = (f32[96,9216]{1,0:T(8,128)}, f32[96,9216]{1,0:T(8,128)}) custom-call(s32[10]{0:T(128)} %get-tuple-element.22.refs_0_, f32[96,9216]{1,0:T(8,128)} %bitcast.10.refs_1_, f32[96,9216]{1,0:T(8,128)} %bitcast.3.refs_2_, f32[96,96,128]{2,1,0:T(8,128)} %copy-done, bf16[192,192]{1,0:T(8,128)(2,1)} %get-tuple-element.14.refs_4_.refs_5_.refs_6_, ...), custom_call_target="tpu_custom_call" | custom-call | flops 16000000000 | bytes 20000000 | tf_op jit(solution)/shard_map/pair_terms/pallas_call | solution.py:233
  53.8 2.7 %pair_terms.6 = (f32[96,9216]{1,0:T(8,128)}, f32[96,9216]{1,0:T(8,128)}) custom-call(s32[10]{0:T(128)} %get-tuple-element.22.refs_0_, f32[96,9216]{1,0:T(8,128)} %bitcast.33, f32[96,9216]{1,0:T(8,128)} %bitcast.3.refs_2_, f32[96,9216]{1,0:T(8,128)} %get-tuple-element.15.refs_3_, f32[96,96,128]{2,1,0:T(8,128)} %copy-done, ...), custom_call_target="tpu_custom_call" | custom-call | flops 16000000000 | bytes 20000000 | tf_op jit(solution)/shard_map/pair_terms/pallas_call | solution.py:233
  56.5 0.0 collective-permute-done.6
  56.5 0.0 copy-start.2
  56.6 1.8 copy-done.2
  58.3 2.7 %pair_terms.9 = (f32[48,9216]{1,0:T(8,128)}, f32[48,9216]{1,0:T(8,128)}) custom-call(s32[10]{0:T(128)} %get-tuple-element.22.refs_0_, f32[96,9216]{1,0:T(8,128)} %bitcast.10.refs_1_, f32[96,9216]{1,0:T(8,128)} %bitcast.38, f32[96,9216]{1,0:T(8,128)} %get-tuple-element.18.refs_3_, f32[96,9216]{1,0:T(8,128)} %get-tuple-element.16.refs_3_.refs_4_, ...), custom_call_target="tpu_custom_call" | custom-call | flops 16000000000 | bytes 20000000 | tf_op jit(solution)/shard_map/pair_terms/pallas_call | solution.py:233
  61.1 1.9 collective-permute-start.8
  63.0 0.9 collective-permute-start.5
  63.9 0.6 slice.27
  65.1 1.3 collective-permute-start.7
  66.4 0.0 collective-permute-done.8
  66.4 1.5 collective-permute-start.9
  67.9 0.0 collective-permute-done.4
  67.9 2.5 %pair_terms.7.refs_3_ = f32[96,9216]{1,0:T(8,128)} custom-call(s32[10]{0:T(128)} %get-tuple-element.22.refs_0_, f32[96,9216]{1,0:T(8,128)} %bitcast.34, f32[96,9216]{1,0:T(8,128)} %bitcast.9.refs_2_, f32[96,9216]{1,0:T(8,128)} %get-tuple-element.16.refs_3_.refs_4_, f32[96,96,128]{2,1,0:T(8,128)} %copy-done, ...), custom_call_target="tpu_custom_call" | custom-call | flops 16000000000 | bytes 20000000 | tf_op jit(solution)/shard_map/pair_terms/pallas_call | solution.py:233
  70.4 0.0 collective-permute-done.2
  70.4 2.5 %pair_terms.8 = f32[96,9216]{1,0:T(8,128)} custom-call(s32[10]{0:T(128)} %get-tuple-element.22.refs_0_, f32[96,9216]{1,0:T(8,128)} %bitcast.35, f32[96,9216]{1,0:T(8,128)} %bitcast.8.refs_2_, f32[96,9216]{1,0:T(8,128)} %pair_terms.7.refs_3_, f32[96,96,128]{2,1,0:T(8,128)} %copy-done, ...), custom_call_target="tpu_custom_call", output_to_operand_aliasing={{}: (3, {})} | custom-call | flops 16000000000 | bytes 20000000 | tf_op jit(solution)/shard_map/pair_terms/pallas_call | solution.py:233
  72.9 0.0 collective-permute-done.5
  73.0 114.4 %collective-permute-done.7 = f32[1,48,9216]{2,1,0:T(8,128)} collective-permute-done((f32[1,48,9216]{2,1,0:T(8,128)}, f32[1,48,9216]{2,1,0:T(8,128)}, u32[]{:S(2)}, u32[]{:S(2)}) %collective-permute-start.7) | collective-permute-done | bytes 1769504 | tf_op jit(solution)/shard_map/ppermute | solution.py:321
  187.3 0.0 collective-permute-done.9
  187.3 4.8 %fusion.9 = f32[1,96,9216]{2,1,0:T(8,128)} fusion(f32[48,9216]{1,0:T(8,128)} %bitcast.17, f32[48,9216]{1,0:T(8,128)} %bitcast.15, f32[1,96,9216]{2,1,0:T(8,128)S(1)} %collective-permute-done.5, f32[96,9216]{1,0:T(8,128)} %pair_terms.8, pred[]{:T(512)} %bitcast), kind=kLoop, calls=%fused_computation.12 | loop fusion | flops 3538944 | bytes 14155777 | tf_op jit(solution)/shard_map/broadcast_in_dim | solution.py:348
  (4 shorter events, 0.0 us)
Async XLA Ops:
  0.0 17.6 %collective-permute-start = (f32[1,96,9216]{2,1,0:T(8,128)}, f32[1,96,9216]{2,1,0:T(8,128)}, u32[]{:S(2)}, u32[]{:S(2)}) collective-permute-start(f32[1,96,9216]{2,1,0:T(8,128)} %param.4), channel_id=1, source_target_pairs={{3,14},{4,9},{12,1},{11,6},{19,30},{20,25},{28,17},{27,22}} | collective-permute-start | bytes 10616840 | tf_op jit(solution)/shard_map/ppermute | solution.py:321
  2.5 44.0 %collective-permute-start.3 = (f32[1,96,9216]{2,1,0:T(8,128)}, f32[1,96,9216]{2,1,0:T(8,128)}, u32[]{:S(2)}, u32[]{:S(2)}) collective-permute-start(f32[1,96,9216]{2,1,0:T(8,128)} %param.4), channel_id=1, source_target_pairs={{8,14},{15,9},{9,11},{14,12},{7,1},{0,6},{6,4},{1,3},{24,30},{31,2... | collective-permute-start | bytes 10616840 | tf_op jit(solution)/shard_map/ppermute | solution.py:321
  17.6 2.1 %copy-start = (f32[96,96,128]{2,1,0:T(8,128)}, f32[96,96,128]{2,1,0:T(8,128)S(1)}, u32[]{:S(2)}) copy-start(f32[96,96,128]{2,1,0:T(8,128)S(1)} %fusion.5.refs_3_.refs_4_.refs_5_) | copy-start | bytes 14155780
  20.4 0.7 collective-permute-start.1
  21.1 0.6 copy-start.1
  23.2 33.3 %collective-permute-start.6 = (f32[1,96,9216]{2,1,0:T(8,128)}, f32[1,96,9216]{2,1,0:T(8,128)S(1)}, u32[]{:S(2)}, u32[]{:S(2)}) collective-permute-start(f32[1,96,9216]{2,1,0:T(8,128)} %bitcast.30), channel_id=1, source_target_pairs={{13,14},{10,9},{2,1},{5,6},{29,30},{26,25},{18,17},{21,22}} | collective-permute-start | bytes 10616840 | tf_op jit(solution)/shard_map/ppermute | solution.py:321
  46.5 21.4 %collective-permute-start.4 = (f32[1,96,9216]{2,1,0:T(8,128)}, f32[1,96,9216]{2,1,0:T(8,128)}, u32[]{:S(2)}, u32[]{:S(2)}) collective-permute-start(f32[1,96,9216]{2,1,0:T(8,128)} %collective-permute-done.3), channel_id=1, source_target_pairs={{9,10},{14,13},{11,14},{12,9},{6,5},{1,2},{4,1},{3,6},{25,26},{30,... | collective-permute-start | bytes 10616840 | tf_op jit(solution)/shard_map/ppermute | solution.py:321
  48.9 21.5 %collective-permute-start.2 = (f32[1,96,9216]{2,1,0:T(8,128)}, f32[1,96,9216]{2,1,0:T(8,128)}, u32[]{:S(2)}, u32[]{:S(2)}) collective-permute-start(f32[1,96,9216]{2,1,0:T(8,128)} %bitcast.31), channel_id=1, source_target_pairs={{5,10},{2,13},{10,5},{13,2},{21,26},{18,29},{26,21},{29,18}} | collective-permute-start | bytes 10616840 | tf_op jit(solution)/shard_map/ppermute | solution.py:321
  56.5 1.8 copy-start.2
  61.1 5.3 %collective-permute-start.8 = (f32[1,48,9216]{2,1,0:T(8,128)}, f32[1,48,9216]{2,1,0:T(8,128)}, u32[]{:S(2)}, u32[]{:S(2)}) collective-permute-start(f32[1,48,9216]{2,1,0:T(8,128)} %bitcast.40), channel_id=1, source_target_pairs={{9,11},{14,12},{6,4},{1,3},{25,27},{30,28},{22,20},{17,19}} | collective-permute-start | bytes 5308424 | tf_op jit(solution)/shard_map/ppermute | solution.py:321
  63.0 10.0 %collective-permute-start.5 = (f32[1,96,9216]{2,1,0:T(8,128)}, f32[1,96,9216]{2,1,0:T(8,128)S(1)}, u32[]{:S(2)}, u32[]{:S(2)}) collective-permute-start(f32[1,96,9216]{2,1,0:T(8,128)} %bitcast.37), channel_id=1, source_target_pairs={{9,4},{14,3},{6,11},{1,12},{25,20},{30,19},{22,27},{17,28}} | collective-permute-start | bytes 10616840 | tf_op jit(solution)/shard_map/ppermute | solution.py:321
  65.1 122.2 %collective-permute-start.7 = (f32[1,48,9216]{2,1,0:T(8,128)}, f32[1,48,9216]{2,1,0:T(8,128)}, u32[]{:S(2)}, u32[]{:S(2)}) collective-permute-start(f32[1,48,9216]{2,1,0:T(8,128)} %bitcast.39), channel_id=1, source_target_pairs={{9,15},{14,8},{6,0},{1,7},{25,31},{30,24},{22,16},{17,23}} | collective-permute-start | bytes 5308424 | tf_op jit(solution)/shard_map/ppermute | solution.py:321
  66.4 120.9 %collective-permute-start.9 = (f32[1,48,9216]{2,1,0:T(8,128)}, f32[1,48,9216]{2,1,0:T(8,128)}, u32[]{:S(2)}, u32[]{:S(2)}) collective-permute-start(f32[1,48,9216]{2,1,0:T(8,128)} %collective-permute-done.8), channel_id=1, source_target_pairs={{11,15},{12,8},{4,0},{3,7},{27,31},{28,24},{20,16},{19,23}} | collective-permute-start | bytes 5308424 | tf_op jit(solution)/shard_map/ppermute | solution.py:321

commit v7 on v6

--- a/solution.py
+++ b/solution.py
@@ -14,6 +14,7 @@
 LANES = 128
 X_STEPS = 6
 PLANE_STEPS = 6
+FAR_ROWS = 40
 
 
 def from_behind(value, axis, by):
@@ -86,6 +87,8 @@
         out_refs["low_a"] = refs.pop(0)
     if "for_b" in has:
         out_refs["for_b"] = refs.pop(0)
+    if "hand_on" in has:
+        refs.pop(0)
     held, near, near_kernel, near_out, sems, kernel_sems, out_sems = refs
     outs = list(out_refs)
     step = pl.program_id(0)
@@ -116,7 +119,7 @@
         span = span_of(chunk)
         source = near_out.at[0 if name != "for_b" else 1]
         if "halves" in has and name != "for_b":
-            rows = pl.ds(points // 2 if name == "low_a" else 0, points // 2)
+            rows = pl.ds(points - FAR_ROWS, FAR_ROWS) if name == "low_a" else pl.ds(0, points - FAR_ROWS)
             source = source.at[rows, span]
         else:
             source = source.at[:, span]
@@ -219,7 +222,7 @@
 
 
 def pair_terms(
-    flags, slot, a, b, constants, sum_a=None, sum_b=None, for_b=False, halves=False, in_place=False, then=None
+    flags, slot, a, b, constants, sum_a=None, sum_b=None, for_b=False, halves=False, in_place=False, then=None, hand_on=False
 ):
     points, plane = a.shape
     kernel, left, right = constants
@@ -228,7 +231,11 @@
     blocks = [a, b, *optional.values()]
     waited = [] if then is None else [then]
     has = list(optional) + ["for_b"] * for_b + ["halves"] * halves + ["then"] * len(waited)
-    rows = ([points // 2] * 2 if halves else [points]) + [points] * for_b
+    has += ["hand_on"] * hand_on
+    rows = ([points - FAR_ROWS, FAR_ROWS] if halves else [points]) + [points] * for_b
+    aliases = {3: 0} if in_place else {}
+    if hand_on:
+        aliases[1] = len(rows)
     anywhere = pl.BlockSpec(memory_space=pl.ANY)
     out = pl.pallas_call(
         functools.partial(pair_body, points, slot, has),
@@ -236,9 +243,11 @@
         in_specs=[pl.BlockSpec(memory_space=pltpu.SMEM)]
         + [anywhere] * (len(blocks) + len(waited) + 1)
         + [pl.BlockSpec(table.shape, lambda i: (0, 0)) for table in (left, right)],
-        out_specs=[anywhere] * len(rows),
-        out_shape=[jax.ShapeDtypeStruct((n, plane), jnp.float32) for n in rows],
-        input_output_aliases={3: 0} if in_place else {},
+        out_specs=[anywhere] * (len(rows) + hand_on),
+        out_shape=[
+            jax.ShapeDtypeStruct((n, plane), jnp.float32) for n in rows + [points] * hand_on
+        ],
+        input_output_aliases=aliases,
         scratch_shapes=[
             pltpu.VMEM((points, points, LANES), jnp.float32),
             pltpu.VMEM((len(blocks), points, plane), jnp.float32),
@@ -248,31 +257,31 @@
             pltpu.SemaphoreType.DMA((PLANE_STEPS,)),
             pltpu.SemaphoreType.DMA((len(rows), X_STEPS)),
         ],
-        compiler_params=pltpu.CompilerParams(vmem_limit_bytes=60 * 2**20),
+        compiler_params=pltpu.CompilerParams(vmem_limit_bytes=62 * 2**20),
         cost_estimate=pl.CostEstimate(
-            flops=16_000_000_000, bytes_accessed=20_000_000, transcendentals=0
+            flops=100_000_000, bytes_accessed=1_000_000, transcendentals=0
         ),
         name="pair_terms",
     )(flags, *blocks, *waited, kernel, left, right)
-    return out if len(rows) > 1 else out[0]
-
-
-def copy_body(block_ref, new_block_ref):
+    return out if len(out) > 1 else out[0]
+
+
+def copy_body(flags_ref, block_ref, new_block_ref):
     new_block_ref[...] = block_ref[...]
 
 
-def copied(block):
+def copied(flags, block):
     points, plane = block.shape
     part = pl.BlockSpec((points, plane // X_STEPS), lambda i: (0, i))
     return pl.pallas_call(
         copy_body,
         grid=(X_STEPS,),
-        in_specs=[part],
+        in_specs=[pl.BlockSpec(memory_space=pltpu.SMEM), part],
         out_specs=part,
         out_shape=jax.ShapeDtypeStruct(block.shape, block.dtype),
-        compiler_params=pltpu.CompilerParams(vmem_limit_bytes=60 * 2**20),
+        compiler_params=pltpu.CompilerParams(vmem_limit_bytes=62 * 2**20),
         name="copied",
-    )(block)
+    )(flags, block)
 
 
 def gate_body(token_ref, left_ref, block_ref, new_left_ref, new_block_ref):
@@ -291,9 +300,26 @@
             jax.ShapeDtypeStruct(block.shape, block.dtype),
         ],
         input_output_aliases={2: 1},
-        compiler_params=pltpu.CompilerParams(vmem_limit_bytes=60 * 2**20),
+        compiler_params=pltpu.CompilerParams(vmem_limit_bytes=62 * 2**20),
         name="gate",
     )(token, left, block)
+
+
+def hold_body(block_ref, then_ref, new_block_ref):
+    del block_ref, then_ref, new_block_ref
+
+
+def hold(block, then):
+    anywhere = pl.BlockSpec(memory_space=pl.ANY)
+    return pl.pallas_call(
+        hold_body,
+        in_specs=[anywhere, anywhere],
+        out_specs=anywhere,
+        out_shape=jax.ShapeDtypeStruct(block.shape, block.dtype),
+        input_output_aliases={0: 0},
+        compiler_params=pltpu.CompilerParams(vmem_limit_bytes=62 * 2**20),
+        name="hold",
+    )(block, then)
 
 
 def both_halves(*pairs):
@@ -327,22 +353,26 @@
     pair = functools.partial(pair_terms, flags)
     crossed = send(own, CROSSING)
     partner = send(own, PARTNERS)
-    own_copy = copied(own)
+    own_copy = copied(flags, own)
     token = crossed[:8, :LANES] + kernel[0, :8] + own_copy[:8, :LANES]
     left, held_back = gate(send(token, ARRIVED), left, own_copy)
     constants = (kernel, left, right)
     single = send(held_back, SINGLES)
     beside = send(held_back, BESIDE)
+
+    partner_sum, crossed_sum, partner = pair(
+        0, partner, crossed, constants, for_b=True, hand_on=True
+    )
     passed = send(partner, PASSED)
-
-    partner_sum, crossed_sum = pair(0, partner, crossed, constants, for_b=True)
     own_sum, crossed_sum = pair(1, own, crossed, constants, sum_b=crossed_sum, for_b=True)
     home = send(crossed_sum, HOME_ACROSS)
-    top, bottom = pair(2, partner, beside, constants, sum_a=partner_sum, halves=True, then=own_sum)
+    top, bottom = pair(
+        2, partner, beside, constants, sum_a=partner_sum, halves=True, then=own_sum
+    )
     bottom = send(bottom, HOME_TURN)
     top = send(top, HOME_FAR)
-    bottom = send(bottom, HOME_TURNED)
     own_sum = pair(3, own, passed, constants, sum_a=own_sum)
+    bottom = send(hold(bottom, own_sum), HOME_TURNED)
     own_sum = pair(4, own, single, constants, sum_a=own_sum, in_place=True)
     own_sum = jnp.where(flags[6] == 1, own_sum, 0.0)
     return (own_sum + home + jnp.concatenate([top, bottom], 0))[None]

time: 193 us -> 193 us (level)
  the two profiles are of different devices: /device:TPU:0 before, /device:TPU:4 now
where the time goes in v7:
time: 193 us; the launch traced here: 192 us
  waiting for transfers between devices  103 us (53%)
  Pallas kernels  52.6 us (27%)
  starting transfers between devices  20.1 us (10%)
  other arithmetic  9.86 us (5%)
  local copies, waits for them, and re-layouts  5.68 us (3%)
    ppermute x10, waiting for transfers between devices, send(): return lax.ppermute(value[None], 'band', pairs)[0]  103 us
    pallas_call x5, Pallas kernels, pair_terms(): pl.pallas_call(functools.partial(pair_body, points, slot, has), grid=(2 *...  45.6 us
    ppermute x10, starting transfers between devices, send(): return lax.ppermute(value[None], 'band', pairs)[0]  20.1 us
    broadcast_in_dim x1, other arithmetic, sixteen_bands(): return (own_sum + home + jnp.concatenate([top, bottom], 0))[None]  6 us
    pallas_call x1, Pallas kernels, copied(): pl.pallas_call(copy_body, grid=(X_STEPS,), in_specs=[pl.BlockSpec(memory_...  5.47 us
  transfers between devices with their start and end apart: 10, of which 3 were waited for; matrix products, arithmetic and copies ran while one was open for 3% of the time, Pallas kernels for 27%

profile of v7, /device:TPU:4, one launch (start us, length us, event | category | flops | bytes accessed | tf_op | source)
XLA Modules:
  0.0 191.9 jit_solution(12845847677597687560)
XLA Ops:
  0.0 2.5 %collective-permute-start = (f32[1,96,9216]{2,1,0:T(8,128)}, f32[1,96,9216]{2,1,0:T(8,128)}, u32[]{:S(2)}, u32[]{:S(2)}) collective-permute-start(f32[1,96,9216]{2,1,0:T(8,128)} %param.4), channel_id=1, source_target_pairs={{3,14},{4,9},{12,1},{11,6},{19,30},{20,25},{28,17},{27,22}} | collective-permute-start | bytes 10616840 | tf_op jit(solution)/shard_map/ppermute | solution.py:347
  2.5 2.4 %collective-permute-start.3 = (f32[1,96,9216]{2,1,0:T(8,128)}, f32[1,96,9216]{2,1,0:T(8,128)}, u32[]{:S(2)}, u32[]{:S(2)}) collective-permute-start(f32[1,96,9216]{2,1,0:T(8,128)} %param.4), channel_id=1, source_target_pairs={{8,14},{15,9},{9,11},{14,12},{7,1},{0,6},{6,4},{1,3},{24,30},{31,2... | collective-permute-start | bytes 10616840 | tf_op jit(solution)/shard_map/ppermute | solution.py:347
  4.9 1.2 constant_dynamic-slice_fusion
  6.1 5.5 %copied.1.block_ref = f32[96,9216]{1,0:T(8,128)} custom-call(s32[10]{0:T(128)} %get-tuple-element.24.flags_ref.refs_0_, f32[96,9216]{1,0:T(8,128)} %bitcast.33), custom_call_target="tpu_custom_call" | custom-call | tf_op jit(solution)/shard_map/copied/pallas_call | solution.py:276
  11.6 0.1 broadcast_add_fusion
  11.7 3.1 %fusion.5.refs_3_.refs_4_.refs_5_ = f32[96,96,128]{2,1,0:T(8,128)S(1)} fusion(f32[128]{0:T(128)S(1)} %fusion.14, f32[96,96]{1,0:T(8,128)S(1)} %broadcast_add_fusion, pred[128]{0:T(512)(128)(4,1)S(1)} %iota_compare_fusion), kind=kLoop, calls=%fused_computation.7 | loop fusion | flops 12976128 | bytes 4756096 | tf_op jit(solution)/shard_map/jit(_where)/select_n | solution.py:39
  14.7 0.0 copy-start
  14.8 0.0 collective-permute-done
  14.8 2.1 %copy-done = f32[96,96,128]{2,1,0:T(8,128)} copy-done((f32[96,96,128]{2,1,0:T(8,128)}, f32[96,96,128]{2,1,0:T(8,128)S(1)}, u32[]{:S(2)}) %copy-start) | copy-done | bytes 4718616
  16.9 0.7 fusion.10
  17.6 1.3 collective-permute-start.1
  18.9 33.2 %collective-permute-done.1 = f32[1,8,128]{2,1,0:T(8,128)S(1)} collective-permute-done((f32[1,8,128]{2,1,0:T(8,128)S(1)}, f32[1,8,128]{2,1,0:T(8,128)S(1)}, u32[]{:S(2)}, u32[]{:S(2)}) %collective-permute-start.1) | collective-permute-done | bytes 4128 | tf_op jit(solution)/shard_map/ppermute | solution.py:347
  52.1 0.0 copy-start.2
  52.1 0.6 copy-done.2
  52.7 1.5 gate.1
  54.2 3.1 %collective-permute-start.6 = (f32[1,96,9216]{2,1,0:T(8,128)}, f32[1,96,9216]{2,1,0:T(8,128)}, u32[]{:S(2)}, u32[]{:S(2)}) collective-permute-start(f32[1,96,9216]{2,1,0:T(8,128)} %bitcast.37), channel_id=1, source_target_pairs={{13,14},{10,9},{2,1},{5,6},{29,30},{26,25},{18,17},{21,22}} | collective-permute-start | bytes 10616840 | tf_op jit(solution)/shard_map/ppermute | solution.py:347
  57.3 0.0 collective-permute-done.3
  57.3 2.5 %pair_terms.5 = (f32[96,9216]{1,0:T(8,128)}, f32[96,9216]{1,0:T(8,128)}, f32[96,9216]{1,0:T(8,128)}) custom-call(s32[10]{0:T(128)} %get-tuple-element.24.flags_ref.refs_0_, f32[96,9216]{1,0:T(8,128)} %bitcast.9.refs_1_, f32[96,9216]{1,0:T(8,128)} %bitcast.3.refs_2_, f32[96,96,128]{2,1,0:T(8,128)} %copy-done, ...), custom_call_target="tpu_custom_call", output_to_operand_aliasing={{2}: (1, {})} | custom-call | flops 100000000 | bytes 1000000 | tf_op jit(solution)/shard_map/pair_terms/pallas_call | solution.py:240
  59.8 1.3 collective-permute-start.4
  61.1 3.5 %collective-permute-start.2 = (f32[1,96,9216]{2,1,0:T(8,128)}, f32[1,96,9216]{2,1,0:T(8,128)}, u32[]{:S(2)}, u32[]{:S(2)}) collective-permute-start(f32[1,96,9216]{2,1,0:T(8,128)} %bitcast.38), channel_id=1, source_target_pairs={{5,10},{2,13},{10,5},{13,2},{21,26},{18,29},{26,21},{29,18}} | collective-permute-start | bytes 10616840 | tf_op jit(solution)/shard_map/ppermute | solution.py:347
  64.5 2.7 %pair_terms.6 = (f32[96,9216]{1,0:T(8,128)}, f32[96,9216]{1,0:T(8,128)}) custom-call(s32[10]{0:T(128)} %get-tuple-element.24.flags_ref.refs_0_, f32[96,9216]{1,0:T(8,128)} %bitcast.34, f32[96,9216]{1,0:T(8,128)} %bitcast.3.refs_2_, f32[96,9216]{1,0:T(8,128)} %get-tuple-element.17.refs_3_, f32[96,96,128]{2,1,0:T(8,128)} %copy-done, ...), custom_call_target="tpu_custom_call" | custom-call | flops 100000000 | bytes 1000000 | tf_op jit(solution)/shard_map/pair_terms/pallas_call | solution.py:240
  67.2 2.5 %collective-permute-start.5 = (f32[1,96,9216]{2,1,0:T(8,128)}, f32[1,96,9216]{2,1,0:T(8,128)}, u32[]{:S(2)}, u32[]{:S(2)}) collective-permute-start(f32[1,96,9216]{2,1,0:T(8,128)} %bitcast.43), channel_id=1, source_target_pairs={{9,4},{14,3},{6,11},{1,12},{25,20},{30,19},{22,27},{17,28}} | collective-permute-start | bytes 10616840 | tf_op jit(solution)/shard_map/ppermute | solution.py:347
  69.7 25.1 %collective-permute-done.6 = f32[1,96,9216]{2,1,0:T(8,128)} collective-permute-done((f32[1,96,9216]{2,1,0:T(8,128)}, f32[1,96,9216]{2,1,0:T(8,128)}, u32[]{:S(2)}, u32[]{:S(2)}) %collective-permute-start.6) | collective-permute-done | bytes 3538976 | tf_op jit(solution)/shard_map/ppermute | solution.py:347
  94.8 2.7 %pair_terms.9 = (f32[56,9216]{1,0:T(8,128)}, f32[40,9216]{1,0:T(8,128)}) custom-call(s32[10]{0:T(128)} %get-tuple-element.24.flags_ref.refs_0_, f32[96,9216]{1,0:T(8,128)} %get-tuple-element.16.refs_1_, f32[96,9216]{1,0:T(8,128)} %bitcast.14.refs_2_, f32[96,9216]{1,0:T(8,128)} %get-tuple-element.20.refs_3_, f32[96,9216]{1,0:T(8,128)} %get-tuple-element.18.refs_3_.refs_4_, ...), custom_call_target="tpu_custom_call" | custom-call | flops 100000000 | bytes 1000000 | tf_op jit(solution)/shard_map/pair_terms/pallas_call | solution.py:240
  97.5 0.8 collective-permute-start.8
  98.2 2.0 %collective-permute-start.7 = (f32[1,56,9216]{2,1,0:T(8,128)}, f32[1,56,9216]{2,1,0:T(8,128)}, u32[]{:S(2)}, u32[]{:S(2)}) collective-permute-start(f32[1,56,9216]{2,1,0:T(8,128)} %bitcast.44), channel_id=1, source_target_pairs={{9,15},{14,8},{6,0},{1,7},{25,31},{30,24},{22,16},{17,23}} | collective-permute-start | bytes 6193160 | tf_op jit(solution)/shard_map/ppermute | solution.py:347
  100.2 44.6 %collective-permute-done.4 = f32[1,96,9216]{2,1,0:T(8,128)} collective-permute-done((f32[1,96,9216]{2,1,0:T(8,128)}, f32[1,96,9216]{2,1,0:T(8,128)}, u32[]{:S(2)}, u32[]{:S(2)}) %collective-permute-start.4) | collective-permute-done | bytes 3538976 | tf_op jit(solution)/shard_map/ppermute | solution.py:347
  144.8 18.9 %pair_terms.7.refs_3_.then_ref = f32[96,9216]{1,0:T(8,128)} custom-call(s32[10]{0:T(128)} %get-tuple-element.24.flags_ref.refs_0_, f32[96,9216]{1,0:T(8,128)} %bitcast.35, f32[96,9216]{1,0:T(8,128)} %bitcast.11.refs_2_, f32[96,9216]{1,0:T(8,128)} %get-tuple-element.18.refs_3_.refs_4_, f32[96,96,128]{2,1,0:T(8,128)} %copy-done, ...), custom_call_target="tpu_custom_call" | custom-call | flops 100000000 | bytes 1000000 | tf_op jit(solution)/shard_map/pair_terms/pallas_call | solution.py:240
  163.7 0.0 collective-permute-done.8
  163.7 0.0 copy-start.1
  163.7 1.1 copy-done.1
  164.8 0.9 collective-permute-start.9
  165.8 0.6 slice.27
  167.0 0.0 collective-permute-done.2
  167.0 18.9 %pair_terms.8 = f32[96,9216]{1,0:T(8,128)} custom-call(s32[10]{0:T(128)} %get-tuple-element.24.flags_ref.refs_0_, f32[96,9216]{1,0:T(8,128)} %bitcast.36, f32[96,9216]{1,0:T(8,128)} %bitcast.8.refs_2_, f32[96,9216]{1,0:T(8,128)} %pair_terms.7.refs_3_.then_ref, f32[96,96,128]{2,1,0:T(8,128)} %copy-done, ...), custom_call_target="tpu_custom_call", output_to_operand_aliasing={{}: (3, {})} | custom-call | flops 100000000 | bytes 1000000 | tf_op jit(solution)/shard_map/pair_terms/pallas_call | solution.py:240
  185.9 0.0 collective-permute-done.5
  185.9 0.0 collective-permute-done.7
  185.9 0.0 collective-permute-done.9
  185.9 6.0 %fusion.9 = f32[1,96,9216]{2,1,0:T(8,128)} fusion(f32[40,9216]{1,0:T(8,128)S(1)} %bitcast.39, f32[56,9216]{1,0:T(8,128)} %bitcast.16, f32[1,96,9216]{2,1,0:T(8,128)} %collective-permute-done.5, f32[96,9216]{1,0:T(8,128)} %pair_terms.8, pred[]{:T(512)} %bitcast), kind=kLoop, calls=%fused_computation.12 | loop fusion | flops 3538944 | bytes 14155777 | tf_op jit(solution)/shard_map/broadcast_in_dim | solution.py:378
  (5 shorter events, 0.0 us)
Async XLA Ops:
  0.0 14.8 %collective-permute-start = (f32[1,96,9216]{2,1,0:T(8,128)}, f32[1,96,9216]{2,1,0:T(8,128)}, u32[]{:S(2)}, u32[]{:S(2)}) collective-permute-start(f32[1,96,9216]{2,1,0:T(8,128)} %param.4), channel_id=1, source_target_pairs={{3,14},{4,9},{12,1},{11,6},{19,30},{20,25},{28,17},{27,22}} | collective-permute-start | bytes 10616840 | tf_op jit(solution)/shard_map/ppermute | solution.py:347
  2.5 54.8 %collective-permute-start.3 = (f32[1,96,9216]{2,1,0:T(8,128)}, f32[1,96,9216]{2,1,0:T(8,128)}, u32[]{:S(2)}, u32[]{:S(2)}) collective-permute-start(f32[1,96,9216]{2,1,0:T(8,128)} %param.4), channel_id=1, source_target_pairs={{8,14},{15,9},{9,11},{14,12},{7,1},{0,6},{6,4},{1,3},{24,30},{31,2... | collective-permute-start | bytes 10616840 | tf_op jit(solution)/shard_map/ppermute | solution.py:347
  14.7 2.1 %copy-start = (f32[96,96,128]{2,1,0:T(8,128)}, f32[96,96,128]{2,1,0:T(8,128)S(1)}, u32[]{:S(2)}) copy-start(f32[96,96,128]{2,1,0:T(8,128)S(1)} %fusion.5.refs_3_.refs_4_.refs_5_) | copy-start | bytes 14155780
  17.6 34.5 %collective-permute-start.1 = (f32[1,8,128]{2,1,0:T(8,128)S(1)}, f32[1,8,128]{2,1,0:T(8,128)S(1)}, u32[]{:S(2)}, u32[]{:S(2)}) collective-permute-start(f32[1,8,128]{2,1,0:T(8,128)S(1)} %fusion.10), channel_id=1, source_target_pairs={{14,2},{9,5},{1,13},{6,10},{30,18},{25,21},{17,29},{22,26}} | collective-permute-start | bytes 12296 | tf_op jit(solution)/shard_map/ppermute | solution.py:347
  52.1 0.6 copy-start.2
  54.2 40.6 %collective-permute-start.6 = (f32[1,96,9216]{2,1,0:T(8,128)}, f32[1,96,9216]{2,1,0:T(8,128)}, u32[]{:S(2)}, u32[]{:S(2)}) collective-permute-start(f32[1,96,9216]{2,1,0:T(8,128)} %bitcast.37), channel_id=1, source_target_pairs={{13,14},{10,9},{2,1},{5,6},{29,30},{26,25},{18,17},{21,22}} | collective-permute-start | bytes 10616840 | tf_op jit(solution)/shard_map/ppermute | solution.py:347
  59.8 85.0 %collective-permute-start.4 = (f32[1,96,9216]{2,1,0:T(8,128)}, f32[1,96,9216]{2,1,0:T(8,128)}, u32[]{:S(2)}, u32[]{:S(2)}) collective-permute-start(f32[1,96,9216]{2,1,0:T(8,128)} %bitcast.10), channel_id=1, source_target_pairs={{9,10},{14,13},{11,14},{12,9},{6,5},{1,2},{4,1},{3,6},{25,26},{30,... | collective-permute-start | bytes 10616840 | tf_op jit(solution)/shard_map/ppermute | solution.py:347
  61.1 105.9 %collective-permute-start.2 = (f32[1,96,9216]{2,1,0:T(8,128)}, f32[1,96,9216]{2,1,0:T(8,128)}, u32[]{:S(2)}, u32[]{:S(2)}) collective-permute-start(f32[1,96,9216]{2,1,0:T(8,128)} %bitcast.38), channel_id=1, source_target_pairs={{5,10},{2,13},{10,5},{13,2},{21,26},{18,29},{26,21},{29,18}} | collective-permute-start | bytes 10616840 | tf_op jit(solution)/shard_map/ppermute | solution.py:347
  67.2 118.7 %collective-permute-start.5 = (f32[1,96,9216]{2,1,0:T(8,128)}, f32[1,96,9216]{2,1,0:T(8,128)}, u32[]{:S(2)}, u32[]{:S(2)}) collective-permute-start(f32[1,96,9216]{2,1,0:T(8,128)} %bitcast.43), channel_id=1, source_target_pairs={{9,4},{14,3},{6,11},{1,12},{25,20},{30,19},{22,27},{17,28}} | collective-permute-start | bytes 10616840 | tf_op jit(solution)/shard_map/ppermute | solution.py:347
  97.5 66.2 %collective-permute-start.8 = (f32[1,40,9216]{2,1,0:T(8,128)}, f32[1,40,9216]{2,1,0:T(8,128)S(1)}, u32[]{:S(2)}, u32[]{:S(2)}) collective-permute-start(f32[1,40,9216]{2,1,0:T(8,128)} %bitcast.45), channel_id=1, source_target_pairs={{9,11},{14,12},{6,4},{1,3},{25,27},{30,28},{22,20},{17,19}} | collective-permute-start | bytes 4423688 | tf_op jit(solution)/shard_map/ppermute | solution.py:347
  98.2 87.6 %collective-permute-start.7 = (f32[1,56,9216]{2,1,0:T(8,128)}, f32[1,56,9216]{2,1,0:T(8,128)}, u32[]{:S(2)}, u32[]{:S(2)}) collective-permute-start(f32[1,56,9216]{2,1,0:T(8,128)} %bitcast.44), channel_id=1, source_target_pairs={{9,15},{14,8},{6,0},{1,7},{25,31},{30,24},{22,16},{17,23}} | collective-permute-start | bytes 6193160 | tf_op jit(solution)/shard_map/ppermute | solution.py:347
  163.7 1.1 copy-start.1
  164.8 21.1 %collective-permute-start.9 = (f32[1,40,9216]{2,1,0:T(8,128)}, f32[1,40,9216]{2,1,0:T(8,128)S(1)}, u32[]{:S(2)}, u32[]{:S(2)}) collective-permute-start(f32[1,40,9216]{2,1,0:T(8,128)} %bitcast.41), channel_id=1, source_target_pairs={{11,15},{12,8},{4,0},{3,7},{27,31},{28,24},{20,16},{19,23}} | collective-permute-start | bytes 4423688 | tf_op jit(solution)/shard_map/ppermute | solution.py:347

commit v8 on v7

--- a/solution.py
+++ b/solution.py
@@ -13,7 +13,7 @@
 screening = 5.44
 LANES = 128
 X_STEPS = 6
-PLANE_STEPS = 6
+PLANE_STEPS = 3
 FAR_ROWS = 40
 
 
@@ -284,25 +284,51 @@
     )(flags, block)
 
 
-def gate_body(token_ref, left_ref, block_ref, new_left_ref, new_block_ref):
+def gate_body(token_ref, left_ref, flags_ref, turned_ref, block_ref, new_left_ref, new_block_ref, near, sems):
+    del token_ref, block_ref
     new_left_ref[...] = left_ref[...]
-
-
-def gate(token, left, block):
+    columns = turned_ref.shape[1] // X_STEPS
+
+    @pl.when(flags_ref[TURNS] == 1)
+    def from_turned():
+        spans = [pl.ds(i * columns, columns) for i in range(X_STEPS)]
+        inward = [
+            pltpu.make_async_copy(turned_ref.at[:, span], near.at[:, span], sems.at[0, i])
+            for i, span in enumerate(spans)
+        ]
+        outward = [
+            pltpu.make_async_copy(near.at[:, span], new_block_ref.at[:, span], sems.at[1, i])
+            for i, span in enumerate(spans)
+        ]
+        for copy in inward:
+            copy.start()
+        for first, second in zip(inward, outward):
+            first.wait()
+            second.start()
+        for copy in outward:
+            copy.wait()
+
+
+def gate(token, left, flags, turned, block):
     in_vmem = pl.BlockSpec(memory_space=pltpu.VMEM)
+    in_smem = pl.BlockSpec(memory_space=pltpu.SMEM)
     anywhere = pl.BlockSpec(memory_space=pl.ANY)
     return pl.pallas_call(
         gate_body,
-        in_specs=[in_vmem, in_vmem, anywhere],
+        in_specs=[in_vmem, in_vmem, in_smem, anywhere, anywhere],
         out_specs=[in_vmem, anywhere],
         out_shape=[
             jax.ShapeDtypeStruct(left.shape, left.dtype),
             jax.ShapeDtypeStruct(block.shape, block.dtype),
         ],
-        input_output_aliases={2: 1},
+        input_output_aliases={4: 1},
+        scratch_shapes=[
+            pltpu.VMEM(block.shape, block.dtype),
+            pltpu.SemaphoreType.DMA((2, X_STEPS)),
+        ],
         compiler_params=pltpu.CompilerParams(vmem_limit_bytes=62 * 2**20),
         name="gate",
-    )(token, left, block)
+    )(token, left, flags, turned, block)
 
 
 def hold_body(block_ref, then_ref, new_block_ref):
@@ -329,17 +355,16 @@
 CROSSING = both_halves((3, 14), (4, 9))
 PARTNERS = both_halves((8, 14), (15, 9), (9, 11), (14, 12))
 ARRIVED = both_halves((14, 2), (9, 5))
-SINGLES = both_halves((5, 10), (2, 13))
-BESIDE = both_halves((13, 14), (10, 9))
-PASSED = both_halves((9, 10), (14, 13), (11, 14), (12, 9))
+SECOND = both_halves((5, 10), (2, 13), (11, 14), (12, 9))
+BESIDE = both_halves((13, 14), (10, 9), (15, 10), (8, 13))
 HOME_ACROSS = both_halves((9, 4), (14, 3))
 HOME_FAR = both_halves((9, 15), (14, 8))
 HOME_TURN = both_halves((9, 11), (14, 12))
 HOME_TURNED = both_halves((11, 15), (12, 8))
-HUB_FLAGS = (1, 0, 1, 0, 1, 1, 1, 1, 0, 0)
-SINGLE_FLAGS = (0, 0, 0, 0, 0, 0, 1, 0, 1, 1)
-FLAGS = {9: HUB_FLAGS, 14: HUB_FLAGS, 6: HUB_FLAGS, 1: HUB_FLAGS}
-FLAGS.update({10: SINGLE_FLAGS, 13: SINGLE_FLAGS, 5: SINGLE_FLAGS, 2: SINGLE_FLAGS})
+TURNS = 10
+FLAGS = {i: (1, 0, 1, 0, 1, 1, 0, 0, 1, 1, 0) for i in (9, 14, 6, 1)}
+FLAGS.update({i: (0, 0, 0, 0, 0, 0, 1, 0, 1, 1, 0) for i in (10, 13, 5, 2)})
+FLAGS.update({i: (0,) * TURNS + (1,) for i in (11, 12, 4, 3)})
 
 
 def sixteen_bands(orbitals, constants):
@@ -348,22 +373,19 @@
 
     kernel, left, right = constants
     own = orbitals[0]
-    flags = jnp.asarray([FLAGS.get(i, (0,) * 10) for i in range(16)], jnp.int32)
+    flags = jnp.asarray([FLAGS.get(i, (0,) * (TURNS + 1)) for i in range(16)], jnp.int32)
     flags = flags[lax.axis_index("band")]
     pair = functools.partial(pair_terms, flags)
     crossed = send(own, CROSSING)
     partner = send(own, PARTNERS)
     own_copy = copied(flags, own)
     token = crossed[:8, :LANES] + kernel[0, :8] + own_copy[:8, :LANES]
-    left, held_back = gate(send(token, ARRIVED), left, own_copy)
+    left, held_back = gate(send(token, ARRIVED), left, flags, partner, own_copy)
     constants = (kernel, left, right)
-    single = send(held_back, SINGLES)
     beside = send(held_back, BESIDE)
-
-    partner_sum, crossed_sum, partner = pair(
-        0, partner, crossed, constants, for_b=True, hand_on=True
-    )
-    passed = send(partner, PASSED)
+    second = send(held_back, SECOND)
+
+    partner_sum, crossed_sum = pair(0, partner, crossed, constants, for_b=True)
     own_sum, crossed_sum = pair(1, own, crossed, constants, sum_b=crossed_sum, for_b=True)
     home = send(crossed_sum, HOME_ACROSS)
     top, bottom = pair(
@@ -371,10 +393,10 @@
     )
     bottom = send(bottom, HOME_TURN)
     top = send(top, HOME_FAR)
-    own_sum = pair(3, own, passed, constants, sum_a=own_sum)
+    own_sum = pair(3, own, beside, constants, sum_a=own_sum, in_place=True)
+    own_sum = pair(4, own, second, constants, sum_a=own_sum)
     bottom = send(hold(bottom, own_sum), HOME_TURNED)
-    own_sum = pair(4, own, single, constants, sum_a=own_sum, in_place=True)
-    own_sum = jnp.where(flags[6] == 1, own_sum, 0.0)
+    own_sum = jnp.where(flags[8] == 1, own_sum, 0.0)
     return (own_sum + home + jnp.concatenate([top, bottom], 0))[None]
 
 

time: 193 us -> 187 us (0.969)
  the two profiles are of different devices: /device:TPU:4 before, /device:TPU:6 now
where the time goes in v8:
time: 187 us; the launch traced here: 186 us
  waiting for transfers between devices  105 us (56%)
  Pallas kernels  47.8 us (26%)
  starting transfers between devices  16.9 us (9%)
  other arithmetic  9.85 us (5%)
  local copies, waits for them, and re-layouts  5.72 us (3%)
    ppermute x9, waiting for transfers between devices, send(): return lax.ppermute(value[None], 'band', pairs)[0]  105 us
    pallas_call x5, Pallas kernels, pair_terms(): pl.pallas_call(functools.partial(pair_body, points, slot, has), grid=(2 *...  40.6 us
    ppermute x9, starting transfers between devices, send(): return lax.ppermute(value[None], 'band', pairs)[0]  16.9 us
    broadcast_in_dim x1, other arithmetic, sixteen_bands(): return (own_sum + home + jnp.concatenate([top, bottom], 0))[None]  5.99 us
    pallas_call x1, Pallas kernels, copied(): pl.pallas_call(copy_body, grid=(X_STEPS,), in_specs=[pl.BlockSpec(memory_...  5.47 us
    unnamed x6, local copies, waits for them, and re-layouts  3.89 us
  transfers between devices with their start and end apart: 9, of which 2 were waited for; matrix products, arithmetic and copies ran while one was open for 3% of the time, Pallas kernels for 25%

profile of v8, /device:TPU:6, one launch (start us, length us, event | category | flops | bytes accessed | tf_op | source)
XLA Modules:
  0.0 186.0 jit_solution(12350901948768681799)
XLA Ops:
  0.0 2.5 %collective-permute-start = (f32[1,96,9216]{2,1,0:T(8,128)}, f32[1,96,9216]{2,1,0:T(8,128)}, u32[]{:S(2)}, u32[]{:S(2)}) collective-permute-start(f32[1,96,9216]{2,1,0:T(8,128)} %param.4), channel_id=1, source_target_pairs={{3,14},{4,9},{12,1},{11,6},{19,30},{20,25},{28,17},{27,22}} | collective-permute-start | bytes 10616840 | tf_op jit(solution)/shard_map/ppermute | solution.py:372
  2.5 2.4 %collective-permute-start.2 = (f32[1,96,9216]{2,1,0:T(8,128)}, f32[1,96,9216]{2,1,0:T(8,128)}, u32[]{:S(2)}, u32[]{:S(2)}) collective-permute-start(f32[1,96,9216]{2,1,0:T(8,128)} %param.4), channel_id=1, source_target_pairs={{8,14},{15,9},{9,11},{14,12},{7,1},{0,6},{6,4},{1,3},{24,30},{31,2... | collective-permute-start | bytes 10616840 | tf_op jit(solution)/shard_map/ppermute | solution.py:372
  4.9 1.3 constant_dynamic-slice_fusion
  6.1 5.5 %copied.1.block_ref = f32[96,9216]{1,0:T(8,128)} custom-call(s32[11]{0:T(128)} %get-tuple-element.22.flags_ref.refs_0_, f32[96,9216]{1,0:T(8,128)} %bitcast.31), custom_call_target="tpu_custom_call" | custom-call | tf_op jit(solution)/shard_map/copied/pallas_call | solution.py:276
  11.7 0.1 broadcast_add_fusion
  11.7 3.1 %fusion.5.refs_3_.refs_4_.refs_5_ = f32[96,96,128]{2,1,0:T(8,128)S(1)} fusion(f32[128]{0:T(128)S(1)} %fusion.14, f32[96,96]{1,0:T(8,128)S(1)} %broadcast_add_fusion, pred[128]{0:T(512)(128)(4,1)S(1)} %iota_compare_fusion), kind=kLoop, calls=%fused_computation.7 | loop fusion | flops 12976128 | bytes 4756096 | tf_op jit(solution)/shard_map/jit(_where)/select_n | solution.py:39
  14.8 0.0 copy-start
  14.8 0.0 collective-permute-done
  14.8 2.1 %copy-done = f32[96,96,128]{2,1,0:T(8,128)} copy-done((f32[96,96,128]{2,1,0:T(8,128)}, f32[96,96,128]{2,1,0:T(8,128)S(1)}, u32[]{:S(2)}) %copy-start) | copy-done | bytes 4718616
  16.9 0.7 fusion.10
  17.6 1.3 collective-permute-start.1
  18.9 0.0 collective-permute-done.2
  18.9 33.1 %collective-permute-done.1 = f32[1,8,128]{2,1,0:T(8,128)S(1)} collective-permute-done((f32[1,8,128]{2,1,0:T(8,128)S(1)}, f32[1,8,128]{2,1,0:T(8,128)S(1)}, u32[]{:S(2)}, u32[]{:S(2)}) %collective-permute-start.1) | collective-permute-done | bytes 4128 | tf_op jit(solution)/shard_map/ppermute | solution.py:372
  52.1 0.0 copy-start.2
  52.1 0.6 copy-done.2
  52.7 1.7 gate.1
  54.3 1.9 %collective-permute-start.4 = (f32[1,96,9216]{2,1,0:T(8,128)}, f32[1,96,9216]{2,1,0:T(8,128)}, u32[]{:S(2)}, u32[]{:S(2)}) collective-permute-start(f32[1,96,9216]{2,1,0:T(8,128)} %bitcast.35), channel_id=1, source_target_pairs={{13,14},{10,9},{15,10},{8,13},{2,1},{5,6},{0,5},{7,2},{29,30},{26,... | collective-permute-start | bytes 10616840 | tf_op jit(solution)/shard_map/ppermute | solution.py:372
  56.3 2.8 %collective-permute-start.3 = (f32[1,96,9216]{2,1,0:T(8,128)}, f32[1,96,9216]{2,1,0:T(8,128)}, u32[]{:S(2)}, u32[]{:S(2)}) collective-permute-start(f32[1,96,9216]{2,1,0:T(8,128)} %bitcast.36), channel_id=1, source_target_pairs={{5,10},{2,13},{11,14},{12,9},{10,5},{13,2},{4,1},{3,6},{21,26},{18... | collective-permute-start | bytes 10616840 | tf_op jit(solution)/shard_map/ppermute | solution.py:372
  59.1 2.2 %pair_terms.5 = (f32[96,9216]{1,0:T(8,128)}, f32[96,9216]{1,0:T(8,128)}) custom-call(s32[11]{0:T(128)} %get-tuple-element.22.flags_ref.refs_0_, f32[96,9216]{1,0:T(8,128)} %bitcast.7.turned_ref.refs_1_, f32[96,9216]{1,0:T(8,128)} %bitcast.3.refs_2_, f32[96,96,128]{2,1,0:T(8,128)} %copy-done, bf16[192,192]{1,0:T(8,128)(2,1)} %get-tuple-element.14.refs_4_.refs_5_.refs_6_, ...), custom_call_target="tpu_custom_call" | custom-call | flops 100000000 | bytes 1000000 | tf_op jit(solution)/shard_map/pair_terms/pallas_call | solution.py:240
  61.3 2.4 %pair_terms.6 = (f32[96,9216]{1,0:T(8,128)}, f32[96,9216]{1,0:T(8,128)}) custom-call(s32[11]{0:T(128)} %get-tuple-element.22.flags_ref.refs_0_, f32[96,9216]{1,0:T(8,128)} %bitcast.32, f32[96,9216]{1,0:T(8,128)} %bitcast.3.refs_2_, f32[96,9216]{1,0:T(8,128)} %get-tuple-element.15.refs_3_, f32[96,96,128]{2,1,0:T(8,128)} %copy-done, ...), custom_call_target="tpu_custom_call" | custom-call | flops 100000000 | bytes 1000000 | tf_op jit(solution)/shard_map/pair_terms/pallas_call | solution.py:240
  63.7 2.5 %collective-permute-start.5 = (f32[1,96,9216]{2,1,0:T(8,128)}, f32[1,96,9216]{2,1,0:T(8,128)}, u32[]{:S(2)}, u32[]{:S(2)}) collective-permute-start(f32[1,96,9216]{2,1,0:T(8,128)} %bitcast.41), channel_id=1, source_target_pairs={{9,4},{14,3},{6,11},{1,12},{25,20},{30,19},{22,27},{17,28}} | collective-permute-start | bytes 10616840 | tf_op jit(solution)/shard_map/ppermute | solution.py:372
  66.2 71.9 %collective-permute-done.4 = f32[1,96,9216]{2,1,0:T(8,128)} collective-permute-done((f32[1,96,9216]{2,1,0:T(8,128)}, f32[1,96,9216]{2,1,0:T(8,128)}, u32[]{:S(2)}, u32[]{:S(2)}) %collective-permute-start.4) | collective-permute-done | bytes 3538976 | tf_op jit(solution)/shard_map/ppermute | solution.py:372
  138.1 2.4 %pair_terms.9 = (f32[56,9216]{1,0:T(8,128)}, f32[40,9216]{1,0:T(8,128)}) custom-call(s32[11]{0:T(128)} %get-tuple-element.22.flags_ref.refs_0_, f32[96,9216]{1,0:T(8,128)} %bitcast.7.turned_ref.refs_1_, f32[96,9216]{1,0:T(8,128)} %bitcast.10.refs_2_, f32[96,9216]{1,0:T(8,128)} %get-tuple-element.18.refs_3_, f32[96,9216]{1,0:T(8,128)} %get-tuple-element.16.refs_3_.refs_4_, ...), custom_call_target="tpu_custom_call" | custom-call | flops 100000000 | bytes 1000000 | tf_op jit(solution)/shard_map/pair_terms/pallas_call | solution.py:240
  140.4 0.8 collective-permute-start.7
  141.2 2.0 %collective-permute-start.6 = (f32[1,56,9216]{2,1,0:T(8,128)}, f32[1,56,9216]{2,1,0:T(8,128)}, u32[]{:S(2)}, u32[]{:S(2)}) collective-permute-start(f32[1,56,9216]{2,1,0:T(8,128)} %bitcast.42), channel_id=1, source_target_pairs={{9,15},{14,8},{6,0},{1,7},{25,31},{30,24},{22,16},{17,23}} | collective-permute-start | bytes 6193160 | tf_op jit(solution)/shard_map/ppermute | solution.py:372
  143.2 16.8 %pair_terms.7.refs_3_ = f32[96,9216]{1,0:T(8,128)} custom-call(s32[11]{0:T(128)} %get-tuple-element.22.flags_ref.refs_0_, f32[96,9216]{1,0:T(8,128)} %bitcast.33, f32[96,9216]{1,0:T(8,128)} %bitcast.10.refs_2_, f32[96,9216]{1,0:T(8,128)} %get-tuple-element.16.refs_3_.refs_4_, f32[96,96,128]{2,1,0:T(8,128)} %copy-done, ...), custom_call_target="tpu_custom_call", output_to_operand_aliasing={{}: (3, {})} | custom-call | flops 100000000 | bytes 1000000 | tf_op jit(solution)/shard_map/pair_terms/pallas_call | solution.py:240
  160.0 0.0 collective-permute-done.3
  160.0 16.9 %pair_terms.8.then_ref = f32[96,9216]{1,0:T(8,128)} custom-call(s32[11]{0:T(128)} %get-tuple-element.22.flags_ref.refs_0_, f32[96,9216]{1,0:T(8,128)} %bitcast.34, f32[96,9216]{1,0:T(8,128)} %bitcast.9.refs_2_, f32[96,9216]{1,0:T(8,128)} %pair_terms.7.refs_3_, f32[96,96,128]{2,1,0:T(8,128)} %copy-done, ...), custom_call_target="tpu_custom_call" | custom-call | flops 100000000 | bytes 1000000 | tf_op jit(solution)/shard_map/pair_terms/pallas_call | solution.py:240
  176.9 0.0 collective-permute-done.7
  176.9 0.0 copy-start.1
  176.9 1.2 copy-done.1
  178.1 0.7 collective-permute-start.8
  178.9 0.6 slice.27
  180.0 0.0 collective-permute-done.5
  180.0 0.0 collective-permute-done.6
  180.0 0.0 collective-permute-done.8
  180.0 6.0 %fusion.9 = f32[1,96,9216]{2,1,0:T(8,128)} fusion(f32[40,9216]{1,0:T(8,128)S(1)} %bitcast.39, f32[56,9216]{1,0:T(8,128)} %bitcast.14, f32[1,96,9216]{2,1,0:T(8,128)} %collective-permute-done.5, f32[96,9216]{1,0:T(8,128)} %pair_terms.8.then_ref, pred[]{:T(512)} %bitcast), kind=kLoop, calls=%fused_computation.12 | loop fusion | flops 3538944 | bytes 14155777 | tf_op jit(solution)/shard_map/broadcast_in_dim | solution.py:400
  (5 shorter events, 0.0 us)
Async XLA Ops:
  0.0 14.8 %collective-permute-start = (f32[1,96,9216]{2,1,0:T(8,128)}, f32[1,96,9216]{2,1,0:T(8,128)}, u32[]{:S(2)}, u32[]{:S(2)}) collective-permute-start(f32[1,96,9216]{2,1,0:T(8,128)} %param.4), channel_id=1, source_target_pairs={{3,14},{4,9},{12,1},{11,6},{19,30},{20,25},{28,17},{27,22}} | collective-permute-start | bytes 10616840 | tf_op jit(solution)/shard_map/ppermute | solution.py:372
  2.5 16.5 %collective-permute-start.2 = (f32[1,96,9216]{2,1,0:T(8,128)}, f32[1,96,9216]{2,1,0:T(8,128)}, u32[]{:S(2)}, u32[]{:S(2)}) collective-permute-start(f32[1,96,9216]{2,1,0:T(8,128)} %param.4), channel_id=1, source_target_pairs={{8,14},{15,9},{9,11},{14,12},{7,1},{0,6},{6,4},{1,3},{24,30},{31,2... | collective-permute-start | bytes 10616840 | tf_op jit(solution)/shard_map/ppermute | solution.py:372
  14.8 2.1 %copy-start = (f32[96,96,128]{2,1,0:T(8,128)}, f32[96,96,128]{2,1,0:T(8,128)S(1)}, u32[]{:S(2)}) copy-start(f32[96,96,128]{2,1,0:T(8,128)S(1)} %fusion.5.refs_3_.refs_4_.refs_5_) | copy-start | bytes 14155780
  17.6 34.4 %collective-permute-start.1 = (f32[1,8,128]{2,1,0:T(8,128)S(1)}, f32[1,8,128]{2,1,0:T(8,128)S(1)}, u32[]{:S(2)}, u32[]{:S(2)}) collective-permute-start(f32[1,8,128]{2,1,0:T(8,128)S(1)} %fusion.10), channel_id=1, source_target_pairs={{14,2},{9,5},{1,13},{6,10},{30,18},{25,21},{17,29},{22,26}} | collective-permute-start | bytes 12296 | tf_op jit(solution)/shard_map/ppermute | solution.py:372
  52.1 0.6 copy-start.2
  54.3 83.7 %collective-permute-start.4 = (f32[1,96,9216]{2,1,0:T(8,128)}, f32[1,96,9216]{2,1,0:T(8,128)}, u32[]{:S(2)}, u32[]{:S(2)}) collective-permute-start(f32[1,96,9216]{2,1,0:T(8,128)} %bitcast.35), channel_id=1, source_target_pairs={{13,14},{10,9},{15,10},{8,13},{2,1},{5,6},{0,5},{7,2},{29,30},{26,... | collective-permute-start | bytes 10616840 | tf_op jit(solution)/shard_map/ppermute | solution.py:372
  56.3 103.8 %collective-permute-start.3 = (f32[1,96,9216]{2,1,0:T(8,128)}, f32[1,96,9216]{2,1,0:T(8,128)}, u32[]{:S(2)}, u32[]{:S(2)}) collective-permute-start(f32[1,96,9216]{2,1,0:T(8,128)} %bitcast.36), channel_id=1, source_target_pairs={{5,10},{2,13},{11,14},{12,9},{10,5},{13,2},{4,1},{3,6},{21,26},{18... | collective-permute-start | bytes 10616840 | tf_op jit(solution)/shard_map/ppermute | solution.py:372
  63.7 116.3 %collective-permute-start.5 = (f32[1,96,9216]{2,1,0:T(8,128)}, f32[1,96,9216]{2,1,0:T(8,128)}, u32[]{:S(2)}, u32[]{:S(2)}) collective-permute-start(f32[1,96,9216]{2,1,0:T(8,128)} %bitcast.41), channel_id=1, source_target_pairs={{9,4},{14,3},{6,11},{1,12},{25,20},{30,19},{22,27},{17,28}} | collective-permute-start | bytes 10616840 | tf_op jit(solution)/shard_map/ppermute | solution.py:372
  140.4 36.5 %collective-permute-start.7 = (f32[1,40,9216]{2,1,0:T(8,128)}, f32[1,40,9216]{2,1,0:T(8,128)S(1)}, u32[]{:S(2)}, u32[]{:S(2)}) collective-permute-start(f32[1,40,9216]{2,1,0:T(8,128)} %bitcast.43), channel_id=1, source_target_pairs={{9,11},{14,12},{6,4},{1,3},{25,27},{30,28},{22,20},{17,19}} | collective-permute-start | bytes 4423688 | tf_op jit(solution)/shard_map/ppermute | solution.py:372
  141.2 38.8 %collective-permute-start.6 = (f32[1,56,9216]{2,1,0:T(8,128)}, f32[1,56,9216]{2,1,0:T(8,128)}, u32[]{:S(2)}, u32[]{:S(2)}) collective-permute-start(f32[1,56,9216]{2,1,0:T(8,128)} %bitcast.42), channel_id=1, source_target_pairs={{9,15},{14,8},{6,0},{1,7},{25,31},{30,24},{22,16},{17,23}} | collective-permute-start | bytes 6193160 | tf_op jit(solution)/shard_map/ppermute | solution.py:372
  176.9 1.2 copy-start.1
  178.1 1.9 %collective-permute-start.8 = (f32[1,40,9216]{2,1,0:T(8,128)}, f32[1,40,9216]{2,1,0:T(8,128)S(1)}, u32[]{:S(2)}, u32[]{:S(2)}) collective-permute-start(f32[1,40,9216]{2,1,0:T(8,128)} %bitcast.38), channel_id=1, source_target_pairs={{11,15},{12,8},{4,0},{3,7},{27,31},{28,24},{20,16},{19,23}} | collective-permute-start | bytes 4423688 | tf_op jit(solution)/shard_map/ppermute | solution.py:372
